TPU v7x, 512 devices: a whole 4x4x16 slice. The times are simulated.
512 devices in a mesh: seq: 32 (over y, x, core), dp: 16 (over z).
Axes of the slice: x: 4, y: 4, z: 16, core: 2. Of those that a mesh axis runs over, the one named last changes fastest.
Arguments:
- student_query: bfloat16 [16, 4096, 768], P('dp', 'seq'), may hold values from -40 to 40
- key_cache: bfloat16 [16, 4096, 768], P('dp', 'seq'), may hold values from -40 to 40
- value_cache: bfloat16 [16, 4096, 768], P('dp', 'seq'), may hold values from -6 to 6
- grad_rows: bfloat16 [16, 4096, 1536], P('dp', 'seq'), may hold values from -1.5 to 1.5
- out_weight: bfloat16 [768, 1536], P('dp'), may hold values from -0.21875 to 0.21875
- return_counts: int32 [16, 32, 32], P('dp'), may hold values from 0 to 8, as said below
- block_sizes: int32 [16, 5], P('dp'), may hold values from 0 to 1560, as said below
Outputs:
- grad_query: bfloat16 [16, 4096, 768], P('dp', 'seq')
- grad_out_weight: float32 [768, 1536], P('seq', 'dp')
Inputs may be any that keep to these rules, and one draw needn't show every extreme that they name: return_counts[c, s, o] is the number of rows that teacher shard s holds for frame owner o in clip c; every shard holds 128 rows in all and every owner receives 128 rows in all. `block_sizes`: the window's frame blocks in order, summing to 4096: a first block of fewer than 1560 positions (possibly empty), then whole frames of 1560 positions, then the rest of the window, then empty blocks.
All inputs are finite; a program needn't handle non-finite values.
Results may differ from a plain program's by a relative error of at most 0.018.
Values may be sent and summed in bfloat16 or wider, within the bound.
No kernel may reach another device: no remote copies, remote signals or barrier semaphores. Data moves between devices by JAX's collectives and lax.ppermute only.
A program may use at most 64 MiB of HBM per device.

v0:
```python
import jax
import jax.numpy as jnp
from jax import lax
from jax.sharding import PartitionSpec as P

HEAD_DIM = 128


block_rows = 512


def block_scores(key_rows, value_rows, first_key, query_heads, grad_heads, limits):
    key_count = key_rows.shape[0]
    head_count = query_heads.shape[1]
    head_size = query_heads.shape[2]
    key_heads = key_rows.reshape(key_count, head_count, head_size)
    value_heads = value_rows.reshape(key_count, head_count, head_size)
    scores = jnp.einsum(
        "rhd,nhd->hrn", query_heads, key_heads, preferred_element_type=jnp.float32
    ) * head_size ** (-0.5)
    positions = first_key + jnp.arange(key_count, dtype=jnp.int32)
    visible = (positions[None, :] < limits[:, None])[None, :, :]
    scores = jnp.where(visible, scores, -1e30)
    grad_probs = jnp.einsum(
        "rhd,nhd->hrn", grad_heads, value_heads, preferred_element_type=jnp.float32
    )
    return (key_heads, value_heads, scores, visible, grad_probs)


def gather_stats(running, key_rows, value_rows, first_key, query_heads, grad_heads, limits):
    running_peak, norm_sum, centre_sum = running
    key_heads, value_heads, scores, visible, grad_probs = block_scores(
        key_rows, value_rows, first_key, query_heads, grad_heads, limits
    )
    new_peak = jnp.maximum(running_peak, jnp.max(scores, axis=2))
    rescale = jnp.exp(running_peak - new_peak)
    weights = jnp.where(visible, jnp.exp(scores - new_peak[:, :, None]), 0.0)
    norm_sum = rescale * norm_sum + jnp.sum(weights, axis=2)
    centre_sum = rescale * centre_sum + jnp.sum(weights * grad_probs, axis=2)
    return (new_peak, norm_sum, centre_sum)


def make_grads(stats):
    peak, norm_sum, centre = stats

    def add_grads(running, key_rows, value_rows, first_key, query_heads, grad_heads, limits):
        attended_sum, query_sum = running
        key_heads, value_heads, scores, visible, grad_probs = block_scores(
            key_rows, value_rows, first_key, query_heads, grad_heads, limits
        )
        probs = jnp.where(visible, jnp.exp(scores - peak[:, :, None]), 0.0) / norm_sum[:, :, None]
        probs_low = probs.astype(jnp.bfloat16)
        grad_scores = (probs * (grad_probs - centre[:, :, None])).astype(jnp.bfloat16)
        attended_sum = attended_sum + jnp.einsum(
            "hrn,nhd->hrd", probs_low, value_heads, preferred_element_type=jnp.float32
        )
        query_sum = query_sum + jnp.einsum(
            "hrn,nhd->hrd", grad_scores, key_heads, preferred_element_type=jnp.float32
        )
        return (attended_sum, query_sum)

    return add_grads


def fold_keys(step_fn, running, key_rows, value_rows, first_key, query_heads, grad_heads, limits):
    key_count = key_rows.shape[0]
    block_count = key_count // block_rows

    def visit_block(folded, blocks_in):
        block_first = first_key + blocks_in[2] * block_rows
        return (
            step_fn(
                folded, blocks_in[0], blocks_in[1], block_first, query_heads, grad_heads, limits
            ),
            None,
        )

    stacked = (
        key_rows.reshape(block_count, block_rows, key_rows.shape[1]),
        value_rows.reshape(block_count, block_rows, value_rows.shape[1]),
        jnp.arange(block_count, dtype=jnp.int32),
    )
    running, _ = lax.scan(visit_block, running, stacked)
    return running


def shards(
    student_query, key_cache, value_cache, grad_rows, out_weight, return_counts, block_sizes
):
    queries = student_query[0]
    teacher_rows = grad_rows[0]
    counts = return_counts[0]
    block_lengths = block_sizes[0]
    peer_count = lax.axis_size("seq")
    my_index = lax.axis_index("seq")
    row_count = queries.shape[0]
    head_width = queries.shape[1]
    feature_count = teacher_rows.shape[1]
    capacity = 2 * row_count // peer_count
    shard_ends = jnp.cumsum(counts, axis=1)
    shard_starts = shard_ends - counts
    my_counts = lax.dynamic_index_in_dim(counts, my_index, 0, keepdims=False)
    my_starts = lax.dynamic_index_in_dim(shard_starts, my_index, 0, keepdims=False)
    slot_index = jnp.arange(capacity, dtype=jnp.int32)
    source_row = jnp.minimum(my_starts[:, None] + slot_index[None, :], row_count - 1)
    filled = slot_index[None, :] < my_counts[:, None]
    packed = jnp.where(filled[:, :, None], teacher_rows[source_row], jnp.zeros((), jnp.bfloat16))
    arrived = lax.all_to_all(packed, "seq", split_axis=0, concat_axis=0, tiled=True)
    inbound = lax.dynamic_index_in_dim(counts, my_index, 1, keepdims=False)
    inbound_ends = jnp.cumsum(inbound)
    local_rows = jnp.arange(row_count, dtype=jnp.int32)
    earlier = inbound_ends[None, :] <= local_rows[:, None]
    sender = jnp.sum(earlier.astype(jnp.int32), axis=1)
    offset_in = local_rows - jnp.sum(jnp.where(earlier, inbound[None, :], 0), axis=1)
    ordered = arrived.reshape(peer_count * capacity, feature_count)[sender * capacity + offset_in]
    head_grad = lax.dot_general(
        ordered,
        lax.all_gather(out_weight, "dp", axis=0, tiled=True),
        (((1,), (1,)), ((), ())),
        preferred_element_type=jnp.float32,
    ).astype(jnp.bfloat16)
    head_size = HEAD_DIM
    head_count = head_width // head_size
    query_heads = queries.reshape(row_count, head_count, head_size)
    grad_heads = head_grad.reshape(row_count, head_count, head_size)
    block_ends = jnp.cumsum(block_lengths)
    position_end = row_count * peer_count
    positions = my_index * row_count + local_rows
    limits = jnp.min(
        jnp.where(block_ends[None, :] > positions[:, None], block_ends[None, :], position_end),
        axis=1,
    )
    zeros_rows = jnp.zeros((head_count, row_count), jnp.float32)
    zeros_heads = jnp.zeros((head_count, row_count, head_size), jnp.float32)
    first_stats = (jnp.full((head_count, row_count), -1e30, jnp.float32), zeros_rows, zeros_rows)
    all_keys, all_values = (
        lax.all_gather(key_cache[0], "seq", axis=0, tiled=True),
        lax.all_gather(value_cache[0], "seq", axis=0, tiled=True),
    )
    peak, norm_sum, centre_sum = fold_keys(
        gather_stats, first_stats, all_keys, all_values, 0, query_heads, grad_heads, limits
    )
    grad_step = make_grads((peak, norm_sum, centre_sum / norm_sum))
    attended_sum, query_sum = fold_keys(
        grad_step,
        (zeros_heads, zeros_heads),
        all_keys,
        all_values,
        0,
        query_heads,
        grad_heads,
        limits,
    )
    attended = attended_sum.transpose(1, 0, 2).reshape(row_count, head_width).astype(jnp.bfloat16)
    grad_query_rows = (
        (query_sum * head_size ** (-0.5))
        .transpose(1, 0, 2)
        .reshape(row_count, head_width)
        .astype(jnp.bfloat16)
    )
    partial_value = lax.dot_general(
        attended, ordered, (((0,), (0,)), ((), ())), preferred_element_type=jnp.float32
    )
    reduced = lax.psum_scatter(
        partial_value.astype(jnp.bfloat16), "seq", scatter_dimension=0, tiled=True
    ).astype(jnp.float32)
    summed = lax.psum_scatter(reduced, "dp", scatter_dimension=1, tiled=True)
    return (grad_query_rows[None], summed / float(lax.axis_size("dp")))


def solution(mesh):
    in_specs = (
        P("dp", "seq", None),
        P("dp", "seq", None),
        P("dp", "seq", None),
        P("dp", "seq", None),
        P("dp", None),
        P("dp", None, None),
        P("dp", None),
    )
    out_specs = (P("dp", "seq", None), P("seq", "dp"))
    return jax.shard_map(shards, mesh=mesh, in_specs=in_specs, out_specs=out_specs, check_vma=False)
```

profile of v0, /device:TPU:6, one launch (start us, length us, event | category | flops | bytes accessed | tf_op | source)
XLA Modules:
  0.0 534.4 jit_solution(11950020743030907612)
XLA Ops:
  13.6 9.5 %all-to-all-start = ((bf16[32,8,1536]{2,1,0:T(8,128)(2,1)}), bf16[32,8,1536]{2,1,0:T(8,128)(2,1)S(1)}, u32[]{:S(2)}, u32[]{:S(2)}) async-start(bf16[32,8,1536]{2,1,0:T(8,128)(2,1)} %bitcast_select_fusion.2), calls=%async_computation | async-start | bytes 1572864 | tf_op jit(solution)/shard_map/all_to_all | solution.py:108
  24.3 10.9 %all-to-all-done = bf16[32,8,1536]{2,1,0:T(8,128)(2,1)S(1)} async-done(((bf16[32,8,1536]{2,1,0:T(8,128)(2,1)}), bf16[32,8,1536]{2,1,0:T(8,128)(2,1)S(1)}, u32[]{:S(2)}, u32[]{:S(2)}) %all-to-all-start) | async-done | bytes 786464 | tf_op jit(solution)/shard_map/all_to_all | solution.py:108
  36.0 52.6 %all-gather.6.cloned.1.call-done = bf16[768,1536]{1,0:T(8,128)(2,1)} async-done(((bf16[48,1536]{1,0:T(8,128)(2,1)}), bf16[768,1536]{1,0:T(8,128)(2,1)}) %all-gather.6.cloned.1.call-update) | async-done | bytes 2359312 | tf_op jit(solution)/shard_map/all_gather | solution.py:118
  88.6 2.5 convolution_convert_fusion.1
  92.2 60.1 %all-gather.8.cloned.1.call-done = bf16[1,4096,768]{2,1,0:T(8,128)(2,1)} async-done(((bf16[1,128,768]{2,1,0:T(8,128)(2,1)}), bf16[1,4096,768]{2,1,0:T(8,128)(2,1)}) %all-gather.8.cloned.1.call-update) | async-done | bytes 6291472 | tf_op jit(solution)/shard_map/all_gather | solution.py:137
  152.3 8.7 %copy.90 = bf16[8,512,768]{1,2,0:T(8,128)(2,1)} copy(bf16[8,512,768]{2,1,0:T(8,128)(2,1)} %bitcast.127) | data formatting | bytes 12582912
  160.9 58.0 %all-gather.10.cloned.1.call-done = bf16[1,4096,768]{2,1,0:T(8,128)(2,1)} async-done(((bf16[1,128,768]{2,1,0:T(8,128)(2,1)}), bf16[1,4096,768]{2,1,0:T(8,128)(2,1)}) %all-gather.10.cloned.1.call-update) | async-done | bytes 6291472 | tf_op jit(solution)/shard_map/all_gather | solution.py:138
  219.0 8.6 %copy.88 = bf16[8,512,768]{1,2,0:T(8,128)(2,1)} copy(bf16[8,512,768]{2,1,0:T(8,128)(2,1)} %bitcast.128) | data formatting | bytes 12582912
  227.6 42.1 %while.28 = (s32[]{:T(128)}, f32[6,128]{1,0:T(8,128)S(1)}, f32[6,128]{1,0:T(8,128)S(1)}, f32[6,128]{1,0:T(8,128)S(1)}, s32[8]{0:T(128)S(1)}, /*index=5*/s32[128]...) while((s32[]{:T(128)}, f32[6,128]{1,0:T(8,128)S(1)}, ...), condition=%wide.region_10.11_spmd.clone, body=%wide.region_6.10_spmd.clone.sunk | while | flops 205330176 | bytes 10152624 | solution.py:83
  231.0 1.6 fusion.55
  236.2 1.6 fusion.55
  239.5 1.5 constant_dynamic-slice_fusion.9
  241.5 1.6 fusion.55
  244.7 1.5 constant_dynamic-slice_fusion.9
  246.7 1.6 fusion.55
  250.0 1.5 constant_dynamic-slice_fusion.9
  252.0 1.6 fusion.55
  257.3 1.6 fusion.55
  262.5 1.6 fusion.55
  267.8 1.6 fusion.55
  270.2 77.4 %while.29 = (s32[]{:T(128)}, f32[6,128,128]{2,1,0:T(8,128)}, f32[6,128,128]{2,1,0:T(8,128)}, s32[8]{0:T(128)}, s32[128]{0:T(128)S(1)}, /*index=5*/bf16[8,512,768...) while((s32[]{:T(128)}, f32[6,128,128]{2,1,0:T(8,128)}, ...), condition=%wide.region_12.13_spmd.clone, body=%wide.region_11.12_spmd.clone.sunk | while | flops 406651392 | bytes 14694136 | solution.py:83
  273.7 1.6 fusion.65
  275.3 2.3 fusion.66
  282.3 1.6 fusion.65
  283.9 2.5 fusion.66
  286.4 2.2 convolution_add_fusion.2
  292.1 1.6 fusion.65
  293.7 2.5 fusion.66
  296.2 2.2 convolution_add_fusion.2
  301.9 1.6 fusion.65
  303.5 2.5 fusion.66
  306.1 2.2 convolution_add_fusion.2
  311.8 1.6 fusion.65
  313.4 2.5 fusion.66
  315.9 2.2 convolution_add_fusion.2
  321.6 1.6 fusion.65
  323.2 2.5 fusion.66
  325.7 2.2 convolution_add_fusion.2
  331.4 1.6 fusion.65
  333.0 2.5 fusion.66
  335.5 2.2 convolution_add_fusion.2
  341.2 1.6 fusion.65
  342.8 2.5 fusion.66
  345.3 2.2 convolution_add_fusion.2
  348.7 3.2 convolution_convert_fusion
  352.0 102.0 %reduce-scatter.5.cloned.1.call-done = bf16[24,1536]{1,0:T(8,128)(2,1)} async-done(((bf16[768,1536]{1,0:T(8,128)(2,1)}), bf16[24,1536]{1,0:T(8,128)(2,1)}) %reduce-scatter.5.cloned.1.call-update) | async-done | bytes 73744 | tf_op jit(solution)/shard_map/reduce_scatter | solution.py:164
  454.0 1.9 copy.105
  457.0 69.4 %reduce-scatter.7.cloned.1.call-done = f32[96,24]{1,0:T(8,128)} async-done(((f32[1536,24]{1,0:T(8,128)}), f32[96,24]{1,0:T(8,128)}) %reduce-scatter.7.cloned.1.call-update) | async-done | bytes 9232
  (193 shorter events, 57.3 us)
Async XLA Ops:
  7.2 4.0 copy-start
  7.2 81.5 %all-gather.6.cloned.1.call-start = ((), (), s32[]{:S(2)}) async-start(), calls=%async_computation.3 | async-start | bytes 2506752 | tf_op jit(solution)/shard_map/all_gather | solution.py:118
  7.9 144.4 %all-gather.8.cloned.1.call-start = ((), (), s32[]{:S(2)}) async-start(), calls=%async_computation.5 | async-start | bytes 6488064 | tf_op jit(solution)/shard_map/all_gather | solution.py:137
  8.7 210.3 %all-gather.10.cloned.1.call-start = ((), (), s32[]{:S(2)}) async-start(), calls=%async_computation.6 | async-start | bytes 6488064 | tf_op jit(solution)/shard_map/all_gather | solution.py:138
  11.2 1.3 copy-start.6
  12.6 10.6 %copy-start.7 = (s32[1,5]{1,0:T(1,128)S(1)}, s32[1,5]{1,0:T(1,128)}, u32[]{:S(2)}) copy-start(s32[1,5]{1,0:T(1,128)} %param.17) | copy-start | bytes 64
  12.6 11.1 %copy-start.5 = (bf16[1,128,768]{2,1,0:T(8,128)(2,1)S(1)}, bf16[1,128,768]{2,1,0:T(8,128)(2,1)}, u32[]{:S(2)}) copy-start(bf16[1,128,768]{2,1,0:T(8,128)(2,1)} %param.11) | copy-start | bytes 589828
  13.6 21.5 %all-to-all-start = ((bf16[32,8,1536]{2,1,0:T(8,128)(2,1)}), bf16[32,8,1536]{2,1,0:T(8,128)(2,1)S(1)}, u32[]{:S(2)}, u32[]{:S(2)}) async-start(bf16[32,8,1536]{2,1,0:T(8,128)(2,1)} %bitcast_select_fusion.2), calls=%async_computation | async-start | bytes 1572864 | tf_op jit(solution)/shard_map/all_to_all | solution.py:108
  23.1 430.9 %reduce-scatter.5.cloned.1.call-start = ((), (), s32[]{:S(2)}) async-start(), calls=%async_computation.4 | async-start | bytes 2433024 | tf_op jit(solution)/shard_map/reduce_scatter | solution.py:164
  36.0 55.3 %copy-start.4 = (bf16[128,1536]{1,0:T(8,128)(2,1)}, bf16[128,1536]{1,0:T(8,128)(2,1)S(1)}, u32[]{:S(2)}) copy-start(bf16[128,1536]{1,0:T(8,128)(2,1)S(1)} %gather_fusion.1) | copy-start | bytes 1179652
  270.2 1.9 copy-start.2
  277.6 1.2 copy-start.3
  278.8 1.9 copy-start.2
  286.4 2.2 copy-start.3
  288.6 1.9 copy-start.2
  296.2 2.2 copy-start.3
  298.4 1.9 copy-start.2
  306.1 2.2 copy-start.3
  308.3 1.9 copy-start.2
  315.9 2.2 copy-start.3
  318.1 1.9 copy-start.2
  325.7 2.2 copy-start.3
  327.9 1.9 copy-start.2
  335.5 2.2 copy-start.3
  337.7 1.9 copy-start.2
  345.3 2.2 copy-start.3
  351.9 104.0 %copy-start.1 = (f32[6,128,128]{2,1,0:T(8,128)S(1)}, f32[6,128,128]{2,1,0:T(8,128)}, u32[]{:S(2)}) copy-start(f32[6,128,128]{2,1,0:T(8,128)} %get-tuple-element.122) | copy-start | bytes 1179652
  351.9 174.5 %reduce-scatter.7.cloned.1.call-start = ((), (), s32[]{:S(2)}) async-start(), calls=%async_computation.7 | async-start | bytes 835584
Sparse Core Ops, SparseCore 0:
  10.1 78.5 all-gather.5
  91.8 60.4 all-gather.7
  155.4 63.5 all-gather.9
  352.0 101.8 reduce-scatter.4
  456.8 69.5 reduce-scatter.6
where the time goes:
time: 537 us; the launch traced here: 534 us
  waiting for transfers between devices  355 us (66%)
  matrix products  71.3 us (13%)
  local copies, waits for them, and re-layouts  64.9 us (12%)
  between operations  14 us (3%)
  loops' own time  10.8 us (2%)
  starting transfers between devices  9.65 us (2%)
  other arithmetic  8.67 us (2%)
    reduce_scatter x1, waiting for transfers between devices, shards(): lax.psum_scatter(partial_value.astype(jnp.bfloat16), 'seq', scatter_dimen...  102 us
    unnamed x6, waiting for transfers between devices  71.5 us
    all_gather x1, waiting for transfers between devices, shards(): lax.all_gather(key_cache[0], 'seq', axis=0, tiled=True)  60.1 us
    all_gather x1, waiting for transfers between devices, shards(): lax.all_gather(value_cache[0], 'seq', axis=0, tiled=True)  58 us
    all_gather x1, waiting for transfers between devices, shards(): lax.all_gather(out_weight, 'dp', axis=0, tiled=True)  52.6 us
    dynamic_slice x32, local copies, waits for them, and re-layouts, fold_keys(): running, _ = lax.scan(visit_block, running, stacked)  38.3 us
    unnamed x20, local copies, waits for them, and re-layouts  22.1 us
    dot_general x8, matrix products, add_grads(): jnp.einsum('hrn,nhd->hrd', grad_scores, key_heads, preferred_element_type...  20 us
  transfers between devices with their start and end apart: 6, of which 6 were waited for; matrix products, arithmetic and copies ran while one was open for 4% of the time, Pallas kernels for 0%

commit v1 on v0

v1 whole, which is shorter than its diff:
```python
import functools

import jax
import jax.numpy as jnp
from jax import lax
from jax.experimental import pallas as pl
from jax.experimental.pallas import tpu as pltpu
from jax.sharding import PartitionSpec as P

HEAD_DIM = 128
SIDE = 4
CORES = 2
LOG2_E = 1.4426950408889634
HIDDEN = -1e30
LOWEST = -1e20
MIB = 1024 * 1024
NT = (((1,), (1,)), ((), ()))
NN = (((1,), (0,)), ((), ()))


def moves(dy, dx, dcore):
    pairs = []
    for y in range(SIDE):
        for x in range(SIDE):
            for core in range(CORES):
                there = ((y + dy) % SIDE * SIDE + (x + dx) % SIDE) * CORES + (core + dcore) % CORES
                pairs.append(((y * SIDE + x) * CORES + core, there))
    return pairs


def send(value, dy=0, dx=0, dcore=0):
    return lax.ppermute(value, "seq", moves(dy, dx, dcore))


def tiles_of(refs):
    tiles = []
    for first in (0, 5):
        for place in range(3):
            tiles.append((refs[first + place].at[0], refs[first + place].at[1]))
        tiles.append((refs[first + 3], refs[first + 4]))
    return tiles


def forward_kernel(head_count, scale, limit_ref, place_ref, query_ref, *refs):
    tiles = tiles_of(refs[:10])
    attended_ref, exact_ref, level_ref = refs[10:]
    limits = limit_ref[...]
    rows = query_ref.shape[0]
    for head in range(head_count):
        columns = pl.ds(head * HEAD_DIM, HEAD_DIM)
        query = query_ref[:, columns]
        peak = jnp.full((rows, 1), LOWEST, jnp.float32)
        norm = jnp.zeros((rows, 1), jnp.float32)
        total = jnp.zeros((rows, HEAD_DIM), jnp.float32)
        for index, (key_ref, value_ref) in enumerate(tiles):
            scores = lax.dot_general(query, key_ref[:, columns], NT, preferred_element_type=jnp.float32)
            visible = place_ref[index : index + 1, :] < limits
            scores = jnp.where(visible, scores * (scale * LOG2_E), HIDDEN)
            new_peak = jnp.maximum(peak, jnp.max(scores, axis=1, keepdims=True))
            rescale = jnp.exp2(peak - new_peak)
            weights = jnp.exp2(scores - new_peak)
            norm = norm * rescale + jnp.sum(weights, axis=1, keepdims=True)
            total = total * rescale + lax.dot_general(
                weights.astype(jnp.bfloat16), value_ref[:, columns], NN, preferred_element_type=jnp.float32
            )
            peak = new_peak
        total = total / norm
        attended_ref[:, columns] = total.astype(jnp.bfloat16)
        exact_ref[:, columns] = total
        level_ref[:, columns] = jnp.broadcast_to(peak + jnp.log2(norm), (rows, HEAD_DIM))


def backward_kernel(head_count, scale, limit_ref, place_ref, query_ref, grad_ref, exact_ref, level_ref, *refs):
    tiles = tiles_of(refs[:10])
    out_ref = refs[10]
    limits = limit_ref[...]
    rows = query_ref.shape[0]
    for head in range(head_count):
        columns = pl.ds(head * HEAD_DIM, HEAD_DIM)
        query = query_ref[:, columns]
        grad = grad_ref[:, columns]
        level = level_ref[:, pl.ds(head * HEAD_DIM, 1)]
        centre = jnp.sum(grad.astype(jnp.float32) * exact_ref[:, columns], axis=1, keepdims=True)
        total = jnp.zeros((rows, HEAD_DIM), jnp.float32)
        for index, (key_ref, value_ref) in enumerate(tiles):
            keys = key_ref[:, columns]
            scores = lax.dot_general(query, keys, NT, preferred_element_type=jnp.float32)
            visible = place_ref[index : index + 1, :] < limits
            probs = jnp.exp2(jnp.where(visible, scores * (scale * LOG2_E) - level, HIDDEN))
            grad_probs = lax.dot_general(grad, value_ref[:, columns], NT, preferred_element_type=jnp.float32)
            grad_scores = (probs * (grad_probs - centre)).astype(jnp.bfloat16)
            total = total + lax.dot_general(grad_scores, keys, NN, preferred_element_type=jnp.float32)
        out_ref[:, columns] = (total * scale).astype(jnp.bfloat16)


def whole(count):
    return [pl.BlockSpec(memory_space=pltpu.VMEM)] * count


def order_rows(teacher_rows, counts, me):
    row_count, feature_count = teacher_rows.shape
    peer_count = counts.shape[0]
    capacity = 2 * row_count // peer_count
    mine = lax.dynamic_index_in_dim(counts, me, 0, keepdims=False)
    starts = jnp.cumsum(mine) - mine
    slot = jnp.arange(capacity, dtype=jnp.int32)
    source_row = jnp.minimum(starts[:, None] + slot[None, :], row_count - 1)
    packed = teacher_rows[source_row]
    arrived = lax.all_to_all(packed, "seq", split_axis=0, concat_axis=0, tiled=True)
    inbound = lax.dynamic_index_in_dim(counts, me, 1, keepdims=False)
    inbound_ends = jnp.cumsum(inbound)
    local_rows = jnp.arange(row_count, dtype=jnp.int32)
    earlier = inbound_ends[None, :] <= local_rows[:, None]
    sender = jnp.sum(earlier.astype(jnp.int32), axis=1)
    offset_in = local_rows - jnp.sum(jnp.where(earlier, inbound[None, :], 0), axis=1)
    return arrived.reshape(peer_count * capacity, feature_count)[sender * capacity + offset_in]


def shards(student_query, key_cache, value_cache, grad_rows, out_weight, return_counts, block_sizes):
    queries, keys, values = student_query[0], key_cache[0], value_cache[0]
    me = lax.axis_index("seq")
    core = me % CORES
    at_x = me // CORES % SIDE
    at_y = me // (CORES * SIDE)
    row_count, head_width = queries.shape
    width = head_width // CORES
    head_count = width // HEAD_DIM
    scale = HEAD_DIM ** -0.5
    peer_count = lax.axis_size("seq")
    clip_count = lax.axis_size("dp")

    def half(rows, which):
        return lax.dynamic_slice(rows, (0, which * width), (row_count, width))

    weight = lax.all_gather(out_weight, "dp", axis=0, tiled=True)
    mine = jnp.stack([half(keys, core), half(values, core)])
    swapped = send(jnp.stack([half(keys, 1 - core), half(values, 1 - core), half(queries, 1 - core)]), dcore=1)
    theirs = swapped[:2]
    query = jnp.concatenate([half(queries, core), swapped[2]], axis=0)

    def spread(block, first, second):
        row = jnp.concatenate(
            [block, send(block, **{first: 1}), send(block, **{first: -1}), send(block, **{first: 2})], axis=1
        )
        before = send(row, **{second: 1})
        after = send(row, **{second: -1})
        return [row, before, after, send(before[0], **{second: 1}), send(after[1], **{second: -1})]

    tiles = spread(mine, "dx", "dy") + spread(theirs, "dy", "dx")
    steps = jnp.array([0, -1, 1, 2], jnp.int32)
    near_y = (at_y + steps) % SIDE
    near_x = (at_x + steps) % SIDE
    seats = jnp.concatenate(
        [
            (near_y[:, None] * SIDE + near_x[None, :]) * CORES + core,
            (near_y[None, :] * SIDE + near_x[:, None]) * CORES + (1 - core),
        ],
        axis=0,
    )
    local_rows = jnp.arange(row_count, dtype=jnp.int32)
    places = (seats[:, :, None] * row_count + local_rows[None, None, :]).reshape(2 * SIDE, SIDE * row_count)

    block_ends = jnp.cumsum(block_sizes[0])
    positions = jnp.concatenate([me * row_count + local_rows, (me + 1 - 2 * core) * row_count + local_rows])
    limits = jnp.min(
        jnp.where(block_ends[None, :] > positions[:, None], block_ends[None, :], row_count * peer_count),
        axis=1,
        keepdims=True,
    )

    both = CORES * row_count
    attended, exact, level = pl.pallas_call(
        functools.partial(forward_kernel, head_count, scale),
        out_shape=[
            jax.ShapeDtypeStruct((both, width), jnp.bfloat16),
            jax.ShapeDtypeStruct((both, width), jnp.float32),
            jax.ShapeDtypeStruct((both, width), jnp.float32),
        ],
        in_specs=whole(13),
        out_specs=whole(3),
        compiler_params=pltpu.CompilerParams(vmem_limit_bytes=40 * MIB),
        cost_estimate=pl.CostEstimate(flops=int(8e9), bytes_accessed=int(8e6), transcendentals=0),
        name="attend",
    )(limits, places, query, *tiles)

    own_ordered = order_rows(grad_rows[0], return_counts[0], me)
    ordered = jnp.concatenate([own_ordered, send(own_ordered, dcore=1)], axis=0)
    partial_sum = lax.dot_general(
        attended, ordered, (((0,), (0,)), ((), ())), preferred_element_type=jnp.float32
    ).astype(jnp.bfloat16)
    chip_count = SIDE * SIDE
    share = width // chip_count
    groups = [[chip * CORES + which for chip in range(chip_count)] for which in range(CORES)]
    pieces = lax.all_to_all(
        partial_sum.reshape(chip_count, share, -1), "seq", 0, 0, axis_index_groups=groups, tiled=True
    )

    head_grad = lax.dot_general(
        ordered,
        lax.dynamic_slice_in_dim(weight, core * width, width, axis=0),
        NT,
        preferred_element_type=jnp.float32,
    ).astype(jnp.bfloat16)
    grad_query = pl.pallas_call(
        functools.partial(backward_kernel, head_count, scale),
        out_shape=jax.ShapeDtypeStruct((both, width), jnp.bfloat16),
        in_specs=whole(16),
        out_specs=pl.BlockSpec(memory_space=pltpu.VMEM),
        compiler_params=pltpu.CompilerParams(vmem_limit_bytes=40 * MIB),
        cost_estimate=pl.CostEstimate(flops=int(8e9), bytes_accessed=int(8e6), transcendentals=0),
        name="attend_grad",
    )(limits, places, query, head_grad, exact, level, *tiles)
    own_grad = grad_query[:row_count]
    other_grad = send(grad_query[row_count:], dcore=1)
    grad_query_rows = jnp.where(
        core == 0,
        jnp.concatenate([own_grad, other_grad], axis=1),
        jnp.concatenate([other_grad, own_grad], axis=1),
    )

    clip_sum = jnp.sum(pieces.astype(jnp.float32), axis=0)
    clip_parts = clip_sum.reshape(share, clip_count, -1).transpose(1, 0, 2)
    terms = lax.all_to_all(clip_parts, "dp", 0, 0, tiled=True)
    total = jnp.sum(terms, axis=0) / float(clip_count)
    total = lax.ppermute(
        total, "seq", [(chip * CORES + which, which * chip_count + chip) for chip in range(chip_count) for which in range(CORES)]
    )
    return (grad_query_rows[None], total)


def solution(mesh):
    in_specs = (
        P("dp", "seq", None),
        P("dp", "seq", None),
        P("dp", "seq", None),
        P("dp", "seq", None),
        P("dp", None),
        P("dp", None, None),
        P("dp", None),
    )
    out_specs = (P("dp", "seq", None), P("seq", "dp"))
    return jax.shard_map(shards, mesh=mesh, in_specs=in_specs, out_specs=out_specs, check_vma=False)
```

time: 537 us -> 211 us (0.39)
  waiting for transfers between devices: 355 us -> 27.2 us
  matrix products: 71.3 us -> 2.73 us
  starting transfers between devices: 9.65 us -> 65.8 us
  blocking collectives: 0 us -> 52.6 us
  local copies, waits for them, and re-layouts: 64.9 us -> 19.3 us
  Pallas kernels: 0 us -> 17.8 us
  loops' own time: 10.8 us -> 0 us
    all_gather x3 -> x1, waiting for transfers between devices: 171 us -> 0.01 us  [shards(): weight = lax.all_gather(out_weight, 'dp', axis=0, tiled=True)]
    reduce_scatter x1 -> x0, waiting for transfers between devices: 102 us -> none  [shards(): lax.psum_scatter(partial_value.astype(jnp.bfloat16), 'seq', scatter_dimen...]
    unnamed x6 -> x1, waiting for transfers between devices: 71.5 us -> 0.02 us
    dot_general x41 -> x1, matrix products: 68.1 us -> 2.23 us  [shards(): lax.dot_general(ordered, lax.dynamic_slice_in_dim(weight, core * width, w...]
    ppermute x0 -> x18, starting transfers between devices: none -> 59.4 us  [the longest x17 54.9 us: send(): return lax.ppermute(value, 'seq', moves(dy, dx, dcore))]
    all_to_all x0 -> x2, blocking collectives: none -> 52.6 us  [the longest x1 29.5 us: shards(): terms = lax.all_to_all(clip_parts, 'dp', 0, 0, tiled=True)]
    dynamic_slice x33 -> x3, local copies, waits for them, and re-layouts: 38.5 us -> 2.87 us  [the longest x2 2.69 us: half(): return lax.dynamic_slice(rows, (0, which * width), (row_count, width))]
    ppermute x0 -> x18, waiting for transfers between devices: none -> 27.1 us  [the longest x17 25.1 us: send(): return lax.ppermute(value, 'seq', moves(dy, dx, dcore))]
  transfers between devices with their start and end apart: 6 -> 20, of which waited for: 6 -> 6; matrix products, arithmetic and copies ran while one was open for 4% -> 10% of each run, Pallas kernels for 0% -> 5%
where the time goes in v1:
time: 211 us; the launch traced here: 208 us
  starting transfers between devices  65.8 us (31%)
  blocking collectives  52.6 us (25%)
  waiting for transfers between devices  27.2 us (13%)
  local copies, waits for them, and re-layouts  19.3 us (9%)
  Pallas kernels  17.8 us (8%)
  between operations  14.7 us (7%)
  other arithmetic  7.79 us (4%)
  matrix products  2.73 us (1%)
    ppermute x17, starting transfers between devices, send(): return lax.ppermute(value, 'seq', moves(dy, dx, dcore))  54.9 us
    all_to_all x1, blocking collectives, shards(): terms = lax.all_to_all(clip_parts, 'dp', 0, 0, tiled=True)  29.5 us
    ppermute x17, waiting for transfers between devices, send(): return lax.ppermute(value, 'seq', moves(dy, dx, dcore))  25.1 us
    all_to_all x1, blocking collectives, shards(): lax.all_to_all(partial_sum.reshape(chip_count, share, -1), 'seq', 0, 0, a...  23.1 us
    pallas_call x1, Pallas kernels, shards(): pl.pallas_call(functools.partial(forward_kernel, head_count, scale), out_...  9.4 us
    pallas_call x1, Pallas kernels, shards(): pl.pallas_call(functools.partial(backward_kernel, head_count, scale), out...  8.36 us
    all_to_all x1, starting transfers between devices, order_rows(): lax.all_to_all(packed, 'seq', split_axis=0, concat_axis=0, tiled=True)  6.41 us
    ppermute x1, starting transfers between devices, shards(): lax.ppermute(total, 'seq', [(chip * CORES + which, which * chip_count + c...  4.44 us
  transfers between devices with their start and end apart: 20, of which 6 were waited for; matrix products, arithmetic and copies ran while one was open for 10% of the time, Pallas kernels for 5%

profile of v1, /device:TPU:6, one launch (start us, length us, event | category | flops | bytes accessed | tf_op | source)
XLA Modules:
  0.0 207.9 jit_solution(11287968719114023981)
XLA Ops:
  7.3 1.0 constant_dynamic-slice_fusion.1
  8.2 1.7 dynamic-slice_bitcast_fusion
  10.0 3.3 %collective-permute-start.4 = (bf16[2,128,384]{2,1,0:T(8,128)(2,1)S(1)}, bf16[2,128,384]{2,1,0:T(8,128)(2,1)S(1)}, u32[]{:S(2)}, u32[]{:S(2)}) collective-permute-start(bf16[2,128,384]{2,1,0:T(8,128)(2,1)S(1)} %pad_maximum_fusion.4), channel_id=1, source_target_pairs={{0,64},{16,80},{32,96},{48,112},{64,0},{80,16},{96,32},{112,48},{1... | collective-permute-start | bytes 589832 | tf_op jit(solution)/shard_map/ppermute | solution.py:32
  13.3 7.2 %collective-permute-start.3 = (bf16[2,128,384]{2,1,0:T(8,128)(2,1)S(1)}, bf16[2,128,384]{2,1,0:T(8,128)(2,1)S(1)}, u32[]{:S(2)}, u32[]{:S(2)}) collective-permute-start(bf16[2,128,384]{2,1,0:T(8,128)(2,1)S(1)} %pad_maximum_fusion.4), channel_id=1, source_target_pairs={{0,96},{16,112},{32,0},{48,16},{64,32},{80,48},{96,64},{112,80},{1... | collective-permute-start | bytes 589832 | tf_op jit(solution)/shard_map/ppermute | solution.py:32
  20.5 1.9 collective-permute-start.2
  22.5 1.9 collective-permute-start
  25.0 2.2 %gather_fusion = bf16[256,1536]{1,0:T(8,128)(2,1)} fusion(bf16[128,1536]{1,0:T(8,128)(2,1)S(1)} %bitcast.48, s32[1024]{0:T(1024)S(1)} %pad_clamp_fusion.1), kind=kCustom, calls=%fused_computation | custom fusion | bytes 1573888 | tf_op jit(solution)/shard_map/gather | solution.py:108
  27.1 6.4 %all-to-all-start = ((bf16[32,8,1536]{2,1,0:T(8,128)(2,1)}), bf16[32,8,1536]{2,1,0:T(8,128)(2,1)}, u32[]{:S(2)}, u32[]{:S(2)}) async-start(bf16[32,8,1536]{2,1,0:T(8,128)(2,1)} %bitcast.10), calls=%async_computation | async-start | bytes 1572864 | tf_op jit(solution)/shard_map/all_to_all | solution.py:109
  34.6 4.7 %collective-permute-start.6 = (bf16[2,512,384]{2,1,0:T(8,128)(2,1)S(1)}, bf16[2,512,384]{2,1,0:T(8,128)(2,1)S(1)}, u32[]{:S(2)}, u32[]{:S(2)}) collective-permute-start(bf16[2,512,384]{2,1,0:T(8,128)(2,1)S(1)} %pad_maximum_fusion.refs_0_), channel_id=1, source_target_pairs={{0,384},{16,400},{32,416},{48,432},{64,448},{80,464},{96,480},{112... | collective-permute-start | bytes 2359304 | tf_op jit(solution)/shard_map/ppermute | solution.py:32
  39.3 0.7 slice.39
  40.1 2.7 %collective-permute-start.11 = (bf16[2,128,384]{2,1,0:T(8,128)(2,1)}, bf16[2,128,384]{2,1,0:T(8,128)(2,1)S(1)}, u32[]{:S(2)}, u32[]{:S(2)}) collective-permute-start(bf16[2,128,384]{2,1,0:T(8,128)(2,1)} %slice.39), channel_id=1, source_target_pairs={{0,256},{16,272},{32,288},{48,304},{64,320},{80,336},{96,352},{112... | collective-permute-start | bytes 589832 | tf_op jit(solution)/shard_map/ppermute | solution.py:32
  42.8 3.1 %collective-permute-start.10 = (bf16[2,128,384]{2,1,0:T(8,128)(2,1)}, bf16[2,128,384]{2,1,0:T(8,128)(2,1)S(1)}, u32[]{:S(2)}, u32[]{:S(2)}) collective-permute-start(bf16[2,128,384]{2,1,0:T(8,128)(2,1)} %slice.39), channel_id=1, source_target_pairs={{0,384},{16,400},{32,416},{48,432},{64,448},{80,464},{96,480},{112... | collective-permute-start | bytes 589832 | tf_op jit(solution)/shard_map/ppermute | solution.py:32
  45.8 2.8 %collective-permute-start.9 = (bf16[2,128,384]{2,1,0:T(8,128)(2,1)}, bf16[2,128,384]{2,1,0:T(8,128)(2,1)}, u32[]{:S(2)}, u32[]{:S(2)}) collective-permute-start(bf16[2,128,384]{2,1,0:T(8,128)(2,1)} %slice.39), channel_id=1, source_target_pairs={{0,128},{16,144},{32,160},{48,176},{64,192},{80,208},{96,224},{112... | collective-permute-start | bytes 589832 | tf_op jit(solution)/shard_map/ppermute | solution.py:32
  48.7 0.8 copy.28.limit_ref
  49.5 2.8 %collective-permute-start.5 = (bf16[2,512,384]{2,1,0:T(8,128)(2,1)S(1)}, bf16[2,512,384]{2,1,0:T(8,128)(2,1)S(1)}, u32[]{:S(2)}, u32[]{:S(2)}) collective-permute-start(bf16[2,512,384]{2,1,0:T(8,128)(2,1)S(1)} %pad_maximum_fusion.refs_0_), channel_id=1, source_target_pairs={{0,128},{16,144},{32,160},{48,176},{64,192},{80,208},{96,224},{112... | collective-permute-start | bytes 2359304 | tf_op jit(solution)/shard_map/ppermute | solution.py:32
  52.9 16.9 %collective-permute-done.10 = bf16[2,128,384]{2,1,0:T(8,128)(2,1)S(1)} collective-permute-done((bf16[2,128,384]{2,1,0:T(8,128)(2,1)}, bf16[2,128,384]{2,1,0:T(8,128)(2,1)S(1)}, u32[]{:S(2)}, u32[]{:S(2)}) %collective-permute-start.10) | collective-permute-done | bytes 196640 | tf_op jit(solution)/shard_map/ppermute | solution.py:32
  70.5 1.3 pad_maximum_fusion.1.refs_5_
  71.8 2.8 %collective-permute-start.13 = (bf16[2,512,384]{2,1,0:T(8,128)(2,1)S(1)}, bf16[2,512,384]{2,1,0:T(8,128)(2,1)}, u32[]{:S(2)}, u32[]{:S(2)}) collective-permute-start(bf16[2,512,384]{2,1,0:T(8,128)(2,1)S(1)} %pad_maximum_fusion.1.refs_5_), channel_id=1, source_target_pairs={{0,96},{16,112},{32,0},{48,16},{64,32},{80,48},{96,64},{112,80},{1... | collective-permute-start | bytes 2359304 | tf_op jit(solution)/shard_map/ppermute | solution.py:32
  74.6 0.9 slice_bitcast_fusion.5
  75.5 4.3 %collective-permute-start.12 = (bf16[2,512,384]{2,1,0:T(8,128)(2,1)S(1)}, bf16[2,512,384]{2,1,0:T(8,128)(2,1)}, u32[]{:S(2)}, u32[]{:S(2)}) collective-permute-start(bf16[2,512,384]{2,1,0:T(8,128)(2,1)S(1)} %pad_maximum_fusion.1.refs_5_), channel_id=1, source_target_pairs={{0,32},{16,48},{32,64},{48,80},{64,96},{80,112},{96,0},{112,16},{1... | collective-permute-start | bytes 2359304 | tf_op jit(solution)/shard_map/ppermute | solution.py:32
  79.8 1.6 pad_maximum_fusion.3.query_ref
  81.4 3.4 %gather_fusion.1 = bf16[128,1536]{1,0:T(8,128)(2,1)} fusion(bf16[256,1536]{1,0:T(8,128)(2,1)} %bitcast.11, s32[1024]{0:T(1024)} %pad_clamp_fusion), kind=kCustom, calls=%fused_computation.1 | custom fusion | bytes 786944 | tf_op jit(solution)/shard_map/gather | solution.py:116
  84.7 2.0 collective-permute-start.1
  86.8 4.3 %collective-permute-start.8 = (bf16[512,384]{1,0:T(8,128)(2,1)S(1)}, bf16[512,384]{1,0:T(8,128)(2,1)S(1)}, u32[]{:S(2)}, u32[]{:S(2)}) collective-permute-start(bf16[512,384]{1,0:T(8,128)(2,1)S(1)} %slice_bitcast_fusion.2), channel_id=1, source_target_pairs={{0,384},{16,400},{32,416},{48,432},{64,448},{80,464},{96,480},{112... | collective-permute-start | bytes 1179656 | tf_op jit(solution)/shard_map/ppermute | solution.py:32
  91.2 2.1 collective-permute-start.7
  93.3 1.1 collective-permute-done.13.refs_7_
  94.4 1.0 slice_bitcast_fusion
  95.4 1.9 collective-permute-start.15
  97.4 1.0 slice_bitcast_fusion.1
  98.4 5.3 %collective-permute-start.14 = (bf16[512,384]{1,0:T(8,128)(2,1)S(1)}, bf16[512,384]{1,0:T(8,128)(2,1)S(1)}, u32[]{:S(2)}, u32[]{:S(2)}) collective-permute-start(bf16[512,384]{1,0:T(8,128)(2,1)S(1)} %slice_bitcast_fusion.1), channel_id=1, source_target_pairs={{0,32},{16,48},{32,64},{48,80},{64,96},{80,112},{96,0},{112,16},{1... | collective-permute-start | bytes 1179656 | tf_op jit(solution)/shard_map/ppermute | solution.py:32
  103.8 1.8 collective-permute-done.7.refs_3_
  105.7 3.0 %collective-permute-done.15.refs_9_ = bf16[512,384]{1,0:T(8,128)(2,1)S(1)} collective-permute-done((bf16[512,384]{1,0:T(8,128)(2,1)S(1)}, bf16[512,384]{1,0:T(8,128)(2,1)S(1)}, u32[]{:S(2)}, u32[]{:S(2)}) %collective-permute-start.15) | collective-permute-done | bytes 393248 | tf_op jit(solution)/shard_map/ppermute | solution.py:32
  108.7 2.2 %collective-permute-done.14.refs_8_ = bf16[512,384]{1,0:T(8,128)(2,1)S(1)} collective-permute-done((bf16[512,384]{1,0:T(8,128)(2,1)S(1)}, bf16[512,384]{1,0:T(8,128)(2,1)S(1)}, u32[]{:S(2)}, u32[]{:S(2)}) %collective-permute-start.14) | collective-permute-done | bytes 393248 | tf_op jit(solution)/shard_map/ppermute | solution.py:32
  110.9 9.4 %attend.1 = (bf16[256,384]{1,0:T(8,128)(2,1)S(1)}, f32[256,384]{1,0:T(8,128)S(1)}, f32[256,384]{1,0:T(8,128)S(1)}) custom-call(s32[256,1]{1,0:T(8,128)S(1)} %copy-done.3, s32[8,512]{1,0:T(8,128)S(1)} %bitcast_add_fusion.place_ref, bf16[256,384]{1,0:T(8,128)(2,1)S(1)} %copy-done.1, bf16[2,512,384]{2,1,0:T(8,128)(2,1)S(1)} %pad_maximum_fusion.refs_0_, ...), custom_call_target="tpu_custom_call" | custom-call | flops 8000000000 | bytes 8000000 | tf_op jit(solution)/shard_map/attend/pallas_call | solution.py:172
  120.9 23.1 %all_to_all.15 = bf16[16,24,1536]{2,1,0:T(8,128)(2,1)S(1)} all-to-all(bf16[16,24,1536]{2,1,0:T(8,128)(2,1)S(1)} %bitcast.49), channel_id=1, replica_groups={{0,32,64,96,128,160,192,224,256,288,320,352,384,416,448,480},{16,48,80,..., dimensions={0} | all-to-all | bytes 2359296 | tf_op jit(solution)/shard_map/all_to_all | solution.py:194
  144.0 0.8 convert_reduce_fusion
  144.8 1.7 reshape.296
  146.5 1.0 copy.29
  147.5 29.5 %all_to_all.16 = f32[16,24,96]{2,1,0:T(8,128)} all-to-all(f32[16,24,96]{2,1,0:T(8,128)S(1)} %copy.29), channel_id=1, replica_groups=mesh['seq'=32,'dp'=16] {'dp'}, dimensions={0} | all-to-all | bytes 294912 | tf_op jit(solution)/shard_map/all_to_all | solution.py:223
  177.0 1.5 reduce_sum.42
  178.6 2.2 %fusion.2.grad_ref = bf16[256,384]{1,0:T(8,128)(2,1)S(1)} fusion(bf16[256,1536]{1,0:T(8,128)(2,1)} %copy-done.17, bf16[768,1536]{1,0:T(8,128)(2,1)} %all-gather.2.cloned.1.call-done, s32[]{:T(128)S(6)} %select_n.96), kind=kOutput, calls=%fused_computation.6 | convolution fusion | flops 302088192 | bytes 2162692 | tf_op jit(solution)/shard_map/dot_general | solution.py:198
  180.9 1.0 copy-done.14
  181.9 1.0 copy-done.16
  182.9 8.4 %attend_grad.1 = bf16[256,384]{1,0:T(8,128)(2,1)S(1)} custom-call(s32[256,1]{1,0:T(8,128)S(1)} %copy-done.4, s32[8,512]{1,0:T(8,128)S(1)} %bitcast_add_fusion.place_ref, bf16[256,384]{1,0:T(8,128)(2,1)S(1)} %copy-done.2, bf16[256,384]{1,0:T(8,128)(2,1)S(1)} %fusion.2.grad_ref, f32[256,384]{1,0:T(8,128)S(1)} %copy-done.14, f32[256,384]{1,0:T(8,128)S(1)} %copy-done.16, ...), custom_call_target="tpu_custom_call" | custom-call | flops 8000000000 | bytes 8000000 | tf_op jit(solution)/shard_map/attend_grad/pallas_call | solution.py:204
  191.3 1.9 collective-permute-start.16
  193.2 4.4 %collective-permute-start.17 = (f32[24,96]{1,0:T(8,128)S(1)}, f32[24,96]{1,0:T(8,128)S(1)}, u32[]{:S(2)}, u32[]{:S(2)}) collective-permute-start(f32[24,96]{1,0:T(8,128)S(1)} %broadcast_multiply_fusion), channel_id=1, source_target_pairs={{0,0},{16,256},{32,16},{48,272},{64,32},{80,288},{96,48},{112,304}... | collective-permute-start | bytes 27656 | tf_op jit(solution)/shard_map/ppermute | solution.py:225
  197.7 2.0 collective-permute-done.17
  199.7 0.7 maximum_select_fusion
  (100 shorter events, 4.3 us)
Async XLA Ops:
  7.2 17.8 %copy-start = (bf16[1,128,1536]{2,1,0:T(8,128)(2,1)S(1)}, bf16[1,128,1536]{2,1,0:T(8,128)(2,1)}, u32[]{:S(2)}) copy-start(bf16[1,128,1536]{2,1,0:T(8,128)(2,1)} %param.11) | copy-start | bytes 1179652
  7.2 17.3 %copy-start.23 = (s32[1,32,32]{2,1,0:T(8,128)S(1)}, s32[1,32,32]{2,1,0:T(8,128)}, u32[]{:S(2)}) copy-start(s32[1,32,32]{2,1,0:T(8,128)} %param.13) | copy-start | bytes 12292
  7.2 171.4 %all-gather.2.cloned.1.call-start = ((), (), s32[]{:S(2)}) async-start(), calls=%async_computation.3 | async-start | bytes 2506752 | tf_op jit(solution)/shard_map/all_gather | solution.py:135
  10.0 24.5 %collective-permute-start.4 = (bf16[2,128,384]{2,1,0:T(8,128)(2,1)S(1)}, bf16[2,128,384]{2,1,0:T(8,128)(2,1)S(1)}, u32[]{:S(2)}, u32[]{:S(2)}) collective-permute-start(bf16[2,128,384]{2,1,0:T(8,128)(2,1)S(1)} %pad_maximum_fusion.4), channel_id=1, source_target_pairs={{0,64},{16,80},{32,96},{48,112},{64,0},{80,16},{96,32},{112,48},{1... | collective-permute-start | bytes 589832 | tf_op jit(solution)/shard_map/ppermute | solution.py:32
  13.3 21.2 %collective-permute-start.3 = (bf16[2,128,384]{2,1,0:T(8,128)(2,1)S(1)}, bf16[2,128,384]{2,1,0:T(8,128)(2,1)S(1)}, u32[]{:S(2)}, u32[]{:S(2)}) collective-permute-start(bf16[2,128,384]{2,1,0:T(8,128)(2,1)S(1)} %pad_maximum_fusion.4), channel_id=1, source_target_pairs={{0,96},{16,112},{32,0},{48,16},{64,32},{80,48},{96,64},{112,80},{1... | collective-permute-start | bytes 589832 | tf_op jit(solution)/shard_map/ppermute | solution.py:32
  20.5 14.0 %collective-permute-start.2 = (bf16[2,128,384]{2,1,0:T(8,128)(2,1)S(1)}, bf16[2,128,384]{2,1,0:T(8,128)(2,1)S(1)}, u32[]{:S(2)}, u32[]{:S(2)}) collective-permute-start(bf16[2,128,384]{2,1,0:T(8,128)(2,1)S(1)} %pad_maximum_fusion.4), channel_id=1, source_target_pairs={{0,32},{16,48},{32,64},{48,80},{64,96},{80,112},{96,0},{112,16},{1... | collective-permute-start | bytes 589832 | tf_op jit(solution)/shard_map/ppermute | solution.py:32
  22.5 16.8 %collective-permute-start = (bf16[3,128,384]{2,1,0:T(8,128)(2,1)S(1)}, bf16[3,128,384]{2,1,0:T(8,128)(2,1)S(1)}, u32[]{:S(2)}, u32[]{:S(2)}) collective-permute-start(bf16[3,128,384]{2,1,0:T(8,128)(2,1)S(1)} %pad_maximum_fusion.2), channel_id=1, source_target_pairs={{0,16},{16,0},{32,48},{48,32},{64,80},{80,64},{96,112},{112,96},{1... | collective-permute-start | bytes 884744 | tf_op jit(solution)/shard_map/ppermute | solution.py:32
  27.1 6.8 %copy-start.24 = (s32[4]{0:T(128)S(1)}, s32[4]{0:T(128)}, u32[]{:S(2)}) copy-start(s32[4]{0:T(128)} %constant.119.clone) | copy-start | bytes 52
  27.1 7.2 %copy-start.25 = (s32[1,5]{1,0:T(1,128)S(1)}, s32[1,5]{1,0:T(1,128)}, u32[]{:S(2)}) copy-start(s32[1,5]{1,0:T(1,128)} %param.14) | copy-start | bytes 64
  27.1 54.2 %all-to-all-start = ((bf16[32,8,1536]{2,1,0:T(8,128)(2,1)}), bf16[32,8,1536]{2,1,0:T(8,128)(2,1)}, u32[]{:S(2)}, u32[]{:S(2)}) async-start(bf16[32,8,1536]{2,1,0:T(8,128)(2,1)} %bitcast.10), calls=%async_computation | async-start | bytes 1572864 | tf_op jit(solution)/shard_map/all_to_all | solution.py:109
  34.6 52.2 %collective-permute-start.6 = (bf16[2,512,384]{2,1,0:T(8,128)(2,1)S(1)}, bf16[2,512,384]{2,1,0:T(8,128)(2,1)S(1)}, u32[]{:S(2)}, u32[]{:S(2)}) collective-permute-start(bf16[2,512,384]{2,1,0:T(8,128)(2,1)S(1)} %pad_maximum_fusion.refs_0_), channel_id=1, source_target_pairs={{0,384},{16,400},{32,416},{48,432},{64,448},{80,464},{96,480},{112... | collective-permute-start | bytes 2359304 | tf_op jit(solution)/shard_map/ppermute | solution.py:32
  39.3 9.4 %copy-start.19 = (bf16[3,128,384]{2,1,0:T(8,128)(2,1)}, bf16[3,128,384]{2,1,0:T(8,128)(2,1)S(1)}, u32[]{:S(2)}) copy-start(bf16[3,128,384]{2,1,0:T(8,128)(2,1)S(1)} %collective-permute-done) | copy-start | bytes 884740
  40.1 12.8 %collective-permute-start.11 = (bf16[2,128,384]{2,1,0:T(8,128)(2,1)}, bf16[2,128,384]{2,1,0:T(8,128)(2,1)S(1)}, u32[]{:S(2)}, u32[]{:S(2)}) collective-permute-start(bf16[2,128,384]{2,1,0:T(8,128)(2,1)} %slice.39), channel_id=1, source_target_pairs={{0,256},{16,272},{32,288},{48,304},{64,320},{80,336},{96,352},{112... | collective-permute-start | bytes 589832 | tf_op jit(solution)/shard_map/ppermute | solution.py:32
  42.8 27.0 %collective-permute-start.10 = (bf16[2,128,384]{2,1,0:T(8,128)(2,1)}, bf16[2,128,384]{2,1,0:T(8,128)(2,1)S(1)}, u32[]{:S(2)}, u32[]{:S(2)}) collective-permute-start(bf16[2,128,384]{2,1,0:T(8,128)(2,1)} %slice.39), channel_id=1, source_target_pairs={{0,384},{16,400},{32,416},{48,432},{64,448},{80,464},{96,480},{112... | collective-permute-start | bytes 589832 | tf_op jit(solution)/shard_map/ppermute | solution.py:32
  45.8 24.6 %collective-permute-start.9 = (bf16[2,128,384]{2,1,0:T(8,128)(2,1)}, bf16[2,128,384]{2,1,0:T(8,128)(2,1)}, u32[]{:S(2)}, u32[]{:S(2)}) collective-permute-start(bf16[2,128,384]{2,1,0:T(8,128)(2,1)} %slice.39), channel_id=1, source_target_pairs={{0,128},{16,144},{32,160},{48,176},{64,192},{80,208},{96,224},{112... | collective-permute-start | bytes 589832 | tf_op jit(solution)/shard_map/ppermute | solution.py:32
  49.5 41.6 %collective-permute-start.5 = (bf16[2,512,384]{2,1,0:T(8,128)(2,1)S(1)}, bf16[2,512,384]{2,1,0:T(8,128)(2,1)S(1)}, u32[]{:S(2)}, u32[]{:S(2)}) collective-permute-start(bf16[2,512,384]{2,1,0:T(8,128)(2,1)S(1)} %pad_maximum_fusion.refs_0_), channel_id=1, source_target_pairs={{0,128},{16,144},{32,160},{48,176},{64,192},{80,208},{96,224},{112... | collective-permute-start | bytes 2359304 | tf_op jit(solution)/shard_map/ppermute | solution.py:32
  52.9 16.9 %copy-start.20 = (bf16[2,128,384]{2,1,0:T(8,128)(2,1)}, bf16[2,128,384]{2,1,0:T(8,128)(2,1)S(1)}, u32[]{:S(2)}) copy-start(bf16[2,128,384]{2,1,0:T(8,128)(2,1)S(1)} %collective-permute-done.11) | copy-start | bytes 589828
  69.8 0.7 copy-start.21
  71.8 22.6 %collective-permute-start.13 = (bf16[2,512,384]{2,1,0:T(8,128)(2,1)S(1)}, bf16[2,512,384]{2,1,0:T(8,128)(2,1)}, u32[]{:S(2)}, u32[]{:S(2)}) collective-permute-start(bf16[2,512,384]{2,1,0:T(8,128)(2,1)S(1)} %pad_maximum_fusion.1.refs_5_), channel_id=1, source_target_pairs={{0,96},{16,112},{32,0},{48,16},{64,32},{80,48},{96,64},{112,80},{1... | collective-permute-start | bytes 2359304 | tf_op jit(solution)/shard_map/ppermute | solution.py:32
  75.5 21.9 %collective-permute-start.12 = (bf16[2,512,384]{2,1,0:T(8,128)(2,1)S(1)}, bf16[2,512,384]{2,1,0:T(8,128)(2,1)}, u32[]{:S(2)}, u32[]{:S(2)}) collective-permute-start(bf16[2,512,384]{2,1,0:T(8,128)(2,1)S(1)} %pad_maximum_fusion.1.refs_5_), channel_id=1, source_target_pairs={{0,32},{16,48},{32,64},{48,80},{64,96},{80,112},{96,0},{112,16},{1... | collective-permute-start | bytes 2359304 | tf_op jit(solution)/shard_map/ppermute | solution.py:32
  84.7 19.0 %copy-start.18 = (bf16[128,1536]{1,0:T(8,128)(2,1)S(1)}, bf16[128,1536]{1,0:T(8,128)(2,1)}, u32[]{:S(2)}) copy-start(bf16[128,1536]{1,0:T(8,128)(2,1)} %gather_fusion.1) | copy-start | bytes 1179652
  84.7 19.0 %collective-permute-start.1 = (bf16[128,1536]{1,0:T(8,128)(2,1)}, bf16[128,1536]{1,0:T(8,128)(2,1)S(1)}, u32[]{:S(2)}, u32[]{:S(2)}) collective-permute-start(bf16[128,1536]{1,0:T(8,128)(2,1)} %gather_fusion.1), channel_id=1, source_target_pairs={{0,16},{16,0},{32,48},{48,32},{64,80},{80,64},{96,112},{112,96},{1... | collective-permute-start | bytes 1179656 | tf_op jit(solution)/shard_map/ppermute | solution.py:32
  86.8 17.0 %collective-permute-start.8 = (bf16[512,384]{1,0:T(8,128)(2,1)S(1)}, bf16[512,384]{1,0:T(8,128)(2,1)S(1)}, u32[]{:S(2)}, u32[]{:S(2)}) collective-permute-start(bf16[512,384]{1,0:T(8,128)(2,1)S(1)} %slice_bitcast_fusion.2), channel_id=1, source_target_pairs={{0,384},{16,400},{32,416},{48,432},{64,448},{80,464},{96,480},{112... | collective-permute-start | bytes 1179656 | tf_op jit(solution)/shard_map/ppermute | solution.py:32
  91.2 19.7 %copy-start.1 = (bf16[256,384]{1,0:T(8,128)(2,1)S(1)}, bf16[256,384]{1,0:T(8,128)(2,1)}, u32[]{:S(2)}) copy-start(bf16[256,384]{1,0:T(8,128)(2,1)} %pad_maximum_fusion.3.query_ref) | copy-start | bytes 589828
  91.2 19.7 %copy-start.3 = (s32[256,1]{1,0:T(8,128)S(1)}, s32[256,1]{1,0:T(8,128)}, u32[]{:S(2)}) copy-start(s32[256,1]{1,0:T(8,128)} %copy.28.limit_ref) | copy-start | bytes 3076
  91.2 14.5 %collective-permute-start.7 = (bf16[512,384]{1,0:T(8,128)(2,1)S(1)}, bf16[512,384]{1,0:T(8,128)(2,1)S(1)}, u32[]{:S(2)}, u32[]{:S(2)}) collective-permute-start(bf16[512,384]{1,0:T(8,128)(2,1)S(1)} %slice_bitcast_fusion.3), channel_id=1, source_target_pairs={{0,128},{16,144},{32,160},{48,176},{64,192},{80,208},{96,224},{112... | collective-permute-start | bytes 1179656 | tf_op jit(solution)/shard_map/ppermute | solution.py:32
  95.4 13.2 %collective-permute-start.15 = (bf16[512,384]{1,0:T(8,128)(2,1)S(1)}, bf16[512,384]{1,0:T(8,128)(2,1)S(1)}, u32[]{:S(2)}, u32[]{:S(2)}) collective-permute-start(bf16[512,384]{1,0:T(8,128)(2,1)S(1)} %slice_bitcast_fusion), channel_id=1, source_target_pairs={{0,96},{16,112},{32,0},{48,16},{64,32},{80,48},{96,64},{112,80},{1... | collective-permute-start | bytes 1179656 | tf_op jit(solution)/shard_map/ppermute | solution.py:32
  98.4 12.5 %collective-permute-start.14 = (bf16[512,384]{1,0:T(8,128)(2,1)S(1)}, bf16[512,384]{1,0:T(8,128)(2,1)S(1)}, u32[]{:S(2)}, u32[]{:S(2)}) collective-permute-start(bf16[512,384]{1,0:T(8,128)(2,1)S(1)} %slice_bitcast_fusion.1), channel_id=1, source_target_pairs={{0,32},{16,48},{32,64},{48,80},{64,96},{80,112},{96,0},{112,16},{1... | collective-permute-start | bytes 1179656 | tf_op jit(solution)/shard_map/ppermute | solution.py:32
  103.8 16.6 %copy-start.17 = (bf16[256,1536]{1,0:T(8,128)(2,1)}, bf16[256,1536]{1,0:T(8,128)(2,1)S(1)}, u32[]{:S(2)}) copy-start(bf16[256,1536]{1,0:T(8,128)(2,1)S(1)} %constant_dynamic-update-slice_fusion) | copy-start | bytes 2359300
  103.8 16.5 %copy-start.5 = (bf16[512,384]{1,0:T(8,128)(2,1)}, bf16[512,384]{1,0:T(8,128)(2,1)S(1)}, u32[]{:S(2)}) copy-start(bf16[512,384]{1,0:T(8,128)(2,1)S(1)} %collective-permute-done.8.refs_4_) | copy-start | bytes 1179652
  105.7 14.6 %copy-start.7 = (bf16[512,384]{1,0:T(8,128)(2,1)}, bf16[512,384]{1,0:T(8,128)(2,1)S(1)}, u32[]{:S(2)}) copy-start(bf16[512,384]{1,0:T(8,128)(2,1)S(1)} %collective-permute-done.7.refs_3_) | copy-start | bytes 1179652
  108.7 11.7 %copy-start.9 = (bf16[512,384]{1,0:T(8,128)(2,1)}, bf16[512,384]{1,0:T(8,128)(2,1)S(1)}, u32[]{:S(2)}) copy-start(bf16[512,384]{1,0:T(8,128)(2,1)S(1)} %collective-permute-done.15.refs_9_) | copy-start | bytes 1179652
  110.9 9.4 %copy-start.11 = (bf16[512,384]{1,0:T(8,128)(2,1)}, bf16[512,384]{1,0:T(8,128)(2,1)S(1)}, u32[]{:S(2)}) copy-start(bf16[512,384]{1,0:T(8,128)(2,1)S(1)} %collective-permute-done.14.refs_8_) | copy-start | bytes 1179652
  120.4 23.6 %copy-start.13 = (f32[256,384]{1,0:T(8,128)}, f32[256,384]{1,0:T(8,128)S(1)}, u32[]{:S(2)}) copy-start(f32[256,384]{1,0:T(8,128)S(1)} %get-tuple-element.5.exact_ref) | copy-start | bytes 1179652
  120.4 23.6 %copy-start.15 = (f32[256,384]{1,0:T(8,128)}, f32[256,384]{1,0:T(8,128)S(1)}, u32[]{:S(2)}) copy-start(f32[256,384]{1,0:T(8,128)S(1)} %get-tuple-element.6.level_ref) | copy-start | bytes 1179652
  178.5 2.3 %copy-start.2 = (bf16[256,384]{1,0:T(8,128)(2,1)S(1)}, bf16[256,384]{1,0:T(8,128)(2,1)}, u32[]{:S(2)}) copy-start(bf16[256,384]{1,0:T(8,128)(2,1)} %pad_maximum_fusion.3.query_ref) | copy-start | bytes 589828
  178.5 2.3 %copy-start.4 = (s32[256,1]{1,0:T(8,128)S(1)}, s32[256,1]{1,0:T(8,128)}, u32[]{:S(2)}) copy-start(s32[256,1]{1,0:T(8,128)} %copy.28.limit_ref) | copy-start | bytes 3076
  178.6 2.3 %copy-start.6 = (bf16[512,384]{1,0:T(8,128)(2,1)S(1)}, bf16[512,384]{1,0:T(8,128)(2,1)}, u32[]{:S(2)}) copy-start(bf16[512,384]{1,0:T(8,128)(2,1)} %copy-done.5) | copy-start | bytes 1179652
  178.6 2.3 %copy-start.8 = (bf16[512,384]{1,0:T(8,128)(2,1)S(1)}, bf16[512,384]{1,0:T(8,128)(2,1)}, u32[]{:S(2)}) copy-start(bf16[512,384]{1,0:T(8,128)(2,1)} %copy-done.7) | copy-start | bytes 1179652
  178.6 2.3 %copy-start.10 = (bf16[512,384]{1,0:T(8,128)(2,1)S(1)}, bf16[512,384]{1,0:T(8,128)(2,1)}, u32[]{:S(2)}) copy-start(bf16[512,384]{1,0:T(8,128)(2,1)} %copy-done.9) | copy-start | bytes 1179652
  178.6 2.3 %copy-start.12 = (bf16[512,384]{1,0:T(8,128)(2,1)S(1)}, bf16[512,384]{1,0:T(8,128)(2,1)}, u32[]{:S(2)}) copy-start(bf16[512,384]{1,0:T(8,128)(2,1)} %copy-done.11) | copy-start | bytes 1179652
  180.9 1.0 copy-start.14
  181.9 1.0 copy-start.16
  182.9 10.3 %copy-start.22 = (f32[24,96]{1,0:T(8,128)S(1)}, f32[24,96]{1,0:T(8,128)}, u32[]{:S(2)}) copy-start(f32[24,96]{1,0:T(8,128)} %reduce_sum.42) | copy-start | bytes 27652
  191.3 8.4 %collective-permute-start.16 = (bf16[128,384]{1,0:T(8,128)(2,1)S(1)}, bf16[128,384]{1,0:T(8,128)(2,1)S(1)}, u32[]{:S(2)}, u32[]{:S(2)}) collective-permute-start(bf16[128,384]{1,0:T(8,128)(2,1)S(1)} %get-tuple-element.11), channel_id=1, source_target_pairs={{0,16},{16,0},{32,48},{48,32},{64,80},{80,64},{96,112},{112,96},{1... | collective-permute-start | bytes 294920 | tf_op jit(solution)/shard_map/ppermute | solution.py:32
  193.2 6.5 %collective-permute-start.17 = (f32[24,96]{1,0:T(8,128)S(1)}, f32[24,96]{1,0:T(8,128)S(1)}, u32[]{:S(2)}, u32[]{:S(2)}) collective-permute-start(f32[24,96]{1,0:T(8,128)S(1)} %broadcast_multiply_fusion), channel_id=1, source_target_pairs={{0,0},{16,256},{32,16},{48,272},{64,32},{80,288},{96,48},{112,304}... | collective-permute-start | bytes 27656 | tf_op jit(solution)/shard_map/ppermute | solution.py:225
Sparse Core Ops, SparseCore 0:
  22.6 76.0 all-gather.1

commit v2 on v1

v2 whole, which is shorter than its diff:
```python
import functools

import jax
import jax.numpy as jnp
from jax import lax
from jax.experimental import pallas as pl
from jax.experimental.pallas import tpu as pltpu
from jax.sharding import PartitionSpec as P

HEAD_DIM = 128
SIDE = 4
CORES = 2
PAIR = 2
SLOTS = SIDE * PAIR
QUERY_SLOTS = 2
KEY_SLOTS = 4
LOG2_E = 1.4426950408889634
HIDDEN = -1e30
LOWEST = -1e20
MIB = 1024 * 1024
NT = (((1,), (1,)), ((), ()))
NN = (((1,), (0,)), ((), ()))
TN = (((0,), (0,)), ((), ()))


def seat(y, x, core):
    return (y % SIDE * SIDE + x % SIDE) * CORES + core % CORES


def send(value, dx=0, dcore=0):
    pairs = [
        (seat(y, x, core), seat(y, x + dx, core + dcore))
        for y in range(SIDE)
        for x in range(SIDE)
        for core in range(CORES)
    ]
    return lax.ppermute(value, "seq", pairs)


def trade(slots):
    groups = [
        [seat(y, PAIR * side + x, core) for y in range(SIDE) for x in range(PAIR)]
        for side in range(SIDE // PAIR)
        for core in range(CORES)
    ]
    return lax.all_to_all(slots, "seq", 0, 0, axis_index_groups=groups, tiled=True)


def tiles_of(refs):
    return [
        (ref.at[pl.ds(first, KEY_SLOTS), 0], ref.at[pl.ds(first, KEY_SLOTS), 1])
        for ref in refs
        for first in range(0, SLOTS, KEY_SLOTS)
    ]


def rows_of(ref):
    return ref[...].reshape(-1, HEAD_DIM)


def attend_blocks(scale, first_tile, limit_ref, place_ref, input_ref, tiles, start, finish):
    for block in range(SLOTS // QUERY_SLOTS):
        slots = pl.ds(block * QUERY_SLOTS, QUERY_SLOTS)
        query = rows_of(input_ref.at[slots, 0])
        limits = limit_ref[slots].reshape(-1, 1)
        peak, norm, total = start(slots, query.shape[0])
        for index, (key_ref, value_ref) in enumerate(tiles):
            scores = lax.dot_general(query, rows_of(key_ref), NT, preferred_element_type=jnp.float32)
            visible = place_ref[first_tile + index : first_tile + index + 1, :] < limits
            scores = jnp.where(visible, scores * (scale * LOG2_E), HIDDEN)
            new_peak = jnp.maximum(peak, jnp.max(scores, axis=1, keepdims=True))
            rescale = jnp.exp2(peak - new_peak)
            weights = jnp.exp2(scores - new_peak)
            norm = norm * rescale + jnp.sum(weights, axis=1, keepdims=True)
            total = total * rescale + lax.dot_general(
                weights.astype(jnp.bfloat16), rows_of(value_ref), NN, preferred_element_type=jnp.float32
            )
            peak = new_peak
        finish(slots, peak, norm, total)


def split_rows(rows):
    return rows.reshape(QUERY_SLOTS, -1, rows.shape[1])


def near_kernel(scale, limit_ref, place_ref, input_ref, own_ref, core_ref, peak_ref, norm_ref, total_ref):
    def start(slots, rows):
        return (
            jnp.full((rows, 1), LOWEST, jnp.float32),
            jnp.zeros((rows, 1), jnp.float32),
            jnp.zeros((rows, HEAD_DIM), jnp.float32),
        )

    def finish(slots, peak, norm, total):
        peak_ref[slots] = split_rows(peak)
        norm_ref[slots] = split_rows(norm)
        total_ref[slots] = split_rows(total)

    attend_blocks(scale, 0, limit_ref, place_ref, input_ref, tiles_of([own_ref, core_ref]), start, finish)


def far_kernel(
    scale, limit_ref, place_ref, input_ref, own_ref, core_ref, peak_ref, norm_ref, total_ref, attended_ref, exact_ref, level_ref
):
    def start(slots, rows):
        return (
            peak_ref[slots].reshape(rows, 1),
            norm_ref[slots].reshape(rows, 1),
            total_ref[slots].reshape(rows, HEAD_DIM),
        )

    def finish(slots, peak, norm, total):
        total = total / norm
        attended_ref[slots] = split_rows(total.astype(jnp.bfloat16))
        exact_ref[slots] = split_rows(total)
        level_ref[slots] = split_rows(peak + jnp.log2(norm))

    tiles = tiles_of([own_ref, core_ref])
    attend_blocks(scale, len(tiles), limit_ref, place_ref, input_ref, tiles, start, finish)


def grad_kernel(
    scale, limit_ref, place_ref, input_ref, grad_ref, exact_ref, level_ref, own_ref, core_ref, far_ref, far_core_ref, out_ref
):
    tiles = tiles_of([own_ref, core_ref, far_ref, far_core_ref])
    for block in range(SLOTS // QUERY_SLOTS):
        slots = pl.ds(block * QUERY_SLOTS, QUERY_SLOTS)
        query = rows_of(input_ref.at[slots, 0])
        limits = limit_ref[slots].reshape(-1, 1)
        level = level_ref[slots].reshape(-1, 1)
        grad = rows_of(grad_ref.at[slots])
        centre = jnp.sum(grad.astype(jnp.float32) * rows_of(exact_ref.at[slots]), axis=1, keepdims=True)
        total = jnp.zeros((query.shape[0], HEAD_DIM), jnp.float32)
        for index, (key_ref, value_ref) in enumerate(tiles):
            keys = rows_of(key_ref)
            scores = lax.dot_general(query, keys, NT, preferred_element_type=jnp.float32)
            visible = place_ref[index : index + 1, :] < limits
            probs = jnp.exp2(jnp.where(visible, scores * (scale * LOG2_E) - level, HIDDEN))
            grad_probs = lax.dot_general(grad, rows_of(value_ref), NT, preferred_element_type=jnp.float32)
            grad_scores = (probs * (grad_probs - centre)).astype(jnp.bfloat16)
            total = total + lax.dot_general(grad_scores, keys, NN, preferred_element_type=jnp.float32)
        out_ref[slots] = split_rows((total * scale).astype(jnp.bfloat16))


def project_kernel(head_count, rows_ref, weight_ref, out_ref):
    rows = rows_ref[...]
    for slot in range(SLOTS):
        head = slot % head_count
        out_ref[slot] = lax.dot_general(
            rows, weight_ref[pl.ds(head * HEAD_DIM, HEAD_DIM), :], NT, preferred_element_type=jnp.float32
        ).astype(jnp.bfloat16)


def outer_kernel(own_ref, other_ref, own_rows_ref, other_rows_ref, out_ref):
    own_rows = own_rows_ref[...]
    other_rows = other_rows_ref[...]
    for head in range(own_ref.shape[0]):
        term = lax.dot_general(own_ref[head], own_rows, TN, preferred_element_type=jnp.float32)
        term = term + lax.dot_general(other_ref[head], other_rows, TN, preferred_element_type=jnp.float32)
        out_ref[pl.ds(head * HEAD_DIM, HEAD_DIM), :] = term.astype(jnp.bfloat16)


def pack_kernel(head_count, query_ref, key_ref, value_ref, out_ref):
    for slot in range(SLOTS):
        columns = pl.ds(slot % head_count * HEAD_DIM, HEAD_DIM)
        for place, ref in enumerate((query_ref, key_ref, value_ref)):
            out_ref[slot, place] = ref[0, :, columns]


def join_kernel(head_count, slots_ref, out_ref):
    for head in range(head_count):
        out_ref[0, :, pl.ds(head * HEAD_DIM, HEAD_DIM)] = slots_ref[head]


def sum_kernel(pieces_ref, out_ref):
    total = pieces_ref[0].astype(jnp.float32)
    for chip in range(1, pieces_ref.shape[0]):
        total = total + pieces_ref[chip].astype(jnp.float32)
    total = total.astype(jnp.bfloat16)
    width = out_ref.shape[2]
    for clip in range(out_ref.shape[0]):
        out_ref[clip] = total[:, clip * width : (clip + 1) * width]


def call(kernel, out_shape, name, flops):
    def run(*operands):
        return pl.pallas_call(
            kernel,
            out_shape=[jax.ShapeDtypeStruct(shape, dtype) for shape, dtype in out_shape],
            in_specs=[pl.BlockSpec(memory_space=pltpu.VMEM)] * len(operands),
            out_specs=[pl.BlockSpec(memory_space=pltpu.VMEM)] * len(out_shape),
            compiler_params=pltpu.CompilerParams(vmem_limit_bytes=24 * MIB),
            cost_estimate=pl.CostEstimate(flops=int(flops), bytes_accessed=int(1e6), transcendentals=0),
            name=name,
        )(*operands)

    return run


def pack_rows(teacher_rows, counts, me):
    row_count = teacher_rows.shape[0]
    capacity = 2 * row_count // counts.shape[0]
    mine = lax.dynamic_index_in_dim(counts, me, 0, keepdims=False)
    starts = jnp.cumsum(mine) - mine
    slot = jnp.arange(capacity, dtype=jnp.int32)
    source_row = jnp.minimum(starts[:, None] + slot[None, :], row_count - 1)
    return teacher_rows[source_row]


def unpack_rows(arrived, counts, me, row_count):
    peer_count, capacity, feature_count = arrived.shape
    inbound = lax.dynamic_index_in_dim(counts, me, 1, keepdims=False)
    inbound_ends = jnp.cumsum(inbound)
    local_rows = jnp.arange(row_count, dtype=jnp.int32)
    earlier = inbound_ends[None, :] <= local_rows[:, None]
    sender = jnp.sum(earlier.astype(jnp.int32), axis=1)
    offset_in = local_rows - jnp.sum(jnp.where(earlier, inbound[None, :], 0), axis=1)
    return arrived.reshape(peer_count * capacity, feature_count)[sender * capacity + offset_in]


def shards(student_query, key_cache, value_cache, grad_rows, out_weight, return_counts, block_sizes):
    counts = return_counts[0]
    me = lax.axis_index("seq")
    core = me % CORES
    side = me // CORES % SIDE // PAIR
    row_count, head_width = student_query.shape[1:]
    head_count = head_width // HEAD_DIM
    scale = HEAD_DIM ** -0.5
    peer_count = lax.axis_size("seq")
    clip_count = lax.axis_size("dp")
    local_rows = jnp.arange(row_count, dtype=jnp.int32)

    weight = lax.all_gather(out_weight, "dp", axis=0, tiled=True)

    (slots,) = call(
        functools.partial(pack_kernel, head_count),
        [((SLOTS, 3, row_count, HEAD_DIM), jnp.bfloat16)],
        "pack",
        1e6,
    )(student_query, key_cache, value_cache)
    inputs = trade(slots)
    own = inputs[:, 1:]
    far = send(own, dx=PAIR)
    beside = send(own, dcore=1)
    far_beside = send(far, dcore=1)

    packed, beside = lax.optimization_barrier((pack_rows(grad_rows[0], counts, me), beside))
    arrived = lax.all_to_all(packed, "seq", 0, 0, tiled=True)
    ordered = unpack_rows(arrived, counts, me, row_count)
    other_ordered = send(ordered, dcore=1)

    rank = jnp.arange(SLOTS, dtype=jnp.int32)

    def bases(which_side, which_core):
        return (((rank // PAIR) * SIDE + which_side * PAIR + rank % PAIR) * CORES + which_core) * row_count

    key_bases = jnp.concatenate(
        [bases(side, core), bases(side, 1 - core), bases(1 - side, core), bases(1 - side, 1 - core)]
    )
    places = (key_bases[:, None] + local_rows[None, :]).reshape(-1, KEY_SLOTS * row_count)
    positions = bases(side, core)[:, None] + local_rows[None, :]
    block_ends = jnp.cumsum(block_sizes[0])
    limits = jnp.min(
        jnp.where(block_ends > positions[:, :, None], block_ends, row_count * peer_count), axis=2
    )[:, :, None]

    column = ((SLOTS, row_count, 1), jnp.float32)
    wide = ((SLOTS, row_count, HEAD_DIM), jnp.float32)
    narrow = ((SLOTS, row_count, HEAD_DIM), jnp.bfloat16)
    carry = call(functools.partial(near_kernel, scale), [column, column, wide], "near", 4e9)(
        limits, places, inputs, own, beside
    )
    attended, exact, level = call(functools.partial(far_kernel, scale), [narrow, wide, column], "far", 4e9)(
        limits, places, inputs, far, far_beside, *carry
    )

    returned = trade(attended)
    share_heads = head_count // CORES
    own_part = lax.dynamic_slice_in_dim(returned, core * share_heads, share_heads, axis=0)
    other_part = send(
        lax.dynamic_slice_in_dim(returned, (1 - core) * share_heads, share_heads, axis=0), dcore=1
    )
    feature_count = ordered.shape[1]
    width = share_heads * HEAD_DIM
    (partial_sum,) = call(outer_kernel, [((width, feature_count), jnp.bfloat16)], "outer", 5e8)(
        own_part, other_part, ordered, other_ordered
    )
    chip_count = SIDE * SIDE
    share = width // chip_count
    cores_apart = [[chip * CORES + which for chip in range(chip_count)] for which in range(CORES)]
    pieces = lax.all_to_all(
        partial_sum.reshape(chip_count, share, feature_count), "seq", 0, 0, axis_index_groups=cores_apart, tiled=True
    )

    pieces, late_ordered = lax.optimization_barrier((pieces, ordered))
    (head_grad,) = call(functools.partial(project_kernel, head_count), [narrow], "project", 1e9)(late_ordered, weight)
    (clip_parts,) = call(
        sum_kernel, [((clip_count, share, feature_count // clip_count), jnp.bfloat16)], "sum", 1e6
    )(pieces)
    head_grad, clip_parts = lax.optimization_barrier((trade(head_grad), clip_parts))
    (grad_query,) = call(functools.partial(grad_kernel, scale), [narrow], "attend_grad", 1e10)(
        limits, places, inputs, head_grad, exact, level, own, beside, far, far_beside
    )
    grad_query = trade(grad_query)
    (grad_query_rows,) = call(
        functools.partial(join_kernel, head_count), [((1, row_count, head_width), jnp.bfloat16)], "join", 1e6
    )(grad_query)

    terms = lax.all_to_all(clip_parts, "dp", 0, 0, tiled=True)
    total = jnp.sum(terms.astype(jnp.float32), axis=0) / float(clip_count)
    total = lax.ppermute(
        total,
        "seq",
        [(chip * CORES + which, which * chip_count + chip) for chip in range(chip_count) for which in range(CORES)],
    )
    return (grad_query_rows, total)


def solution(mesh):
    in_specs = (
        P("dp", "seq", None),
        P("dp", "seq", None),
        P("dp", "seq", None),
        P("dp", "seq", None),
        P("dp", None),
        P("dp", None, None),
        P("dp", None),
    )
    out_specs = (P("dp", "seq", None), P("seq", "dp"))
    return jax.shard_map(shards, mesh=mesh, in_specs=in_specs, out_specs=out_specs, check_vma=False)
```

time: 211 us -> 179 us (0.85)
  the two profiles are of different devices: /device:TPU:6 before, /device:TPU:44 now
where the time goes in v2:
time: 179 us; the launch traced here: 178 us
  starting transfers between devices  58.2 us (33%)
  waiting for transfers between devices  33 us (18%)
  Pallas kernels  31 us (17%)
  blocking collectives  22 us (12%)
  local copies, waits for them, and re-layouts  18.3 us (10%)
  between operations  14.3 us (8%)
    pallas_call x8, Pallas kernels, run(): pl.pallas_call(kernel, out_shape=[jax.ShapeDtypeStruct(shape, dtype) for...  31 us
    all_to_all x1, blocking collectives, shards(): lax.all_to_all(partial_sum.reshape(chip_count, share, feature_count), 'se...  22 us
    all_to_all x4, starting transfers between devices, trade(): lax.all_to_all(slots, 'seq', 0, 0, axis_index_groups=groups, tiled=True)  21 us
    all_to_all x4, waiting for transfers between devices, trade(): lax.all_to_all(slots, 'seq', 0, 0, axis_index_groups=groups, tiled=True)  17.2 us
    all_to_all x1, starting transfers between devices, shards(): terms = lax.all_to_all(clip_parts, 'dp', 0, 0, tiled=True)  15.2 us
    unnamed x37, local copies, waits for them, and re-layouts  13 us
    ppermute x5, waiting for transfers between devices, send(): return lax.ppermute(value, 'seq', pairs)  11.7 us
    ppermute x5, starting transfers between devices, send(): return lax.ppermute(value, 'seq', pairs)  10.4 us
  transfers between devices with their start and end apart: 13, of which 7 were waited for; matrix products, arithmetic and copies ran while one was open for 4% of the time, Pallas kernels for 16%

profile of v2, /device:TPU:44, one launch (start us, length us, event | category | flops | bytes accessed | tf_op | source)
XLA Modules:
  0.0 177.9 jit_solution(11041250442514739718)
XLA Ops:
  7.2 1.0 copy-done.3
  8.2 0.9 copy-done.4
  9.1 0.9 copy-done.5
  10.0 1.0 pack.1
  11.0 5.7 %all-to-all-start = ((bf16[8,3,128,128]{3,2,1,0:T(8,128)(2,1)}), bf16[8,3,128,128]{3,2,1,0:T(8,128)(2,1)S(1)}, u32[]{:S(2)}, u32[]{:S(2)}) async-start(bf16[8,3,128,128]{3,2,1,0:T(8,128)(2,1)} %pack.1), calls=%async_computation | async-start | bytes 1572864 | tf_op jit(solution)/shard_map/all_to_all | solution.py:46
  16.7 0.7 all-gather.2.cloned.1.call-update
  18.0 0.2 dynamic-slice_reduce_fusion
  18.2 0.1 reduce.1
  18.6 9.0 %all-to-all-done.input_ref = bf16[8,3,128,128]{3,2,1,0:T(8,128)(2,1)S(1)} async-done(((bf16[8,3,128,128]{3,2,1,0:T(8,128)(2,1)}), bf16[8,3,128,128]{3,2,1,0:T(8,128)(2,1)S(1)}, u32[]{:S(2)}, u32[]{:S(2)}) %all-to-all-start) | async-done | bytes 786464 | tf_op jit(solution)/shard_map/all_to_all | solution.py:46
  27.6 2.7 %collective-permute-start = (bf16[8,2,128,128]{3,2,1,0:T(8,128)(2,1)S(1)}, bf16[8,2,128,128]{3,2,1,0:T(8,128)(2,1)S(1)}, u32[]{:S(2)}, u32[]{:S(2)}) collective-permute-start(bf16[8,2,128,128]{3,2,1,0:T(8,128)(2,1)S(1)} %slice.8.own_ref), channel_id=1, source_target_pairs={{0,64},{16,80},{32,96},{48,112},{64,0},{80,16},{96,32},{112,48},{1... | collective-permute-start | bytes 1572872 | tf_op jit(solution)/shard_map/ppermute | solution.py:37
  30.4 1.9 %collective-permute-start.2 = (bf16[8,2,128,128]{3,2,1,0:T(8,128)(2,1)S(1)}, bf16[8,2,128,128]{3,2,1,0:T(8,128)(2,1)S(1)}, u32[]{:S(2)}, u32[]{:S(2)}) collective-permute-start(bf16[8,2,128,128]{3,2,1,0:T(8,128)(2,1)S(1)} %slice.8.own_ref), channel_id=1, source_target_pairs={{0,16},{16,0},{32,48},{48,32},{64,80},{80,64},{96,112},{112,96},{1... | collective-permute-start | bytes 1572872 | tf_op jit(solution)/shard_map/ppermute | solution.py:37
  32.4 10.5 %collective-permute-done.own_ref.far_ref = bf16[8,2,128,128]{3,2,1,0:T(8,128)(2,1)S(1)} collective-permute-done((bf16[8,2,128,128]{3,2,1,0:T(8,128)(2,1)S(1)}, bf16[8,2,128,128]{3,2,1,0:T(8,128)(2,1)S(1)}, u32[]{:S(2)}, u32[]{:S(2)}) %collective-permute-start) | collective-permute-done | bytes 524320 | tf_op jit(solution)/shard_map/ppermute | solution.py:37
  42.9 1.9 %collective-permute-start.1 = (bf16[8,2,128,128]{3,2,1,0:T(8,128)(2,1)S(1)}, bf16[8,2,128,128]{3,2,1,0:T(8,128)(2,1)}, u32[]{:S(2)}, u32[]{:S(2)}) collective-permute-start(bf16[8,2,128,128]{3,2,1,0:T(8,128)(2,1)S(1)} %collective-permute-done.own_ref.far_ref), channel_id=1, source_target_pairs={{0,16},{16,0},{32,48},{48,32},{64,80},{80,64},{96,112},{112,96},{1... | collective-permute-start | bytes 1572872 | tf_op jit(solution)/shard_map/ppermute | solution.py:37
  44.8 0.2 reduce-window.24
  45.0 2.2 %gather_fusion = bf16[256,1536]{1,0:T(8,128)(2,1)} fusion(bf16[128,1536]{1,0:T(8,128)(2,1)S(1)} %bitcast.29, s32[1024]{0:T(1024)S(1)} %pad_clamp_fusion.1), kind=kCustom, calls=%fused_computation | custom fusion | bytes 1573888 | tf_op jit(solution)/shard_map/gather | solution.py:207
  47.1 8.3 %all-to-all-start.2 = ((bf16[32,8,1536]{2,1,0:T(8,128)(2,1)}), bf16[32,8,1536]{2,1,0:T(8,128)(2,1)}, u32[]{:S(2)}, u32[]{:S(2)}) async-start(bf16[32,8,1536]{2,1,0:T(8,128)(2,1)} %bitcast.8), calls=%async_computation.2 | async-start | bytes 1572864 | tf_op jit(solution)/shard_map/all_to_all | solution.py:248
  55.5 0.2 copy.20.limit_ref
  55.8 1.0 copy-done.10
  56.8 5.4 %near.1 = (f32[8,128,1]{2,1,0:T(8,128)S(1)}, f32[8,128,1]{2,1,0:T(8,128)S(1)}, f32[8,128,128]{2,1,0:T(8,128)S(1)}) custom-call(s32[8,128,1]{2,1,0:T(8,128)S(1)} %copy.20.limit_ref, s32[8,512]{1,0:T(8,128)S(1)} %bitcast_add_fusion.place_ref, bf16[8,3,128,128]{3,2,1,0:T(8,128)(2,1)S(1)} %all-to-all-done.input_ref, bf16[8,2,128,128]{3,2,1,0:T(8,128)(2,1)S(1)} %slice.8.own_ref, ...), custom_call_target="tpu_custom_call" | custom-call | flops 4000000000 | bytes 1000000 | tf_op jit(solution)/shard_map/near/pallas_call | solution.py:187
  62.2 9.6 %far.1 = (bf16[8,128,128]{2,1,0:T(8,128)(2,1)}, f32[8,128,128]{2,1,0:T(8,128)S(1)}, f32[8,128,1]{2,1,0:T(8,128)S(1)}) custom-call(s32[8,128,1]{2,1,0:T(8,128)S(1)} %copy.20.limit_ref, s32[8,512]{1,0:T(8,128)S(1)} %bitcast_add_fusion.place_ref, bf16[8,3,128,128]{3,2,1,0:T(8,128)(2,1)S(1)} %all-to-all-done.input_ref, ...), custom_call_target="tpu_custom_call" | custom-call | flops 4000000000 | bytes 1000000 | tf_op jit(solution)/shard_map/far/pallas_call | solution.py:187
  71.8 0.8 copy-done.12
  72.6 0.8 copy-done.14
  73.4 5.4 %all-to-all-start.1 = ((bf16[8,128,128]{2,1,0:T(8,128)(2,1)}), bf16[8,128,128]{2,1,0:T(8,128)(2,1)S(1)}, u32[]{:S(2)}, u32[]{:S(2)}) async-start(bf16[8,128,128]{2,1,0:T(8,128)(2,1)} %get-tuple-element.18), calls=%async_computation.1 | async-start | bytes 524288 | tf_op jit(solution)/shard_map/all_to_all | solution.py:46
  78.9 2.5 %gather_fusion.1 = bf16[128,1536]{1,0:T(8,128)(2,1)S(1)} fusion(bf16[256,1536]{1,0:T(8,128)(2,1)} %bitcast.9, s32[1024]{0:T(1024)S(1)} %pad_clamp_fusion), kind=kCustom, calls=%fused_computation.1 | custom fusion | bytes 786944 | tf_op jit(solution)/shard_map/gather | solution.py:218
  81.4 1.9 %collective-permute-start.4 = (bf16[128,1536]{1,0:T(8,128)(2,1)S(1)}, bf16[128,1536]{1,0:T(8,128)(2,1)S(1)}, u32[]{:S(2)}, u32[]{:S(2)}) collective-permute-start(bf16[128,1536]{1,0:T(8,128)(2,1)S(1)} %gather_fusion.1), channel_id=1, source_target_pairs={{0,16},{16,0},{32,48},{48,32},{64,80},{80,64},{96,112},{112,96},{1... | collective-permute-start | bytes 1179656 | tf_op jit(solution)/shard_map/ppermute | solution.py:37
  83.3 1.5 all-to-all-done.1
  84.8 1.9 %collective-permute-start.3 = (bf16[3,128,128]{2,1,0:T(8,128)(2,1)S(1)}, bf16[3,128,128]{2,1,0:T(8,128)(2,1)S(1)}, u32[]{:S(2)}, u32[]{:S(2)}) collective-permute-start(bf16[3,128,128]{2,1,0:T(8,128)(2,1)S(1)} %get-tuple-element.28), channel_id=1, source_target_pairs={{0,16},{16,0},{32,48},{48,32},{64,80},{80,64},{96,112},{112,96},{1... | collective-permute-start | bytes 294920 | tf_op jit(solution)/shard_map/ppermute | solution.py:37
  86.7 1.3 collective-permute-done.3.other_ref
  88.0 0.8 outer.1
  88.8 22.0 %all_to_all.35.pieces_ref = bf16[16,24,1536]{2,1,0:T(8,128)(2,1)S(1)} all-to-all(bf16[16,24,1536]{2,1,0:T(8,128)(2,1)S(1)} %bitcast.30), channel_id=1, replica_groups={{0,32,64,96,128,160,192,224,256,288,320,352,384,416,448,480},{16,48,80,..., dimensions={0} | all-to-all | bytes 2359296 | tf_op jit(solution)/shard_map/all_to_all | solution.py:291
  110.8 1.7 copy-done.6
  112.5 1.7 project.1
  114.2 4.8 %all-to-all-start.4 = ((bf16[8,128,128]{2,1,0:T(8,128)(2,1)}), bf16[8,128,128]{2,1,0:T(8,128)(2,1)S(1)}, u32[]{:S(2)}, u32[]{:S(2)}) async-start(bf16[8,128,128]{2,1,0:T(8,128)(2,1)} %project.1), calls=%async_computation.4 | async-start | bytes 524288 | tf_op jit(solution)/shard_map/all_to_all | solution.py:46
  118.9 0.9 sum.1
  119.8 4.6 %all-to-all-done.4.grad_ref = bf16[8,128,128]{2,1,0:T(8,128)(2,1)S(1)} async-done(((bf16[8,128,128]{2,1,0:T(8,128)(2,1)}), bf16[8,128,128]{2,1,0:T(8,128)(2,1)S(1)}, u32[]{:S(2)}, u32[]{:S(2)}) %all-to-all-start.4) | async-done | bytes 262176 | tf_op jit(solution)/shard_map/all_to_all | solution.py:46
  124.5 15.2 %all-to-all-start.6 = ((bf16[16,24,96]{2,1,0:T(8,128)(2,1)}), bf16[16,24,96]{2,1,0:T(8,128)(2,1)S(1)}, u32[]{:S(2)}, u32[]{:S(2)}) async-start(bf16[16,24,96]{2,1,0:T(8,128)(2,1)} %sum.1), calls=%async_computation.6 | async-start | bytes 196608 | tf_op jit(solution)/shard_map/all_to_all | solution.py:309
  139.7 1.0 copy-done.2
  140.7 1.0 copy-done.8
  141.8 1.0 copy-done.11
  142.8 1.0 copy-done.13
  143.9 1.0 copy-done.15
  144.9 10.9 %attend_grad.1 = bf16[8,128,128]{2,1,0:T(8,128)(2,1)} custom-call(s32[8,128,1]{2,1,0:T(8,128)S(1)} %copy-done.2, s32[8,512]{1,0:T(8,128)S(1)} %bitcast_add_fusion.place_ref, bf16[8,3,128,128]{3,2,1,0:T(8,128)(2,1)S(1)} %all-to-all-done.input_ref, bf16[8,128,128]{2,1,0:T(8,128)(2,1)S(1)} %all-to-all-done.4.grad_ref, f32[8,128,128]{2,1,0:T(8,128)S(1)} %copy-done.13, ...), custom_call_target="tpu_custom_call" | custom-call | flops 10000000000 | bytes 1000000 | tf_op jit(solution)/shard_map/attend_grad/pallas_call | solution.py:187
  155.8 5.1 %all-to-all-start.5 = ((bf16[8,128,128]{2,1,0:T(8,128)(2,1)}), bf16[8,128,128]{2,1,0:T(8,128)(2,1)S(1)}, u32[]{:S(2)}, u32[]{:S(2)}) async-start(bf16[8,128,128]{2,1,0:T(8,128)(2,1)} %attend_grad.1), calls=%async_computation.5 | async-start | bytes 524288 | tf_op jit(solution)/shard_map/all_to_all | solution.py:46
  161.0 3.4 %collective-permute-start.5 = (f32[24,96]{1,0:T(8,128)S(1)}, f32[24,96]{1,0:T(8,128)S(1)}, u32[]{:S(2)}, u32[]{:S(2)}) collective-permute-start(f32[24,96]{1,0:T(8,128)S(1)} %broadcast_multiply_fusion), channel_id=1, source_target_pairs={{0,0},{16,256},{32,16},{48,272},{64,32},{80,288},{96,48},{112,304}... | collective-permute-start | bytes 27656 | tf_op jit(solution)/shard_map/ppermute | solution.py:311
  164.3 2.1 %all-to-all-done.5.slots_ref = bf16[8,128,128]{2,1,0:T(8,128)(2,1)S(1)} async-done(((bf16[8,128,128]{2,1,0:T(8,128)(2,1)}), bf16[8,128,128]{2,1,0:T(8,128)(2,1)S(1)}, u32[]{:S(2)}, u32[]{:S(2)}) %all-to-all-start.5) | async-done | bytes 262176 | tf_op jit(solution)/shard_map/all_to_all | solution.py:46
  166.5 0.7 join.1
  167.2 3.3 %collective-permute-done.5 = f32[24,96]{1,0:T(8,128)S(1)} collective-permute-done((f32[24,96]{1,0:T(8,128)S(1)}, f32[24,96]{1,0:T(8,128)S(1)}, u32[]{:S(2)}, u32[]{:S(2)}) %collective-permute-start.5) | collective-permute-done | bytes 9248 | tf_op jit(solution)/shard_map/ppermute | solution.py:311
  170.5 0.6 copy.22
  (55 shorter events, 1.1 us)
Async XLA Ops:
  7.2 37.8 %copy-start = (bf16[1,128,1536]{2,1,0:T(8,128)(2,1)S(1)}, bf16[1,128,1536]{2,1,0:T(8,128)(2,1)}, u32[]{:S(2)}) copy-start(bf16[1,128,1536]{2,1,0:T(8,128)(2,1)} %param.10) | copy-start | bytes 1179652
  7.2 1.0 copy-start.3
  8.2 0.9 copy-start.4
  9.1 0.9 copy-start.5
  11.0 6.5 %copy-start.16 = (s32[1,32,32]{2,1,0:T(8,128)S(1)}, s32[1,32,32]{2,1,0:T(8,128)}, u32[]{:S(2)}) copy-start(s32[1,32,32]{2,1,0:T(8,128)} %param.12) | copy-start | bytes 12292
  11.0 33.7 %copy-start.17 = (s32[1,5]{1,0:T(1,128)S(1)}, s32[1,5]{1,0:T(1,128)}, u32[]{:S(2)}) copy-start(s32[1,5]{1,0:T(1,128)} %param.13) | copy-start | bytes 64
  11.0 16.5 %all-to-all-start = ((bf16[8,3,128,128]{3,2,1,0:T(8,128)(2,1)}), bf16[8,3,128,128]{3,2,1,0:T(8,128)(2,1)S(1)}, u32[]{:S(2)}, u32[]{:S(2)}) async-start(bf16[8,3,128,128]{3,2,1,0:T(8,128)(2,1)} %pack.1), calls=%async_computation | async-start | bytes 1572864 | tf_op jit(solution)/shard_map/all_to_all | solution.py:46
  16.7 94.1 %all-gather.2.cloned.1.call-start = ((), (), s32[]{:S(2)}) async-start(), calls=%async_computation.7 | async-start | bytes 2506752 | tf_op jit(solution)/shard_map/all_gather | solution.py:233
  27.6 15.3 %collective-permute-start = (bf16[8,2,128,128]{3,2,1,0:T(8,128)(2,1)S(1)}, bf16[8,2,128,128]{3,2,1,0:T(8,128)(2,1)S(1)}, u32[]{:S(2)}, u32[]{:S(2)}) collective-permute-start(bf16[8,2,128,128]{3,2,1,0:T(8,128)(2,1)S(1)} %slice.8.own_ref), channel_id=1, source_target_pairs={{0,64},{16,80},{32,96},{48,112},{64,0},{80,16},{96,32},{112,48},{1... | collective-permute-start | bytes 1572872 | tf_op jit(solution)/shard_map/ppermute | solution.py:37
  30.4 16.8 %collective-permute-start.2 = (bf16[8,2,128,128]{3,2,1,0:T(8,128)(2,1)S(1)}, bf16[8,2,128,128]{3,2,1,0:T(8,128)(2,1)S(1)}, u32[]{:S(2)}, u32[]{:S(2)}) collective-permute-start(bf16[8,2,128,128]{3,2,1,0:T(8,128)(2,1)S(1)} %slice.8.own_ref), channel_id=1, source_target_pairs={{0,16},{16,0},{32,48},{48,32},{64,80},{80,64},{96,112},{112,96},{1... | collective-permute-start | bytes 1572872 | tf_op jit(solution)/shard_map/ppermute | solution.py:37
  42.9 19.3 %copy-start.7 = (bf16[8,2,128,128]{3,2,1,0:T(8,128)(2,1)}, bf16[8,2,128,128]{3,2,1,0:T(8,128)(2,1)S(1)}, u32[]{:S(2)}) copy-start(bf16[8,2,128,128]{3,2,1,0:T(8,128)(2,1)S(1)} %collective-permute-done.own_ref.far_ref) | copy-start | bytes 1572868
  42.9 19.3 %collective-permute-start.1 = (bf16[8,2,128,128]{3,2,1,0:T(8,128)(2,1)S(1)}, bf16[8,2,128,128]{3,2,1,0:T(8,128)(2,1)}, u32[]{:S(2)}, u32[]{:S(2)}) collective-permute-start(bf16[8,2,128,128]{3,2,1,0:T(8,128)(2,1)S(1)} %collective-permute-done.own_ref.far_ref), channel_id=1, source_target_pairs={{0,16},{16,0},{32,48},{48,32},{64,80},{80,64},{96,112},{112,96},{1... | collective-permute-start | bytes 1572872 | tf_op jit(solution)/shard_map/ppermute | solution.py:37
  47.1 8.4 %copy-start.9 = (bf16[8,2,128,128]{3,2,1,0:T(8,128)(2,1)}, bf16[8,2,128,128]{3,2,1,0:T(8,128)(2,1)S(1)}, u32[]{:S(2)}) copy-start(bf16[8,2,128,128]{3,2,1,0:T(8,128)(2,1)S(1)} %collective-permute-done.2.core_ref) | copy-start | bytes 1572868
  47.1 26.3 %all-to-all-start.2 = ((bf16[32,8,1536]{2,1,0:T(8,128)(2,1)}), bf16[32,8,1536]{2,1,0:T(8,128)(2,1)}, u32[]{:S(2)}, u32[]{:S(2)}) async-start(bf16[32,8,1536]{2,1,0:T(8,128)(2,1)} %bitcast.8), calls=%async_computation.2 | async-start | bytes 1572864 | tf_op jit(solution)/shard_map/all_to_all | solution.py:248
  55.7 1.0 copy-start.10
  56.8 5.4 %copy-start.1 = (s32[8,128,1]{2,1,0:T(8,128)}, s32[8,128,1]{2,1,0:T(8,128)S(1)}, u32[]{:S(2)}) copy-start(s32[8,128,1]{2,1,0:T(8,128)S(1)} %copy.20.limit_ref) | copy-start | bytes 12292
  71.8 0.8 copy-start.12
  72.6 0.8 copy-start.14
  73.4 11.4 %all-to-all-start.1 = ((bf16[8,128,128]{2,1,0:T(8,128)(2,1)}), bf16[8,128,128]{2,1,0:T(8,128)(2,1)S(1)}, u32[]{:S(2)}, u32[]{:S(2)}) async-start(bf16[8,128,128]{2,1,0:T(8,128)(2,1)} %get-tuple-element.18), calls=%async_computation.1 | async-start | bytes 524288 | tf_op jit(solution)/shard_map/all_to_all | solution.py:46
  81.4 6.6 %collective-permute-start.4 = (bf16[128,1536]{1,0:T(8,128)(2,1)S(1)}, bf16[128,1536]{1,0:T(8,128)(2,1)S(1)}, u32[]{:S(2)}, u32[]{:S(2)}) collective-permute-start(bf16[128,1536]{1,0:T(8,128)(2,1)S(1)} %gather_fusion.1), channel_id=1, source_target_pairs={{0,16},{16,0},{32,48},{48,32},{64,80},{80,64},{96,112},{112,96},{1... | collective-permute-start | bytes 1179656 | tf_op jit(solution)/shard_map/ppermute | solution.py:37
  84.8 3.2 %collective-permute-start.3 = (bf16[3,128,128]{2,1,0:T(8,128)(2,1)S(1)}, bf16[3,128,128]{2,1,0:T(8,128)(2,1)S(1)}, u32[]{:S(2)}, u32[]{:S(2)}) collective-permute-start(bf16[3,128,128]{2,1,0:T(8,128)(2,1)S(1)} %get-tuple-element.28), channel_id=1, source_target_pairs={{0,16},{16,0},{32,48},{48,32},{64,80},{80,64},{96,112},{112,96},{1... | collective-permute-start | bytes 294920 | tf_op jit(solution)/shard_map/ppermute | solution.py:37
  110.8 1.7 copy-start.6
  114.2 10.3 %all-to-all-start.4 = ((bf16[8,128,128]{2,1,0:T(8,128)(2,1)}), bf16[8,128,128]{2,1,0:T(8,128)(2,1)S(1)}, u32[]{:S(2)}, u32[]{:S(2)}) async-start(bf16[8,128,128]{2,1,0:T(8,128)(2,1)} %project.1), calls=%async_computation.4 | async-start | bytes 524288 | tf_op jit(solution)/shard_map/all_to_all | solution.py:46
  124.5 31.3 %all-to-all-start.6 = ((bf16[16,24,96]{2,1,0:T(8,128)(2,1)}), bf16[16,24,96]{2,1,0:T(8,128)(2,1)S(1)}, u32[]{:S(2)}, u32[]{:S(2)}) async-start(bf16[16,24,96]{2,1,0:T(8,128)(2,1)} %sum.1), calls=%async_computation.6 | async-start | bytes 196608 | tf_op jit(solution)/shard_map/all_to_all | solution.py:309
  139.7 1.0 copy-start.2
  140.7 1.0 copy-start.8
  141.8 1.0 copy-start.11
  142.8 1.0 copy-start.13
  143.9 1.0 copy-start.15
  155.8 10.6 %all-to-all-start.5 = ((bf16[8,128,128]{2,1,0:T(8,128)(2,1)}), bf16[8,128,128]{2,1,0:T(8,128)(2,1)S(1)}, u32[]{:S(2)}, u32[]{:S(2)}) async-start(bf16[8,128,128]{2,1,0:T(8,128)(2,1)} %attend_grad.1), calls=%async_computation.5 | async-start | bytes 524288 | tf_op jit(solution)/shard_map/all_to_all | solution.py:46
  161.0 9.5 %collective-permute-start.5 = (f32[24,96]{1,0:T(8,128)S(1)}, f32[24,96]{1,0:T(8,128)S(1)}, u32[]{:S(2)}, u32[]{:S(2)}) collective-permute-start(f32[24,96]{1,0:T(8,128)S(1)} %broadcast_multiply_fusion), channel_id=1, source_target_pairs={{0,0},{16,256},{32,16},{48,272},{64,32},{80,288},{96,48},{112,304}... | collective-permute-start | bytes 27656 | tf_op jit(solution)/shard_map/ppermute | solution.py:311
Sparse Core Ops, SparseCore 0:
  19.6 77.7 all-gather.1

commit v3 on v2

v3 whole, which is shorter than its diff:
```python
import functools

import jax
import jax.numpy as jnp
from jax import lax
from jax.experimental import pallas as pl
from jax.experimental.pallas import tpu as pltpu
from jax.sharding import PartitionSpec as P

HEAD_DIM = 128
SIDE = 4
CORES = 2
PAIR = 2
SLOTS = SIDE * PAIR
QUERY_SLOTS = 2
KEY_SLOTS = 4
LOG2_E = 1.4426950408889634
HIDDEN = -1e30
LOWEST = -1e20
MIB = 1024 * 1024
NT = (((1,), (1,)), ((), ()))
NN = (((1,), (0,)), ((), ()))
TN = (((0,), (0,)), ((), ()))


def seat(y, x, core):
    return (y % SIDE * SIDE + x % SIDE) * CORES + core % CORES


def send(value, dx=0, dcore=0, flip=0):
    pairs = [
        (seat(y, x, core), seat(y, (x + dx) ^ flip, core + dcore))
        for y in range(SIDE)
        for x in range(SIDE)
        for core in range(CORES)
    ]
    return lax.ppermute(value, "seq", pairs)


def trade(slots, across=False):
    groups = [
        [
            seat(y, PAIR * step + fixed if across else PAIR * fixed + step, core)
            for y in range(SIDE)
            for step in range(PAIR)
        ]
        for fixed in range(PAIR)
        for core in range(CORES)
    ]
    return lax.all_to_all(slots, "seq", 0, 0, axis_index_groups=groups, tiled=True)


def tiles_of(refs):
    return [
        (ref.at[pl.ds(first, KEY_SLOTS), 0], ref.at[pl.ds(first, KEY_SLOTS), 1])
        for ref in refs
        for first in range(0, SLOTS, KEY_SLOTS)
    ]


def rows_of(ref):
    return ref[...].reshape(-1, HEAD_DIM)


def masked_keys(key_ref, hidden_ref, tile):
    rows = KEY_SLOTS * key_ref.shape[1]
    return jnp.concatenate([rows_of(key_ref), hidden_ref[pl.ds(tile * rows, rows), :]], axis=1)


def attend_blocks(scale, input_ref, member_ref, hidden_ref, tiles, start, finish):
    for block in range(SLOTS // QUERY_SLOTS):
        slots = pl.ds(block * QUERY_SLOTS, QUERY_SLOTS)
        query = jnp.concatenate([rows_of(input_ref.at[slots, 0]), rows_of(member_ref.at[slots])], axis=1)
        peak, total = start(slots, query.shape[0])
        for index, (key_ref, value_ref) in enumerate(tiles):
            keys = masked_keys(key_ref, hidden_ref, index)
            values = rows_of(value_ref)
            values = jnp.concatenate([values, jnp.ones_like(values)], axis=1)
            scores = lax.dot_general(query, keys, NT, preferred_element_type=jnp.float32)
            new_peak = jnp.maximum(peak, jnp.max(scores, axis=1, keepdims=True))
            rescale = jnp.exp2((peak - new_peak) * (scale * LOG2_E))
            weights = jnp.exp2((scores - new_peak) * (scale * LOG2_E)).astype(jnp.bfloat16)
            total = total * rescale + lax.dot_general(weights, values, NN, preferred_element_type=jnp.float32)
            peak = new_peak
        finish(block, slots, peak, total)


def split_rows(rows):
    return rows.reshape(QUERY_SLOTS, -1, rows.shape[1])


def near_kernel(scale, input_ref, member_ref, hidden_ref, own_ref, core_ref, peak_ref, total_ref):
    def start(slots, rows):
        return jnp.full((rows, 1), LOWEST, jnp.float32), jnp.zeros((rows, 2 * HEAD_DIM), jnp.float32)

    def finish(block, slots, peak, total):
        peak_ref[slots] = split_rows(peak)
        total_ref[slots] = split_rows(total)

    attend_blocks(scale, input_ref, member_ref, hidden_ref, tiles_of([own_ref, core_ref]), start, finish)


def far_kernel(
    scale, input_ref, member_ref, hidden_ref, own_ref, core_ref, peak_ref, total_ref, attended_ref, exact_ref, level_ref
):
    def start(slots, rows):
        return peak_ref[slots].reshape(rows, 1), total_ref[slots].reshape(rows, 2 * HEAD_DIM)

    def finish(block, slots, peak, total):
        norm = total[:, HEAD_DIM:]
        exact = total[:, :HEAD_DIM] / norm
        attended = split_rows(exact.astype(jnp.bfloat16))
        for pair in range(PAIR):
            attended_ref[block * PAIR + pair] = attended
        exact_ref[slots] = split_rows(exact)
        level_ref[slots] = split_rows(peak * (scale * LOG2_E) + jnp.log2(norm))

    tiles = tiles_of([own_ref, core_ref])
    attend_blocks(scale, input_ref, member_ref, hidden_ref, tiles, start, finish)


def grad_kernel(
    scale, input_ref, member_ref, hidden_ref, grad_ref, exact_ref, level_ref, own_ref, core_ref, far_ref, far_core_ref, out_ref
):
    tiles = tiles_of([own_ref, core_ref, far_ref, far_core_ref])
    for block in range(SLOTS // QUERY_SLOTS):
        slots = pl.ds(block * QUERY_SLOTS, QUERY_SLOTS)
        query = jnp.concatenate([rows_of(input_ref.at[slots, 0]), rows_of(member_ref.at[slots])], axis=1)
        level = rows_of(level_ref.at[slots])
        level = jnp.concatenate([level] * KEY_SLOTS, axis=1)
        grad = rows_of(grad_ref.at[slots])
        centre = jnp.sum(grad.astype(jnp.float32) * rows_of(exact_ref.at[slots]), axis=1, keepdims=True)
        total = jnp.zeros((query.shape[0], HEAD_DIM), jnp.float32)
        for index, (key_ref, value_ref) in enumerate(tiles):
            keys = masked_keys(key_ref, hidden_ref, index)
            scores = lax.dot_general(query, keys, NT, preferred_element_type=jnp.float32)
            probs = jnp.exp2(scores * (scale * LOG2_E) - level)
            grad_probs = lax.dot_general(grad, rows_of(value_ref), NT, preferred_element_type=jnp.float32)
            grad_scores = (probs * (grad_probs - centre)).astype(jnp.bfloat16)
            total = total + lax.dot_general(grad_scores, rows_of(key_ref), NN, preferred_element_type=jnp.float32)
        out_ref[slots] = split_rows((total * scale).astype(jnp.bfloat16))


def project_kernel(head_count, rows_ref, weight_ref, out_ref):
    rows = rows_ref[...]
    for slot in range(SLOTS):
        head = slot % head_count
        out_ref[slot] = lax.dot_general(
            rows, weight_ref[pl.ds(head * HEAD_DIM, HEAD_DIM), :], NT, preferred_element_type=jnp.float32
        ).astype(jnp.bfloat16)


def outer_kernel(head_count, parity_ref, own_ref, other_ref, *refs):
    row_refs, out_ref = refs[:-1], refs[-1]
    parity = parity_ref[0]
    rows = jnp.concatenate([ref[...] for ref in row_refs], axis=0)
    for head in range(head_count):
        attended = jnp.concatenate(
            [own_ref[head, parity], own_ref[head, 1 - parity], other_ref[head, parity], other_ref[head, 1 - parity]],
            axis=0,
        )
        term = lax.dot_general(attended, rows, TN, preferred_element_type=jnp.float32)
        out_ref[pl.ds(head * HEAD_DIM, HEAD_DIM), :] = term.astype(jnp.bfloat16)


def pack_kernel(head_count, query_ref, key_ref, value_ref, out_ref, sems):
    copies = []
    for slot in range(SLOTS):
        columns = pl.ds(slot % head_count * HEAD_DIM, HEAD_DIM)
        for place, ref in enumerate((query_ref, key_ref, value_ref)):
            copies.append(
                pltpu.make_async_copy(ref.at[0, :, columns], out_ref.at[slot, place], sems.at[slot, place])
            )
    for copy in copies:
        copy.start()
    for copy in copies:
        copy.wait()


def join_kernel(head_count, slots_ref, out_ref):
    for head in range(head_count):
        out_ref[0, :, pl.ds(head * HEAD_DIM, HEAD_DIM)] = slots_ref[head]


def sum_kernel(pieces_ref, out_ref):
    total = pieces_ref[0].astype(jnp.float32)
    for chip in range(1, pieces_ref.shape[0]):
        total = total + pieces_ref[chip].astype(jnp.float32)
    share, width = out_ref.shape[1:]
    across = total.shape[1] // width
    for clip in range(out_ref.shape[0]):
        row, column = clip // across * share, clip % across * width
        out_ref[clip] = total[row : row + share, column : column + width].astype(jnp.bfloat16)


def block_at(shape, *place):
    return pl.BlockSpec(shape, lambda step: place)


def call(kernel, out_shape, name, flops, scalars=0, **options):
    def run(*operands):
        spaces = [pl.BlockSpec(memory_space=pltpu.SMEM)] * scalars
        spaces = spaces + [pl.BlockSpec()] * (len(operands) - scalars)
        for place, spec in options.get("blocks", {}).items():
            spaces[place] = spec
        return pl.pallas_call(
            kernel,
            out_shape=[jax.ShapeDtypeStruct(shape, dtype) for shape, dtype in out_shape],
            grid=(1,) if "blocks" in options else (),
            in_specs=options.get("in_specs", spaces),
            out_specs=[pl.BlockSpec()] * len(out_shape),
            scratch_shapes=options.get("scratch_shapes", ()),
            compiler_params=pltpu.CompilerParams(vmem_limit_bytes=options.get("limit", 20) * MIB),
            cost_estimate=pl.CostEstimate(flops=int(flops), bytes_accessed=int(1e6), transcendentals=0),
            name=name,
        )(*operands)

    return run


def pack_rows(teacher_rows, counts, me):
    row_count = teacher_rows.shape[0]
    capacity = 2 * row_count // counts.shape[0]
    mine = lax.dynamic_index_in_dim(counts, me, 0, keepdims=False)
    starts = jnp.cumsum(mine) - mine
    slot = jnp.arange(capacity, dtype=jnp.int32)
    source_row = jnp.minimum(starts[:, None] + slot[None, :], row_count - 1)
    return teacher_rows[source_row]


def unpack_rows(arrived, counts, me, row_count):
    peer_count, capacity, feature_count = arrived.shape
    inbound = lax.dynamic_index_in_dim(counts, me, 1, keepdims=False)
    inbound_ends = jnp.cumsum(inbound)
    local_rows = jnp.arange(row_count, dtype=jnp.int32)
    earlier = inbound_ends[None, :] <= local_rows[:, None]
    sender = jnp.sum(earlier.astype(jnp.int32), axis=1)
    offset_in = local_rows - jnp.sum(jnp.where(earlier, inbound[None, :], 0), axis=1)
    return arrived.reshape(peer_count * capacity, feature_count)[sender * capacity + offset_in]


def shards(student_query, key_cache, value_cache, grad_rows, out_weight, return_counts, block_sizes):
    counts = return_counts[0]
    me = lax.axis_index("seq")
    core = me % CORES
    side = me // CORES % SIDE // PAIR
    row_count, head_width = student_query.shape[1:]
    head_count = head_width // HEAD_DIM
    scale = HEAD_DIM ** -0.5
    peer_count = lax.axis_size("seq")
    clip_count = lax.axis_size("dp")
    local_rows = jnp.arange(row_count, dtype=jnp.int32)

    weight = lax.all_gather(out_weight, "dp", axis=0, tiled=True)

    (slots,) = call(
        functools.partial(pack_kernel, head_count),
        [((SLOTS, 3, row_count, HEAD_DIM), jnp.bfloat16)],
        "pack",
        1e6,
        limit=56,
        in_specs=[pl.BlockSpec(memory_space=pl.ANY)] * 3,
        scratch_shapes=[pltpu.SemaphoreType.DMA((SLOTS, 3))],
    )(student_query, key_cache, value_cache)
    inputs = trade(slots)
    own = inputs[:, 1:]
    far = send(own, dx=PAIR)
    beside = send(own, dcore=1)

    rank = jnp.arange(SLOTS, dtype=jnp.int32)

    def bases(which_side, which_core):
        return (((rank // PAIR) * SIDE + which_side * PAIR + rank % PAIR) * CORES + which_core) * row_count

    key_bases = jnp.concatenate(
        [bases(side, core), bases(side, 1 - core), bases(1 - side, core), bases(1 - side, 1 - core)]
    )
    block_ends = jnp.cumsum(block_sizes[0])
    block_starts = block_ends - block_sizes[0]
    pad = HEAD_DIM - block_ends.shape[0]
    ends = jnp.pad(block_ends, (0, pad), constant_values=row_count * peer_count)
    starts = jnp.pad(block_starts, (0, pad), constant_values=row_count * peer_count)
    places = (key_bases[:, None] + local_rows[None, :]).reshape(-1, 1)
    hidden = jnp.where(places < ends[None, :], 0.0, HIDDEN).astype(jnp.bfloat16)
    positions = (bases(side, core)[:, None] + local_rows[None, :])[:, :, None]
    member = ((positions >= starts) & (positions < ends)).astype(jnp.bfloat16)

    column = ((SLOTS, row_count, 1), jnp.float32)
    double = ((SLOTS, row_count, 2 * HEAD_DIM), jnp.float32)
    wide = ((SLOTS, row_count, HEAD_DIM), jnp.float32)
    narrow = ((SLOTS, row_count, HEAD_DIM), jnp.bfloat16)
    pair_narrow = ((SLOTS, PAIR, row_count, HEAD_DIM), jnp.bfloat16)
    only_query = block_at((SLOTS, 1, row_count, HEAD_DIM), 0, 0, 0, 0)
    half_keys = (hidden.shape[0] // 2, HEAD_DIM)
    carry = call(
        functools.partial(near_kernel, scale),
        [column, double],
        "near",
        4e9,
        limit=56,
        blocks={0: only_query, 2: block_at(half_keys, 0, 0)},
    )(
        inputs, member, hidden, own, beside
    )
    packed, far, carry = lax.optimization_barrier((pack_rows(grad_rows[0], counts, me), far, carry))
    far_beside = send(far, dcore=1)
    arrived = lax.all_to_all(packed, "seq", 0, 0, tiled=True)
    attended, exact, level = call(
        functools.partial(far_kernel, scale),
        [pair_narrow, wide, wide],
        "far",
        4e9,
        limit=56,
        blocks={0: only_query, 2: block_at(half_keys, 1, 0)},
    )(
        inputs, member, hidden, far, far_beside, *carry
    )

    attended, arrived = lax.optimization_barrier((attended, arrived))
    ordered = unpack_rows(arrived, counts, me, row_count)
    parity = me // CORES % PAIR
    feature_count = ordered.shape[1]
    quarter = feature_count // (PAIR * CORES)

    def columns_for(which_parity, which_core):
        return lax.dynamic_slice(
            ordered, (0, (which_parity * CORES + which_core) * quarter), (row_count, quarter)
        )

    row_parts = (
        columns_for(parity, core),
        send(columns_for(1 - parity, core), flip=1),
        send(columns_for(parity, 1 - core), dcore=1),
        send(columns_for(1 - parity, 1 - core), flip=1, dcore=1),
    )
    returned = trade(attended)
    (partial_sum,) = call(
        functools.partial(outer_kernel, head_count), [((head_width, quarter), jnp.bfloat16)], "outer", 5e8, scalars=1
    )(parity.reshape(1), returned, send(returned[:head_count], dcore=1), *row_parts)
    pieces = trade(partial_sum.reshape(SLOTS, head_width // SLOTS, quarter), across=True)

    pieces, late_ordered = lax.optimization_barrier((pieces, ordered))
    (head_grad,) = call(functools.partial(project_kernel, head_count), [narrow], "project", 1e9, limit=56)(late_ordered, weight)
    (clip_parts,) = call(
        sum_kernel, [((clip_count, head_width // peer_count, feature_count // clip_count), jnp.bfloat16)], "sum", 1e6
    )(pieces)
    head_grad, clip_parts = lax.optimization_barrier((trade(head_grad), clip_parts))
    (grad_query,) = call(functools.partial(grad_kernel, scale), [narrow], "attend_grad", 1e10, limit=56, blocks={0: only_query})(
        inputs, member, hidden, head_grad, exact, level, own, beside, far, far_beside
    )
    grad_query = trade(grad_query)
    (grad_query_rows,) = call(
        functools.partial(join_kernel, head_count), [((1, row_count, head_width), jnp.bfloat16)], "join", 1e6
    )(grad_query)

    terms = lax.all_to_all(clip_parts, "dp", 0, 0, tiled=True)
    total = jnp.sum(terms.astype(jnp.float32), axis=0) / float(clip_count)
    across = quarter * clip_count // feature_count
    total = lax.ppermute(
        total,
        ("seq", "dp"),
        [
            (
                seat(y, PAIR * half + x, at) * clip_count + clip,
                seat(y, PAIR * half + clip // across // CORES, clip // across % CORES) * clip_count
                + (x * CORES + at) * across
                + clip % across,
            )
            for y in range(SIDE)
            for half in range(PAIR)
            for x in range(PAIR)
            for at in range(CORES)
            for clip in range(clip_count)
        ],
    )
    return (grad_query_rows, total)


def solution(mesh):
    in_specs = (
        P("dp", "seq", None),
        P("dp", "seq", None),
        P("dp", "seq", None),
        P("dp", "seq", None),
        P("dp", None),
        P("dp", None, None),
        P("dp", None),
    )
    out_specs = (P("dp", "seq", None), P("seq", "dp"))
    return jax.shard_map(shards, mesh=mesh, in_specs=in_specs, out_specs=out_specs, check_vma=False)
```

time: 179 us -> 186 us (1.039)
  the two profiles are of different devices: /device:TPU:44 before, /device:TPU:6 now
where the time goes in v3:
time: 186 us; the launch traced here: 183 us
  starting transfers between devices  68.8 us (37%)
  waiting for transfers between devices  40.9 us (22%)
  Pallas kernels  32.9 us (18%)
  blocking collectives  15.5 us (8%)
  between operations  14.4 us (8%)
  local copies, waits for them, and re-layouts  5.82 us (3%)
  other arithmetic  4.62 us (2%)
    pallas_call x8, Pallas kernels, run(): pl.pallas_call(kernel, out_shape=[jax.ShapeDtypeStruct(shape, dtype) for...  32.9 us
    all_to_all x4, waiting for transfers between devices, trade(): lax.all_to_all(slots, 'seq', 0, 0, axis_index_groups=groups, tiled=True)  21.8 us
    all_to_all x4, starting transfers between devices, trade(): lax.all_to_all(slots, 'seq', 0, 0, axis_index_groups=groups, tiled=True)  19.1 us
    ppermute x7, starting transfers between devices, send(): return lax.ppermute(value, 'seq', pairs)  17.8 us
    all_to_all x1, blocking collectives, trade(): lax.all_to_all(slots, 'seq', 0, 0, axis_index_groups=groups, tiled=True)  15.5 us
    all_to_all x1, starting transfers between devices, shards(): terms = lax.all_to_all(clip_parts, 'dp', 0, 0, tiled=True)  15.2 us
    ppermute x1, starting transfers between devices, shards(): lax.ppermute(total, ('seq', 'dp'), [(seat(y, PAIR * half + x, at) * clip_...  11 us
    ppermute x7, waiting for transfers between devices, send(): return lax.ppermute(value, 'seq', pairs)  10.5 us
  transfers between devices with their start and end apart: 15, of which 8 were waited for; matrix products, arithmetic and copies ran while one was open for 4% of the time, Pallas kernels for 15%

profile of v3, /device:TPU:6, one launch (start us, length us, event | category | flops | bytes accessed | tf_op | source)
XLA Modules:
  0.0 182.9 jit_solution(16383418837075372353)
XLA Ops:
  7.2 2.3 %pack.1 = bf16[8,3,128,128]{3,2,1,0:T(8,128)(2,1)} custom-call(bf16[1,128,768]{2,1,0:T(8,128)(2,1)} %query_ref.1, bf16[1,128,768]{2,1,0:T(8,128)(2,1)} %key_ref.1, bf16[1,128,768]{2,1,0:T(8,128)(2,1)} %value_ref.1), custom_call_target="tpu_custom_call" | custom-call | flops 1000000 | bytes 1000000 | tf_op jit(solution)/shard_map/pack/pallas_call | solution.py:206
  9.5 5.9 %all-to-all-start = ((bf16[8,3,128,128]{3,2,1,0:T(8,128)(2,1)}), bf16[8,3,128,128]{3,2,1,0:T(8,128)(2,1)S(1)}, u32[]{:S(2)}, u32[]{:S(2)}) async-start(bf16[8,3,128,128]{3,2,1,0:T(8,128)(2,1)} %pack.1), calls=%async_computation | async-start | bytes 1572864 | tf_op jit(solution)/shard_map/all_to_all | solution.py:50
  15.4 0.7 all-gather.2.cloned.1.call-update
  16.2 0.1 pad_add_fusion
  16.4 0.2 reduce-window.25
  16.6 0.1 copy.13
  16.7 0.1 reduce
  16.8 0.1 compare_select_fusion
  16.9 0.1 reshape.253
  17.0 2.7 %select_convert_fusion.hidden_ref = bf16[4096,128]{1,0:T(8,128)(2,1)} fusion(s32[128]{0:T(128)S(1)} %pad.8, s32[4096]{0:T(1024)S(1)} %add_bitcast_fusion), kind=kLoop, calls=%fused_computation.2 | loop fusion | flops 1572864 | bytes 1065472 | tf_op jit(solution)/shard_map/convert_element_type | solution.py:284
  19.7 7.4 %all-to-all-done.input_ref = bf16[8,3,128,128]{3,2,1,0:T(8,128)(2,1)S(1)} async-done(((bf16[8,3,128,128]{3,2,1,0:T(8,128)(2,1)}), bf16[8,3,128,128]{3,2,1,0:T(8,128)(2,1)S(1)}, u32[]{:S(2)}, u32[]{:S(2)}) %all-to-all-start) | async-done | bytes 786464 | tf_op jit(solution)/shard_map/all_to_all | solution.py:50
  27.2 1.9 %collective-permute-start.1 = (bf16[8,2,128,128]{3,2,1,0:T(8,128)(2,1)S(1)}, bf16[8,2,128,128]{3,2,1,0:T(8,128)(2,1)S(1)}, u32[]{:S(2)}, u32[]{:S(2)}) collective-permute-start(bf16[8,2,128,128]{3,2,1,0:T(8,128)(2,1)S(1)} %slice.12.own_ref), channel_id=1, source_target_pairs={{0,16},{16,0},{32,48},{48,32},{64,80},{80,64},{96,112},{112,96},{1... | collective-permute-start | bytes 1572872 | tf_op jit(solution)/shard_map/ppermute | solution.py:37
  29.1 2.2 %gather_fusion = bf16[256,1536]{1,0:T(8,128)(2,1)} fusion(bf16[128,1536]{1,0:T(8,128)(2,1)S(1)} %bitcast.30, s32[1024]{0:T(1024)S(1)} %pad_clamp_fusion.1), kind=kCustom, calls=%fused_computation | custom fusion | bytes 1573888 | tf_op jit(solution)/shard_map/gather | solution.py:228
  31.4 4.0 %collective-permute-start = (bf16[8,2,128,128]{3,2,1,0:T(8,128)(2,1)S(1)}, bf16[8,2,128,128]{3,2,1,0:T(8,128)(2,1)S(1)}, u32[]{:S(2)}, u32[]{:S(2)}) collective-permute-start(bf16[8,2,128,128]{3,2,1,0:T(8,128)(2,1)S(1)} %slice.12.own_ref), channel_id=1, source_target_pairs={{0,64},{16,80},{32,96},{48,112},{64,0},{80,16},{96,32},{112,48},{1... | collective-permute-start | bytes 1572872 | tf_op jit(solution)/shard_map/ppermute | solution.py:37
  35.4 0.9 and_convert_fusion.member_ref
  36.3 0.8 copy-done.6
  37.1 5.3 %near.1 = (f32[8,128,1]{2,1,0:T(8,128)}, f32[8,128,256]{2,1,0:T(8,128)}) custom-call(bf16[8,3,128,128]{3,2,1,0:T(8,128)(2,1)} %copy-done.1, bf16[8,128,128]{2,1,0:T(8,128)(2,1)} %and_convert_fusion.member_ref, bf16[4096,128]{1,0:T(8,128)(2,1)} %select_convert_fusion.hidden_ref, bf16[8,2,128,128]{3,2,1,0:T(8,128)(2,1)} %copy-done.3, ...), custom_call_target="tpu_custom_call" | custom-call | flops 4000000000 | bytes 1000000 | tf_op jit(solution)/shard_map/near/pallas_call | solution.py:206
  42.4 6.7 %collective-permute-done.own_ref.far_ref = bf16[8,2,128,128]{3,2,1,0:T(8,128)(2,1)S(1)} collective-permute-done((bf16[8,2,128,128]{3,2,1,0:T(8,128)(2,1)S(1)}, bf16[8,2,128,128]{3,2,1,0:T(8,128)(2,1)S(1)}, u32[]{:S(2)}, u32[]{:S(2)}) %collective-permute-start) | collective-permute-done | bytes 524320 | tf_op jit(solution)/shard_map/ppermute | solution.py:37
  49.1 1.9 %collective-permute-start.2 = (bf16[8,2,128,128]{3,2,1,0:T(8,128)(2,1)S(1)}, bf16[8,2,128,128]{3,2,1,0:T(8,128)(2,1)S(1)}, u32[]{:S(2)}, u32[]{:S(2)}) collective-permute-start(bf16[8,2,128,128]{3,2,1,0:T(8,128)(2,1)S(1)} %collective-permute-done.own_ref.far_ref), channel_id=1, source_target_pairs={{0,16},{16,0},{32,48},{48,32},{64,80},{80,64},{96,112},{112,96},{1... | collective-permute-start | bytes 1572872 | tf_op jit(solution)/shard_map/ppermute | solution.py:37
  51.0 5.7 %all-to-all-start.1 = ((bf16[32,8,1536]{2,1,0:T(8,128)(2,1)}), bf16[32,8,1536]{2,1,0:T(8,128)(2,1)S(1)}, u32[]{:S(2)}, u32[]{:S(2)}) async-start(bf16[32,8,1536]{2,1,0:T(8,128)(2,1)} %bitcast.8), calls=%async_computation.1 | async-start | bytes 1572864 | tf_op jit(solution)/shard_map/all_to_all | solution.py:307
  56.8 0.8 copy-done.8
  57.6 7.7 %far.1 = (bf16[8,2,128,128]{3,2,1,0:T(8,128)(2,1)}, f32[8,128,128]{2,1,0:T(8,128)}, f32[8,128,128]{2,1,0:T(8,128)}) custom-call(bf16[8,3,128,128]{3,2,1,0:T(8,128)(2,1)} %copy-done.1, bf16[8,128,128]{2,1,0:T(8,128)(2,1)} %and_convert_fusion.member_ref, bf16[4096,128]{1,0:T(8,128)(2,1)} %select_convert_fusion.hidden_ref, bf16[8,2,128,128]{3,2,1,0:T(8,128)(2,1)} %copy-done.7, ...), custom_call_target="tpu_custom_call" | custom-call | flops 4000000000 | bytes 1000000 | tf_op jit(solution)/shard_map/far/pallas_call | solution.py:206
  65.2 3.5 %all-to-all-done.1 = bf16[32,8,1536]{2,1,0:T(8,128)(2,1)S(1)} async-done(((bf16[32,8,1536]{2,1,0:T(8,128)(2,1)}), bf16[32,8,1536]{2,1,0:T(8,128)(2,1)S(1)}, u32[]{:S(2)}, u32[]{:S(2)}) %all-to-all-start.1) | async-done | bytes 786464 | tf_op jit(solution)/shard_map/all_to_all | solution.py:307
  68.7 4.7 %all-to-all-start.2 = ((bf16[8,2,128,128]{3,2,1,0:T(8,128)(2,1)}), bf16[8,2,128,128]{3,2,1,0:T(8,128)(2,1)S(1)}, u32[]{:S(2)}, u32[]{:S(2)}) async-start(bf16[8,2,128,128]{3,2,1,0:T(8,128)(2,1)} %get-tuple-element.24), calls=%async_computation.2 | async-start | bytes 1048576 | tf_op jit(solution)/shard_map/all_to_all | solution.py:50
  73.5 0.2 dynamic-slice_reduce_fusion
  73.7 0.1 reduce.1
  73.8 0.1 convert_reduce_fusion.1
  73.9 9.0 %all-to-all-done.2.own_ref = bf16[8,2,128,128]{3,2,1,0:T(8,128)(2,1)S(1)} async-done(((bf16[8,2,128,128]{3,2,1,0:T(8,128)(2,1)}), bf16[8,2,128,128]{3,2,1,0:T(8,128)(2,1)S(1)}, u32[]{:S(2)}, u32[]{:S(2)}) %all-to-all-start.2) | async-done | bytes 524320 | tf_op jit(solution)/shard_map/all_to_all | solution.py:50
  83.0 1.9 %collective-permute-start.3 = (bf16[6,2,128,128]{3,2,1,0:T(8,128)(2,1)S(1)}, bf16[6,2,128,128]{3,2,1,0:T(8,128)(2,1)S(1)}, u32[]{:S(2)}, u32[]{:S(2)}) collective-permute-start(bf16[6,2,128,128]{3,2,1,0:T(8,128)(2,1)S(1)} %slice.13), channel_id=1, source_target_pairs={{0,16},{16,0},{32,48},{48,32},{64,80},{80,64},{96,112},{112,96},{1... | collective-permute-start | bytes 1179656 | tf_op jit(solution)/shard_map/ppermute | solution.py:37
  85.0 0.9 gather_fusion.1
  85.9 3.1 %collective-permute-start.4 = (bf16[128,384]{1,0:T(8,128)(2,1)S(1)}, bf16[128,384]{1,0:T(8,128)(2,1)S(1)}, u32[]{:S(2)}, u32[]{:S(2)}) collective-permute-start(bf16[128,384]{1,0:T(8,128)(2,1)S(1)} %get-tuple-element.36), channel_id=1, source_target_pairs={{0,32},{16,48},{32,0},{48,16},{64,96},{80,112},{96,64},{112,80},{1... | collective-permute-start | bytes 294920 | tf_op jit(solution)/shard_map/ppermute | solution.py:37
  89.0 2.1 %collective-permute-start.5 = (bf16[128,384]{1,0:T(8,128)(2,1)S(1)}, bf16[128,384]{1,0:T(8,128)(2,1)S(1)}, u32[]{:S(2)}, u32[]{:S(2)}) collective-permute-start(bf16[128,384]{1,0:T(8,128)(2,1)S(1)} %get-tuple-element.35), channel_id=1, source_target_pairs={{0,16},{16,0},{32,48},{48,32},{64,80},{80,64},{96,112},{112,96},{1... | collective-permute-start | bytes 294920 | tf_op jit(solution)/shard_map/ppermute | solution.py:37
  91.2 2.8 %collective-permute-start.6 = (bf16[128,384]{1,0:T(8,128)(2,1)S(1)}, bf16[128,384]{1,0:T(8,128)(2,1)S(1)}, u32[]{:S(2)}, u32[]{:S(2)}) collective-permute-start(bf16[128,384]{1,0:T(8,128)(2,1)S(1)} %get-tuple-element.34), channel_id=1, source_target_pairs={{0,48},{16,32},{32,16},{48,0},{64,112},{80,96},{96,80},{112,64},{1... | collective-permute-start | bytes 294920 | tf_op jit(solution)/shard_map/ppermute | solution.py:37
  94.0 3.7 %collective-permute-done.6.refs_3_ = bf16[128,384]{1,0:T(8,128)(2,1)S(1)} collective-permute-done((bf16[128,384]{1,0:T(8,128)(2,1)S(1)}, bf16[128,384]{1,0:T(8,128)(2,1)S(1)}, u32[]{:S(2)}, u32[]{:S(2)}) %collective-permute-start.6) | collective-permute-done | bytes 98336 | tf_op jit(solution)/shard_map/ppermute | solution.py:37
  97.8 0.6 outer.1
  98.4 15.5 %all_to_all.35.pieces_ref = bf16[8,96,384]{2,1,0:T(8,128)(2,1)S(1)} all-to-all(bf16[8,96,384]{2,1,0:T(8,128)(2,1)S(1)} %bitcast.31), channel_id=1, replica_groups={{0,64,128,192,256,320,384,448},{16,80,144,208,272,336,400,464},{32,96,1..., dimensions={0} | all-to-all | bytes 1179648 | tf_op jit(solution)/shard_map/all_to_all | solution.py:50
  113.8 3.5 %project.1 = bf16[8,128,128]{2,1,0:T(8,128)(2,1)} custom-call(bf16[128,1536]{1,0:T(8,128)(2,1)} %copy-done.2, bf16[768,1536]{1,0:T(8,128)(2,1)} %all-gather.2.cloned.1.call-done.weight_ref), custom_call_target="tpu_custom_call" | custom-call | flops 1000000000 | bytes 1000000 | tf_op jit(solution)/shard_map/project/pallas_call | solution.py:206
  117.3 3.9 %all-to-all-start.4 = ((bf16[8,128,128]{2,1,0:T(8,128)(2,1)}), bf16[8,128,128]{2,1,0:T(8,128)(2,1)S(1)}, u32[]{:S(2)}, u32[]{:S(2)}) async-start(bf16[8,128,128]{2,1,0:T(8,128)(2,1)} %project.1), calls=%async_computation.4 | async-start | bytes 524288 | tf_op jit(solution)/shard_map/all_to_all | solution.py:50
  121.2 0.8 sum.1
  122.0 5.3 %all-to-all-done.4.grad_ref = bf16[8,128,128]{2,1,0:T(8,128)(2,1)S(1)} async-done(((bf16[8,128,128]{2,1,0:T(8,128)(2,1)}), bf16[8,128,128]{2,1,0:T(8,128)(2,1)S(1)}, u32[]{:S(2)}, u32[]{:S(2)}) %all-to-all-start.4) | async-done | bytes 262176 | tf_op jit(solution)/shard_map/all_to_all | solution.py:50
  127.4 15.2 %all-to-all-start.6 = ((bf16[16,24,96]{2,1,0:T(8,128)(2,1)}), bf16[16,24,96]{2,1,0:T(8,128)(2,1)S(1)}, u32[]{:S(2)}, u32[]{:S(2)}) async-start(bf16[16,24,96]{2,1,0:T(8,128)(2,1)} %sum.1), calls=%async_computation.6 | async-start | bytes 196608 | tf_op jit(solution)/shard_map/all_to_all | solution.py:356
  142.6 12.1 %attend_grad.1 = bf16[8,128,128]{2,1,0:T(8,128)(2,1)} custom-call(bf16[8,3,128,128]{3,2,1,0:T(8,128)(2,1)} %copy-done.1, bf16[8,128,128]{2,1,0:T(8,128)(2,1)} %and_convert_fusion.member_ref, bf16[4096,128]{1,0:T(8,128)(2,1)} %select_convert_fusion.hidden_ref, bf16[8,128,128]{2,1,0:T(8,128)(2,1)} %copy-done.4, f32[8,128,128]{2,1,0:T(8,128)} %get-tuple-element.29.exact_ref, ...), custom_call_target="tpu_custom_call" | custom-call | flops 10000000000 | bytes 1000000 | tf_op jit(solution)/shard_map/attend_grad/pallas_call | solution.py:206
  154.7 1.0 all-to-all-done.6
  155.7 4.5 %all-to-all-start.5 = ((bf16[8,128,128]{2,1,0:T(8,128)(2,1)}), bf16[8,128,128]{2,1,0:T(8,128)(2,1)S(1)}, u32[]{:S(2)}, u32[]{:S(2)}) async-start(bf16[8,128,128]{2,1,0:T(8,128)(2,1)} %attend_grad.1), calls=%async_computation.5 | async-start | bytes 524288 | tf_op jit(solution)/shard_map/all_to_all | solution.py:50
  160.3 11.0 %collective-permute-start.7 = (f32[24,96]{1,0:T(8,128)S(1)}, f32[24,96]{1,0:T(8,128)S(1)}, u32[]{:S(2)}, u32[]{:S(2)}) collective-permute-start(f32[24,96]{1,0:T(8,128)S(1)} %broadcast_multiply_fusion), channel_id=1, source_target_pairs={{0,0},{1,1},{2,2},{3,3},{4,16},{5,17},{6,18},{7,19},{8,32},{9,33},... | collective-permute-start | bytes 27656 | tf_op jit(solution)/shard_map/ppermute | solution.py:359
  171.3 0.7 join.1
  172.0 3.5 %collective-permute-done.7 = f32[24,96]{1,0:T(8,128)S(1)} collective-permute-done((f32[24,96]{1,0:T(8,128)S(1)}, f32[24,96]{1,0:T(8,128)S(1)}, u32[]{:S(2)}, u32[]{:S(2)}) %collective-permute-start.7) | collective-permute-done | bytes 9248 | tf_op jit(solution)/shard_map/ppermute | solution.py:359
  175.5 0.6 copy.16
  (45 shorter events, 0.5 us)
Async XLA Ops:
  7.2 22.0 %copy-start = (bf16[1,128,1536]{2,1,0:T(8,128)(2,1)S(1)}, bf16[1,128,1536]{2,1,0:T(8,128)(2,1)}, u32[]{:S(2)}) copy-start(bf16[1,128,1536]{2,1,0:T(8,128)(2,1)} %param.10) | copy-start | bytes 1179652
  7.2 9.2 %copy-start.9 = (s32[1,5]{1,0:T(1,128)S(1)}, s32[1,5]{1,0:T(1,128)}, u32[]{:S(2)}) copy-start(s32[1,5]{1,0:T(1,128)} %param.13) | copy-start | bytes 64
  7.2 9.4 %copy-start.5 = (s32[1,32,32]{2,1,0:T(8,128)S(1)}, s32[1,32,32]{2,1,0:T(8,128)}, u32[]{:S(2)}) copy-start(s32[1,32,32]{2,1,0:T(8,128)} %param.12) | copy-start | bytes 12292
  9.5 17.7 %all-to-all-start = ((bf16[8,3,128,128]{3,2,1,0:T(8,128)(2,1)}), bf16[8,3,128,128]{3,2,1,0:T(8,128)(2,1)S(1)}, u32[]{:S(2)}, u32[]{:S(2)}) async-start(bf16[8,3,128,128]{3,2,1,0:T(8,128)(2,1)} %pack.1), calls=%async_computation | async-start | bytes 1572864 | tf_op jit(solution)/shard_map/all_to_all | solution.py:50
  15.4 98.4 %all-gather.2.cloned.1.call-start = ((), (), s32[]{:S(2)}) async-start(), calls=%async_computation.7 | async-start | bytes 2506752 | tf_op jit(solution)/shard_map/all_gather | solution.py:254
  27.1 4.2 %copy-start.1 = (bf16[8,3,128,128]{3,2,1,0:T(8,128)(2,1)}, bf16[8,3,128,128]{3,2,1,0:T(8,128)(2,1)S(1)}, u32[]{:S(2)}) copy-start(bf16[8,3,128,128]{3,2,1,0:T(8,128)(2,1)S(1)} %all-to-all-done.input_ref) | copy-start | bytes 2359300
  27.2 4.2 %copy-start.3 = (bf16[8,2,128,128]{3,2,1,0:T(8,128)(2,1)}, bf16[8,2,128,128]{3,2,1,0:T(8,128)(2,1)S(1)}, u32[]{:S(2)}) copy-start(bf16[8,2,128,128]{3,2,1,0:T(8,128)(2,1)S(1)} %slice.12.own_ref) | copy-start | bytes 1572868
  27.2 9.1 %collective-permute-start.1 = (bf16[8,2,128,128]{3,2,1,0:T(8,128)(2,1)S(1)}, bf16[8,2,128,128]{3,2,1,0:T(8,128)(2,1)S(1)}, u32[]{:S(2)}, u32[]{:S(2)}) collective-permute-start(bf16[8,2,128,128]{3,2,1,0:T(8,128)(2,1)S(1)} %slice.12.own_ref), channel_id=1, source_target_pairs={{0,16},{16,0},{32,48},{48,32},{64,80},{80,64},{96,112},{112,96},{1... | collective-permute-start | bytes 1572872 | tf_op jit(solution)/shard_map/ppermute | solution.py:37
  31.4 17.7 %collective-permute-start = (bf16[8,2,128,128]{3,2,1,0:T(8,128)(2,1)S(1)}, bf16[8,2,128,128]{3,2,1,0:T(8,128)(2,1)S(1)}, u32[]{:S(2)}, u32[]{:S(2)}) collective-permute-start(bf16[8,2,128,128]{3,2,1,0:T(8,128)(2,1)S(1)} %slice.12.own_ref), channel_id=1, source_target_pairs={{0,64},{16,80},{32,96},{48,112},{64,0},{80,16},{96,32},{112,48},{1... | collective-permute-start | bytes 1572872 | tf_op jit(solution)/shard_map/ppermute | solution.py:37
  36.3 0.8 copy-start.6
  49.1 7.6 %copy-start.7 = (bf16[8,2,128,128]{3,2,1,0:T(8,128)(2,1)}, bf16[8,2,128,128]{3,2,1,0:T(8,128)(2,1)S(1)}, u32[]{:S(2)}) copy-start(bf16[8,2,128,128]{3,2,1,0:T(8,128)(2,1)S(1)} %collective-permute-done.own_ref.far_ref) | copy-start | bytes 1572868
  49.1 7.6 %collective-permute-start.2 = (bf16[8,2,128,128]{3,2,1,0:T(8,128)(2,1)S(1)}, bf16[8,2,128,128]{3,2,1,0:T(8,128)(2,1)S(1)}, u32[]{:S(2)}, u32[]{:S(2)}) collective-permute-start(bf16[8,2,128,128]{3,2,1,0:T(8,128)(2,1)S(1)} %collective-permute-done.own_ref.far_ref), channel_id=1, source_target_pairs={{0,16},{16,0},{32,48},{48,32},{64,80},{80,64},{96,112},{112,96},{1... | collective-permute-start | bytes 1572872 | tf_op jit(solution)/shard_map/ppermute | solution.py:37
  51.0 17.7 %all-to-all-start.1 = ((bf16[32,8,1536]{2,1,0:T(8,128)(2,1)}), bf16[32,8,1536]{2,1,0:T(8,128)(2,1)S(1)}, u32[]{:S(2)}, u32[]{:S(2)}) async-start(bf16[32,8,1536]{2,1,0:T(8,128)(2,1)} %bitcast.8), calls=%async_computation.1 | async-start | bytes 1572864 | tf_op jit(solution)/shard_map/all_to_all | solution.py:307
  56.8 0.8 copy-start.8
  68.7 14.2 %all-to-all-start.2 = ((bf16[8,2,128,128]{3,2,1,0:T(8,128)(2,1)}), bf16[8,2,128,128]{3,2,1,0:T(8,128)(2,1)S(1)}, u32[]{:S(2)}, u32[]{:S(2)}) async-start(bf16[8,2,128,128]{3,2,1,0:T(8,128)(2,1)} %get-tuple-element.24), calls=%async_computation.2 | async-start | bytes 1048576 | tf_op jit(solution)/shard_map/all_to_all | solution.py:50
  83.0 14.8 %collective-permute-start.3 = (bf16[6,2,128,128]{3,2,1,0:T(8,128)(2,1)S(1)}, bf16[6,2,128,128]{3,2,1,0:T(8,128)(2,1)S(1)}, u32[]{:S(2)}, u32[]{:S(2)}) collective-permute-start(bf16[6,2,128,128]{3,2,1,0:T(8,128)(2,1)S(1)} %slice.13), channel_id=1, source_target_pairs={{0,16},{16,0},{32,48},{48,32},{64,80},{80,64},{96,112},{112,96},{1... | collective-permute-start | bytes 1179656 | tf_op jit(solution)/shard_map/ppermute | solution.py:37
  85.9 28.0 %copy-start.2 = (bf16[128,1536]{1,0:T(8,128)(2,1)}, bf16[128,1536]{1,0:T(8,128)(2,1)S(1)}, u32[]{:S(2)}) copy-start(bf16[128,1536]{1,0:T(8,128)(2,1)S(1)} %gather_fusion.1) | copy-start | bytes 1179652
  85.9 8.1 %collective-permute-start.4 = (bf16[128,384]{1,0:T(8,128)(2,1)S(1)}, bf16[128,384]{1,0:T(8,128)(2,1)S(1)}, u32[]{:S(2)}, u32[]{:S(2)}) collective-permute-start(bf16[128,384]{1,0:T(8,128)(2,1)S(1)} %get-tuple-element.36), channel_id=1, source_target_pairs={{0,32},{16,48},{32,0},{48,16},{64,96},{80,112},{96,64},{112,80},{1... | collective-permute-start | bytes 294920 | tf_op jit(solution)/shard_map/ppermute | solution.py:37
  89.0 5.0 %collective-permute-start.5 = (bf16[128,384]{1,0:T(8,128)(2,1)S(1)}, bf16[128,384]{1,0:T(8,128)(2,1)S(1)}, u32[]{:S(2)}, u32[]{:S(2)}) collective-permute-start(bf16[128,384]{1,0:T(8,128)(2,1)S(1)} %get-tuple-element.35), channel_id=1, source_target_pairs={{0,16},{16,0},{32,48},{48,32},{64,80},{80,64},{96,112},{112,96},{1... | collective-permute-start | bytes 294920 | tf_op jit(solution)/shard_map/ppermute | solution.py:37
  91.2 6.6 %collective-permute-start.6 = (bf16[128,384]{1,0:T(8,128)(2,1)S(1)}, bf16[128,384]{1,0:T(8,128)(2,1)S(1)}, u32[]{:S(2)}, u32[]{:S(2)}) collective-permute-start(bf16[128,384]{1,0:T(8,128)(2,1)S(1)} %get-tuple-element.34), channel_id=1, source_target_pairs={{0,48},{16,32},{32,16},{48,0},{64,112},{80,96},{96,80},{112,64},{1... | collective-permute-start | bytes 294920 | tf_op jit(solution)/shard_map/ppermute | solution.py:37
  117.3 10.1 %all-to-all-start.4 = ((bf16[8,128,128]{2,1,0:T(8,128)(2,1)}), bf16[8,128,128]{2,1,0:T(8,128)(2,1)S(1)}, u32[]{:S(2)}, u32[]{:S(2)}) async-start(bf16[8,128,128]{2,1,0:T(8,128)(2,1)} %project.1), calls=%async_computation.4 | async-start | bytes 524288 | tf_op jit(solution)/shard_map/all_to_all | solution.py:50
  127.4 15.2 %copy-start.4 = (bf16[8,128,128]{2,1,0:T(8,128)(2,1)}, bf16[8,128,128]{2,1,0:T(8,128)(2,1)S(1)}, u32[]{:S(2)}) copy-start(bf16[8,128,128]{2,1,0:T(8,128)(2,1)S(1)} %all-to-all-done.4.grad_ref) | copy-start | bytes 786436
  127.4 28.3 %all-to-all-start.6 = ((bf16[16,24,96]{2,1,0:T(8,128)(2,1)}), bf16[16,24,96]{2,1,0:T(8,128)(2,1)S(1)}, u32[]{:S(2)}, u32[]{:S(2)}) async-start(bf16[16,24,96]{2,1,0:T(8,128)(2,1)} %sum.1), calls=%async_computation.6 | async-start | bytes 196608 | tf_op jit(solution)/shard_map/all_to_all | solution.py:356
  155.7 15.6 %all-to-all-start.5 = ((bf16[8,128,128]{2,1,0:T(8,128)(2,1)}), bf16[8,128,128]{2,1,0:T(8,128)(2,1)S(1)}, u32[]{:S(2)}, u32[]{:S(2)}) async-start(bf16[8,128,128]{2,1,0:T(8,128)(2,1)} %attend_grad.1), calls=%async_computation.5 | async-start | bytes 524288 | tf_op jit(solution)/shard_map/all_to_all | solution.py:50
  160.3 15.2 %collective-permute-start.7 = (f32[24,96]{1,0:T(8,128)S(1)}, f32[24,96]{1,0:T(8,128)S(1)}, u32[]{:S(2)}, u32[]{:S(2)}) collective-permute-start(f32[24,96]{1,0:T(8,128)S(1)} %broadcast_multiply_fusion), channel_id=1, source_target_pairs={{0,0},{1,1},{2,2},{3,3},{4,16},{5,17},{6,18},{7,19},{8,32},{9,33},... | collective-permute-start | bytes 27656 | tf_op jit(solution)/shard_map/ppermute | solution.py:359
Sparse Core Ops, SparseCore 0:
  18.3 77.9 all-gather.1

commit v4 on v3

--- a/solution.py
+++ b/solution.py
@@ -27,9 +27,9 @@
     return (y % SIDE * SIDE + x % SIDE) * CORES + core % CORES
 
 
-def send(value, dx=0, dcore=0, flip=0):
+def send(value, dx=0, dcore=0):
     pairs = [
-        (seat(y, x, core), seat(y, (x + dx) ^ flip, core + dcore))
+        (seat(y, x, core), seat(y, x + dx, core + dcore))
         for y in range(SIDE)
         for x in range(SIDE)
         for core in range(CORES)
@@ -37,17 +37,43 @@
     return lax.ppermute(value, "seq", pairs)
 
 
-def trade(slots, across=False):
+def trade(slots):
     groups = [
-        [
-            seat(y, PAIR * step + fixed if across else PAIR * fixed + step, core)
-            for y in range(SIDE)
-            for step in range(PAIR)
-        ]
-        for fixed in range(PAIR)
+        [seat(y, PAIR * side + x, core) for y in range(SIDE) for x in range(PAIR)]
+        for side in range(PAIR)
         for core in range(CORES)
     ]
     return lax.all_to_all(slots, "seq", 0, 0, axis_index_groups=groups, tiled=True)
+
+
+def holders():
+    return [
+        seat(head // PAIR, PAIR * side + head % PAIR, core)
+        for head in range(SLOTS - PAIR)
+        for side in range(PAIR)
+        for core in range(CORES)
+    ]
+
+
+def place_blocks(block, me):
+    held = holders()
+
+    def pass_on(routes):
+        return lax.ppermute(
+            block, "seq", [(held[3 * turn + take], 4 * turn + put) for turn in range(len(held) // 3) for take, put in routes]
+        )
+
+    unit = block.shape[0] // 4
+    first = pass_on([(0, 0), (1, 1), (2, 3)])
+    second = pass_on([(0, 1), (2, 2)])
+    third = pass_on([(1, 2)])
+    kinds = [
+        first[: 3 * unit],
+        jnp.concatenate([second[3 * unit :], first[: 2 * unit]]),
+        jnp.concatenate([third[2 * unit :], second[:unit]]),
+        first[unit:],
+    ]
+    return lax.select_n(me % 4, *kinds)
 
 
 def tiles_of(refs):
@@ -109,9 +135,7 @@
     def finish(block, slots, peak, total):
         norm = total[:, HEAD_DIM:]
         exact = total[:, :HEAD_DIM] / norm
-        attended = split_rows(exact.astype(jnp.bfloat16))
-        for pair in range(PAIR):
-            attended_ref[block * PAIR + pair] = attended
+        attended_ref[slots] = split_rows(exact.astype(jnp.bfloat16))
         exact_ref[slots] = split_rows(exact)
         level_ref[slots] = split_rows(peak * (scale * LOG2_E) + jnp.log2(norm))
 
@@ -141,26 +165,22 @@
         out_ref[slots] = split_rows((total * scale).astype(jnp.bfloat16))
 
 
-def project_kernel(head_count, rows_ref, weight_ref, out_ref):
-    rows = rows_ref[...]
+def project_kernel(rows_ref, weight_ref, out_ref):
+    weight = weight_ref[...]
     for slot in range(SLOTS):
-        head = slot % head_count
-        out_ref[slot] = lax.dot_general(
-            rows, weight_ref[pl.ds(head * HEAD_DIM, HEAD_DIM), :], NT, preferred_element_type=jnp.float32
-        ).astype(jnp.bfloat16)
-
-
-def outer_kernel(head_count, parity_ref, own_ref, other_ref, *refs):
-    row_refs, out_ref = refs[:-1], refs[-1]
-    parity = parity_ref[0]
-    rows = jnp.concatenate([ref[...] for ref in row_refs], axis=0)
-    for head in range(head_count):
-        attended = jnp.concatenate(
-            [own_ref[head, parity], own_ref[head, 1 - parity], other_ref[head, parity], other_ref[head, 1 - parity]],
-            axis=0,
+        out_ref[slot] = lax.dot_general(rows_ref[slot], weight, NT, preferred_element_type=jnp.float32).astype(
+            jnp.bfloat16
         )
-        term = lax.dot_general(attended, rows, TN, preferred_element_type=jnp.float32)
-        out_ref[pl.ds(head * HEAD_DIM, HEAD_DIM), :] = term.astype(jnp.bfloat16)
+
+
+def outer_kernel(attended_ref, rows_ref, out_ref):
+    parts, share, feature_count = out_ref.shape
+    attended = attended_ref[...].reshape(-1, HEAD_DIM)
+    for first in range(0, feature_count, 4 * HEAD_DIM):
+        columns = pl.ds(first, 4 * HEAD_DIM)
+        rows = rows_ref[:, :, columns].reshape(attended.shape[0], -1)
+        term = lax.dot_general(attended, rows, TN, preferred_element_type=jnp.float32).astype(jnp.bfloat16)
+        out_ref[:, :, columns] = term.reshape(parts, share, -1)
 
 
 def pack_kernel(head_count, query_ref, key_ref, value_ref, out_ref, sems):
@@ -184,13 +204,11 @@
 
 def sum_kernel(pieces_ref, out_ref):
     total = pieces_ref[0].astype(jnp.float32)
-    for chip in range(1, pieces_ref.shape[0]):
-        total = total + pieces_ref[chip].astype(jnp.float32)
-    share, width = out_ref.shape[1:]
-    across = total.shape[1] // width
+    for piece in range(1, pieces_ref.shape[0]):
+        total = total + pieces_ref[piece].astype(jnp.float32)
+    width = out_ref.shape[2]
     for clip in range(out_ref.shape[0]):
-        row, column = clip // across * share, clip % across * width
-        out_ref[clip] = total[row : row + share, column : column + width].astype(jnp.bfloat16)
+        out_ref[clip] = total[:, clip * width : (clip + 1) * width].astype(jnp.bfloat16)
 
 
 def block_at(shape, *place):
@@ -264,8 +282,11 @@
     )(student_query, key_cache, value_cache)
     inputs = trade(slots)
     own = inputs[:, 1:]
+    own, packed = lax.optimization_barrier((own, pack_rows(grad_rows[0], counts, me)))
     far = send(own, dx=PAIR)
     beside = send(own, dcore=1)
+    packed, beside = lax.optimization_barrier((packed, beside))
+    arrived = lax.all_to_all(packed, "seq", 0, 0, tiled=True)
 
     rank = jnp.arange(SLOTS, dtype=jnp.int32)
 
@@ -289,7 +310,6 @@
     double = ((SLOTS, row_count, 2 * HEAD_DIM), jnp.float32)
     wide = ((SLOTS, row_count, HEAD_DIM), jnp.float32)
     narrow = ((SLOTS, row_count, HEAD_DIM), jnp.bfloat16)
-    pair_narrow = ((SLOTS, PAIR, row_count, HEAD_DIM), jnp.bfloat16)
     only_query = block_at((SLOTS, 1, row_count, HEAD_DIM), 0, 0, 0, 0)
     half_keys = (hidden.shape[0] // 2, HEAD_DIM)
     carry = call(
@@ -302,12 +322,15 @@
     )(
         inputs, member, hidden, own, beside
     )
-    packed, far, carry = lax.optimization_barrier((pack_rows(grad_rows[0], counts, me), far, carry))
+    far, carry = lax.optimization_barrier((far, carry))
     far_beside = send(far, dcore=1)
-    arrived = lax.all_to_all(packed, "seq", 0, 0, tiled=True)
+    ordered = unpack_rows(arrived, counts, me, row_count)
+    copies = jnp.broadcast_to(ordered[None], (SLOTS,) + ordered.shape)
+    far_beside, copies = lax.optimization_barrier((far_beside, copies))
+    group_rows = trade(copies)
     attended, exact, level = call(
         functools.partial(far_kernel, scale),
-        [pair_narrow, wide, wide],
+        [narrow, wide, wide],
         "far",
         4e9,
         limit=56,
@@ -316,35 +339,22 @@
         inputs, member, hidden, far, far_beside, *carry
     )
 
-    attended, arrived = lax.optimization_barrier((attended, arrived))
-    ordered = unpack_rows(arrived, counts, me, row_count)
-    parity = me // CORES % PAIR
     feature_count = ordered.shape[1]
-    quarter = feature_count // (PAIR * CORES)
-
-    def columns_for(which_parity, which_core):
-        return lax.dynamic_slice(
-            ordered, (0, (which_parity * CORES + which_core) * quarter), (row_count, quarter)
-        )
-
-    row_parts = (
-        columns_for(parity, core),
-        send(columns_for(1 - parity, core), flip=1),
-        send(columns_for(parity, 1 - core), dcore=1),
-        send(columns_for(1 - parity, 1 - core), flip=1, dcore=1),
-    )
-    returned = trade(attended)
+    parts = PAIR * CORES
+    share = HEAD_DIM // parts
     (partial_sum,) = call(
-        functools.partial(outer_kernel, head_count), [((head_width, quarter), jnp.bfloat16)], "outer", 5e8, scalars=1
-    )(parity.reshape(1), returned, send(returned[:head_count], dcore=1), *row_parts)
-    pieces = trade(partial_sum.reshape(SLOTS, head_width // SLOTS, quarter), across=True)
-
-    pieces, late_ordered = lax.optimization_barrier((pieces, ordered))
-    (head_grad,) = call(functools.partial(project_kernel, head_count), [narrow], "project", 1e9, limit=56)(late_ordered, weight)
-    (clip_parts,) = call(
-        sum_kernel, [((clip_count, head_width // peer_count, feature_count // clip_count), jnp.bfloat16)], "sum", 1e6
-    )(pieces)
-    head_grad, clip_parts = lax.optimization_barrier((trade(head_grad), clip_parts))
+        outer_kernel, [((parts, share, feature_count), jnp.bfloat16)], "outer", 1e9
+    )(attended, group_rows)
+    partners = [
+        [seat(y, PAIR * side + x, at) for side in range(PAIR) for at in range(CORES)]
+        for y in range(SIDE)
+        for x in range(PAIR)
+    ]
+    pieces = lax.all_to_all(partial_sum, "seq", 0, 0, axis_index_groups=partners, tiled=True)
+
+    slot = me // (SIDE * CORES) * PAIR + me // CORES % PAIR
+    head_weight = lax.dynamic_slice_in_dim(weight, slot % head_count * HEAD_DIM, HEAD_DIM, axis=0)
+    (head_grad,) = call(project_kernel, [narrow], "project", 1e9)(group_rows, head_weight)
     (grad_query,) = call(functools.partial(grad_kernel, scale), [narrow], "attend_grad", 1e10, limit=56, blocks={0: only_query})(
         inputs, member, hidden, head_grad, exact, level, own, beside, far, far_beside
     )
@@ -353,26 +363,12 @@
         functools.partial(join_kernel, head_count), [((1, row_count, head_width), jnp.bfloat16)], "join", 1e6
     )(grad_query)
 
+    (clip_parts,) = call(
+        sum_kernel, [((clip_count, share, feature_count // clip_count), jnp.bfloat16)], "sum", 1e6
+    )(pieces)
     terms = lax.all_to_all(clip_parts, "dp", 0, 0, tiled=True)
     total = jnp.sum(terms.astype(jnp.float32), axis=0) / float(clip_count)
-    across = quarter * clip_count // feature_count
-    total = lax.ppermute(
-        total,
-        ("seq", "dp"),
-        [
-            (
-                seat(y, PAIR * half + x, at) * clip_count + clip,
-                seat(y, PAIR * half + clip // across // CORES, clip // across % CORES) * clip_count
-                + (x * CORES + at) * across
-                + clip % across,
-            )
-            for y in range(SIDE)
-            for half in range(PAIR)
-            for x in range(PAIR)
-            for at in range(CORES)
-            for clip in range(clip_count)
-        ],
-    )
+    total = place_blocks(total, me)
     return (grad_query_rows, total)
 
 

time: 186 us -> 177 us (0.952); the launches traced: 183 us -> 176 us
  waiting for transfers between devices: 40.9 us -> 59.7 us
  blocking collectives: 15.5 us -> 0 us
  starting transfers between devices: 68.8 us -> 57 us
  local copies, waits for them, and re-layouts: 5.82 us -> 8.79 us
    all_to_all x4 -> x3, waiting for transfers between devices: 21.8 us -> 39.6 us  [trade(): lax.all_to_all(slots, 'seq', 0, 0, axis_index_groups=groups, tiled=True)]
    all_to_all x1 -> x0, blocking collectives: 15.5 us -> none  [trade(): lax.all_to_all(slots, 'seq', 0, 0, axis_index_groups=groups, tiled=True)]
    ppermute x7 -> x3, starting transfers between devices: 17.8 us -> 7.79 us  [send(): return lax.ppermute(value, 'seq', pairs)]
    ppermute x7 -> x3, waiting for transfers between devices: 10.5 us -> 2.56 us  [send(): return lax.ppermute(value, 'seq', pairs)]
    all_to_all x0 -> x1, starting transfers between devices: none -> 5.87 us  [shards(): lax.all_to_all(partial_sum, 'seq', 0, 0, axis_index_groups=partners, tile...]
    all_to_all x4 -> x3, starting transfers between devices: 19.1 us -> 15.3 us  [trade(): lax.all_to_all(slots, 'seq', 0, 0, axis_index_groups=groups, tiled=True)]
    all_to_all x0 -> x1, waiting for transfers between devices: none -> 3.19 us  [shards(): lax.all_to_all(partial_sum, 'seq', 0, 0, axis_index_groups=partners, tile...]
    ppermute x1 -> x3, starting transfers between devices: 11 us -> 7.97 us  [pass_on(): lax.ppermute(block, 'seq', [(held[3 * turn + take], 4 * turn + put) for t...]
  transfers between devices with their start and end apart: 15 -> 13, of which waited for: 8 -> 9; matrix products, arithmetic and copies ran while one was open for 4% -> 6% of each run, Pallas kernels for 15% -> 15%
where the time goes in v4:
time: 177 us; the launch traced here: 176 us
  waiting for transfers between devices  59.7 us (34%)
  starting transfers between devices  57 us (32%)
  Pallas kernels  31.3 us (18%)
  between operations  14.4 us (8%)
  local copies, waits for them, and re-layouts  8.79 us (5%)
  other arithmetic  5.21 us (3%)
    all_to_all x3, waiting for transfers between devices, trade(): lax.all_to_all(slots, 'seq', 0, 0, axis_index_groups=groups, tiled=True)  39.6 us
    pallas_call x8, Pallas kernels, run(): pl.pallas_call(kernel, out_shape=[jax.ShapeDtypeStruct(shape, dtype) for...  31.3 us
    all_to_all x3, starting transfers between devices, trade(): lax.all_to_all(slots, 'seq', 0, 0, axis_index_groups=groups, tiled=True)  15.3 us
    all_to_all x1, starting transfers between devices, shards(): terms = lax.all_to_all(clip_parts, 'dp', 0, 0, tiled=True)  14.7 us
    ppermute x3, starting transfers between devices, pass_on(): lax.ppermute(block, 'seq', [(held[3 * turn + take], 4 * turn + put) for t...  7.97 us
    ppermute x3, starting transfers between devices, send(): return lax.ppermute(value, 'seq', pairs)  7.79 us
    all_to_all x1, starting transfers between devices, shards(): lax.all_to_all(partial_sum, 'seq', 0, 0, axis_index_groups=partners, tile...  5.87 us
    ppermute x3, waiting for transfers between devices, pass_on(): lax.ppermute(block, 'seq', [(held[3 * turn + take], 4 * turn + put) for t...  5.82 us
  transfers between devices with their start and end apart: 13, of which 9 were waited for; matrix products, arithmetic and copies ran while one was open for 6% of the time, Pallas kernels for 15%

profile of v4, /device:TPU:6, one launch (start us, length us, event | category | flops | bytes accessed | tf_op | source)
XLA Modules:
  0.0 176.4 jit_solution(5615862111507225822)
XLA Ops:
  7.2 2.3 %pack.1 = bf16[8,3,128,128]{3,2,1,0:T(8,128)(2,1)} custom-call(bf16[1,128,768]{2,1,0:T(8,128)(2,1)} %query_ref.1, bf16[1,128,768]{2,1,0:T(8,128)(2,1)} %key_ref.1, bf16[1,128,768]{2,1,0:T(8,128)(2,1)} %value_ref.1), custom_call_target="tpu_custom_call" | custom-call | flops 1000000 | bytes 1000000 | tf_op jit(solution)/shard_map/pack/pallas_call | solution.py:224
  9.5 5.9 %all-to-all-start = ((bf16[8,3,128,128]{3,2,1,0:T(8,128)(2,1)}), bf16[8,3,128,128]{3,2,1,0:T(8,128)(2,1)S(1)}, u32[]{:S(2)}, u32[]{:S(2)}) async-start(bf16[8,3,128,128]{3,2,1,0:T(8,128)(2,1)} %pack.1), calls=%async_computation | async-start | bytes 1572864 | tf_op jit(solution)/shard_map/all_to_all | solution.py:46
  15.4 0.7 all-gather.2.cloned.1.call-update
  16.2 0.1 pad_add_fusion
  16.4 0.2 reduce-window.25
  16.6 0.1 copy.13
  16.7 0.1 reduce
  16.9 0.1 reshape.246
  17.1 2.1 %gather_fusion = bf16[256,1536]{1,0:T(8,128)(2,1)} fusion(bf16[128,1536]{1,0:T(8,128)(2,1)S(1)} %bitcast.28, s32[1024]{0:T(1024)S(1)} %pad_clamp_fusion.1), kind=kCustom, calls=%fused_computation | custom fusion | bytes 1573888 | tf_op jit(solution)/shard_map/gather | solution.py:246
  19.2 2.7 %select_convert_fusion.hidden_ref = bf16[4096,128]{1,0:T(8,128)(2,1)} fusion(s32[128]{0:T(128)S(1)} %pad.8, s32[4096]{0:T(1024)S(1)} %add_bitcast_fusion), kind=kLoop, calls=%fused_computation.2 | loop fusion | flops 1572864 | bytes 1065472 | tf_op jit(solution)/shard_map/convert_element_type | solution.py:305
  21.9 5.3 %all-to-all-done.input_ref = bf16[8,3,128,128]{3,2,1,0:T(8,128)(2,1)S(1)} async-done(((bf16[8,3,128,128]{3,2,1,0:T(8,128)(2,1)}), bf16[8,3,128,128]{3,2,1,0:T(8,128)(2,1)S(1)}, u32[]{:S(2)}, u32[]{:S(2)}) %all-to-all-start) | async-done | bytes 786464 | tf_op jit(solution)/shard_map/all_to_all | solution.py:46
  27.2 1.9 %collective-permute-start.1 = (bf16[8,2,128,128]{3,2,1,0:T(8,128)(2,1)S(1)}, bf16[8,2,128,128]{3,2,1,0:T(8,128)(2,1)S(1)}, u32[]{:S(2)}, u32[]{:S(2)}) collective-permute-start(bf16[8,2,128,128]{3,2,1,0:T(8,128)(2,1)S(1)} %slice.32.own_ref), channel_id=1, source_target_pairs={{0,16},{16,0},{32,48},{48,32},{64,80},{80,64},{96,112},{112,96},{1... | collective-permute-start | bytes 1572872 | tf_op jit(solution)/shard_map/ppermute | solution.py:37
  29.2 4.0 %collective-permute-start = (bf16[8,2,128,128]{3,2,1,0:T(8,128)(2,1)S(1)}, bf16[8,2,128,128]{3,2,1,0:T(8,128)(2,1)S(1)}, u32[]{:S(2)}, u32[]{:S(2)}) collective-permute-start(bf16[8,2,128,128]{3,2,1,0:T(8,128)(2,1)S(1)} %slice.32.own_ref), channel_id=1, source_target_pairs={{0,64},{16,80},{32,96},{48,112},{64,0},{80,16},{96,32},{112,48},{1... | collective-permute-start | bytes 1572872 | tf_op jit(solution)/shard_map/ppermute | solution.py:37
  33.2 0.9 and_convert_fusion.member_ref
  34.1 5.4 %all-to-all-start.1 = ((bf16[32,8,1536]{2,1,0:T(8,128)(2,1)}), bf16[32,8,1536]{2,1,0:T(8,128)(2,1)S(1)}, u32[]{:S(2)}, u32[]{:S(2)}) async-start(bf16[32,8,1536]{2,1,0:T(8,128)(2,1)} %bitcast.7), calls=%async_computation.1 | async-start | bytes 1572864 | tf_op jit(solution)/shard_map/all_to_all | solution.py:289
  39.5 5.3 %near.1 = (f32[8,128,1]{2,1,0:T(8,128)}, f32[8,128,256]{2,1,0:T(8,128)}) custom-call(bf16[8,3,128,128]{3,2,1,0:T(8,128)(2,1)} %copy-done.4, bf16[8,128,128]{2,1,0:T(8,128)(2,1)} %and_convert_fusion.member_ref, bf16[4096,128]{1,0:T(8,128)(2,1)} %select_convert_fusion.hidden_ref, bf16[8,2,128,128]{3,2,1,0:T(8,128)(2,1)} %copy-done.5, ...), custom_call_target="tpu_custom_call" | custom-call | flops 4000000000 | bytes 1000000 | tf_op jit(solution)/shard_map/near/pallas_call | solution.py:224
  44.8 2.6 %collective-permute-done.own_ref.far_ref = bf16[8,2,128,128]{3,2,1,0:T(8,128)(2,1)S(1)} collective-permute-done((bf16[8,2,128,128]{3,2,1,0:T(8,128)(2,1)S(1)}, bf16[8,2,128,128]{3,2,1,0:T(8,128)(2,1)S(1)}, u32[]{:S(2)}, u32[]{:S(2)}) %collective-permute-start) | collective-permute-done | bytes 524320 | tf_op jit(solution)/shard_map/ppermute | solution.py:37
  47.4 1.9 %collective-permute-start.2 = (bf16[8,2,128,128]{3,2,1,0:T(8,128)(2,1)S(1)}, bf16[8,2,128,128]{3,2,1,0:T(8,128)(2,1)S(1)}, u32[]{:S(2)}, u32[]{:S(2)}) collective-permute-start(bf16[8,2,128,128]{3,2,1,0:T(8,128)(2,1)S(1)} %collective-permute-done.own_ref.far_ref), channel_id=1, source_target_pairs={{0,16},{16,0},{32,48},{48,32},{64,80},{80,64},{96,112},{112,96},{1... | collective-permute-start | bytes 1572872 | tf_op jit(solution)/shard_map/ppermute | solution.py:37
  49.3 0.2 dynamic-slice_reduce_fusion
  49.5 0.1 reduce.1
  49.7 0.1 convert_reduce_fusion.1
  49.8 5.2 %all-to-all-done.1 = bf16[32,8,1536]{2,1,0:T(8,128)(2,1)S(1)} async-done(((bf16[32,8,1536]{2,1,0:T(8,128)(2,1)}), bf16[32,8,1536]{2,1,0:T(8,128)(2,1)S(1)}, u32[]{:S(2)}, u32[]{:S(2)}) %all-to-all-start.1) | async-done | bytes 786464 | tf_op jit(solution)/shard_map/all_to_all | solution.py:289
  55.0 0.9 gather_fusion.1
  55.9 1.9 %broadcast_in_dim.29 = bf16[8,128,1536]{2,1,0:T(8,128)(2,1)} broadcast(bf16[128,1536]{1,0:T(8,128)(2,1)S(1)} %gather_fusion.1), dimensions={1,2} | broadcast | bytes 3538944 | tf_op jit(solution)/shard_map/broadcast_in_dim | solution.py:328
  57.8 5.3 %all-to-all-start.2 = ((bf16[8,128,1536]{2,1,0:T(8,128)(2,1)}), bf16[8,128,1536]{2,1,0:T(8,128)(2,1)S(1)}, u32[]{:S(2)}, u32[]{:S(2)}) async-start(bf16[8,128,1536]{2,1,0:T(8,128)(2,1)} %broadcast_in_dim.29), calls=%async_computation.2 | async-start | bytes 6291456 | tf_op jit(solution)/shard_map/all_to_all | solution.py:46
  63.1 7.6 %far.1 = (bf16[8,128,128]{2,1,0:T(8,128)(2,1)}, f32[8,128,128]{2,1,0:T(8,128)}, f32[8,128,128]{2,1,0:T(8,128)}) custom-call(bf16[8,3,128,128]{3,2,1,0:T(8,128)(2,1)} %copy-done.4, bf16[8,128,128]{2,1,0:T(8,128)(2,1)} %and_convert_fusion.member_ref, bf16[4096,128]{1,0:T(8,128)(2,1)} %select_convert_fusion.hidden_ref, bf16[8,2,128,128]{3,2,1,0:T(8,128)(2,1)} %copy-done.8, ...), custom_call_target="tpu_custom_call" | custom-call | flops 4000000000 | bytes 1000000 | tf_op jit(solution)/shard_map/far/pallas_call | solution.py:224
  70.7 30.2 %all-to-all-done.2.rows_ref = bf16[8,128,1536]{2,1,0:T(8,128)(2,1)S(1)} async-done(((bf16[8,128,1536]{2,1,0:T(8,128)(2,1)}), bf16[8,128,1536]{2,1,0:T(8,128)(2,1)S(1)}, u32[]{:S(2)}, u32[]{:S(2)}) %all-to-all-start.2) | async-done | bytes 3145760 | tf_op jit(solution)/shard_map/all_to_all | solution.py:46
  100.9 0.9 copy-done.3
  101.9 0.6 outer.1
  102.5 0.7 copy-done.1
  103.2 5.9 %all-to-all-start.4 = ((bf16[4,32,1536]{2,1,0:T(8,128)(2,1)}), bf16[4,32,1536]{2,1,0:T(8,128)(2,1)}, u32[]{:S(2)}, u32[]{:S(2)}) async-start(bf16[4,32,1536]{2,1,0:T(8,128)(2,1)} %copy-done.1), calls=%async_computation.4 | async-start | bytes 786432 | tf_op jit(solution)/shard_map/all_to_all | solution.py:353
  109.1 1.0 constant_dynamic-slice_fusion.weight_ref
  110.1 1.0 project.1.grad_ref
  111.1 0.7 copy-done.2
  111.8 3.2 %all-to-all-done.4.pieces_ref = bf16[4,32,1536]{2,1,0:T(8,128)(2,1)} async-done(((bf16[4,32,1536]{2,1,0:T(8,128)(2,1)}), bf16[4,32,1536]{2,1,0:T(8,128)(2,1)}, u32[]{:S(2)}, u32[]{:S(2)}) %all-to-all-start.4) | async-done | bytes 393248 | tf_op jit(solution)/shard_map/all_to_all | solution.py:353
  115.0 1.8 %sum.1 = bf16[16,32,96]{2,1,0:T(8,128)(2,1)} custom-call(bf16[4,32,1536]{2,1,0:T(8,128)(2,1)} %all-to-all-done.4.pieces_ref), custom_call_target="tpu_custom_call" | custom-call | flops 1000000 | bytes 1000000 | tf_op jit(solution)/shard_map/sum/pallas_call | solution.py:224
  116.8 14.7 %all-to-all-start.5 = ((bf16[16,32,96]{2,1,0:T(8,128)(2,1)}), bf16[16,32,96]{2,1,0:T(8,128)(2,1)S(1)}, u32[]{:S(2)}, u32[]{:S(2)}) async-start(bf16[16,32,96]{2,1,0:T(8,128)(2,1)} %sum.1), calls=%async_computation.5 | async-start | bytes 262144 | tf_op jit(solution)/shard_map/all_to_all | solution.py:369
  131.4 12.1 %attend_grad.1 = bf16[8,128,128]{2,1,0:T(8,128)(2,1)} custom-call(bf16[8,3,128,128]{3,2,1,0:T(8,128)(2,1)} %copy-done.4, bf16[8,128,128]{2,1,0:T(8,128)(2,1)} %and_convert_fusion.member_ref, bf16[4096,128]{1,0:T(8,128)(2,1)} %select_convert_fusion.hidden_ref, bf16[8,128,128]{2,1,0:T(8,128)(2,1)} %copy-done.2, f32[8,128,128]{2,1,0:T(8,128)} %get-tuple-element.27.exact_ref, ...), custom_call_target="tpu_custom_call" | custom-call | flops 10000000000 | bytes 1000000 | tf_op jit(solution)/shard_map/attend_grad/pallas_call | solution.py:224
  143.5 2.6 %all-to-all-done.5 = bf16[16,32,96]{2,1,0:T(8,128)(2,1)S(1)} async-done(((bf16[16,32,96]{2,1,0:T(8,128)(2,1)}), bf16[16,32,96]{2,1,0:T(8,128)(2,1)S(1)}, u32[]{:S(2)}, u32[]{:S(2)}) %all-to-all-start.5) | async-done | bytes 98336 | tf_op jit(solution)/shard_map/all_to_all | solution.py:369
  146.1 4.1 %all-to-all-start.3 = ((bf16[8,128,128]{2,1,0:T(8,128)(2,1)}), bf16[8,128,128]{2,1,0:T(8,128)(2,1)S(1)}, u32[]{:S(2)}, u32[]{:S(2)}) async-start(bf16[8,128,128]{2,1,0:T(8,128)(2,1)} %attend_grad.1), calls=%async_computation.3 | async-start | bytes 524288 | tf_op jit(solution)/shard_map/all_to_all | solution.py:46
  150.2 1.9 %collective-permute-start.4 = (f32[32,96]{1,0:T(8,128)S(1)}, f32[32,96]{1,0:T(8,128)S(1)}, u32[]{:S(2)}, u32[]{:S(2)}) collective-permute-start(f32[32,96]{1,0:T(8,128)S(1)} %broadcast_multiply_fusion), channel_id=1, source_target_pairs={{0,16},{64,32},{80,80},{48,96},{96,144},{128,160},{144,208},{208,2... | collective-permute-start | bytes 36872 | tf_op jit(solution)/shard_map/ppermute | solution.py:62
  152.2 4.2 %all-to-all-done.3.slots_ref = bf16[8,128,128]{2,1,0:T(8,128)(2,1)S(1)} async-done(((bf16[8,128,128]{2,1,0:T(8,128)(2,1)}), bf16[8,128,128]{2,1,0:T(8,128)(2,1)S(1)}, u32[]{:S(2)}, u32[]{:S(2)}) %all-to-all-start.3) | async-done | bytes 262176 | tf_op jit(solution)/shard_map/all_to_all | solution.py:46
  156.3 0.7 join.1
  157.0 4.8 %collective-permute-start.3 = (f32[32,96]{1,0:T(8,128)S(1)}, f32[32,96]{1,0:T(8,128)S(1)}, u32[]{:S(2)}, u32[]{:S(2)}) collective-permute-start(f32[32,96]{1,0:T(8,128)S(1)} %broadcast_multiply_fusion), channel_id=1, source_target_pairs={{0,0},{16,16},{64,48},{80,64},{32,80},{48,112},{96,128},{112,144},... | collective-permute-start | bytes 36872 | tf_op jit(solution)/shard_map/ppermute | solution.py:62
  161.8 1.3 collective-permute-start.5
  163.1 0.1 collective-permute-done.3
  163.2 5.7 %collective-permute-done.5 = f32[32,96]{1,0:T(8,128)S(1)} collective-permute-done((f32[32,96]{1,0:T(8,128)S(1)}, f32[32,96]{1,0:T(8,128)S(1)}, u32[]{:S(2)}, u32[]{:S(2)}) %collective-permute-start.5) | collective-permute-done | bytes 12320 | tf_op jit(solution)/shard_map/ppermute | solution.py:62
  168.9 0.6 fusion
  (45 shorter events, 0.5 us)
Async XLA Ops:
  7.2 9.9 %copy-start = (bf16[1,128,1536]{2,1,0:T(8,128)(2,1)S(1)}, bf16[1,128,1536]{2,1,0:T(8,128)(2,1)}, u32[]{:S(2)}) copy-start(bf16[1,128,1536]{2,1,0:T(8,128)(2,1)} %param.10) | copy-start | bytes 1179652
  7.2 9.2 %copy-start.10 = (s32[1,5]{1,0:T(1,128)S(1)}, s32[1,5]{1,0:T(1,128)}, u32[]{:S(2)}) copy-start(s32[1,5]{1,0:T(1,128)} %param.13) | copy-start | bytes 64
  7.2 9.4 %copy-start.6 = (s32[1,32,32]{2,1,0:T(8,128)S(1)}, s32[1,32,32]{2,1,0:T(8,128)}, u32[]{:S(2)}) copy-start(s32[1,32,32]{2,1,0:T(8,128)} %param.12) | copy-start | bytes 12292
  9.5 17.7 %all-to-all-start = ((bf16[8,3,128,128]{3,2,1,0:T(8,128)(2,1)}), bf16[8,3,128,128]{3,2,1,0:T(8,128)(2,1)S(1)}, u32[]{:S(2)}, u32[]{:S(2)}) async-start(bf16[8,3,128,128]{3,2,1,0:T(8,128)(2,1)} %pack.1), calls=%async_computation | async-start | bytes 1572864 | tf_op jit(solution)/shard_map/all_to_all | solution.py:46
  15.4 93.7 %all-gather.2.cloned.1.call-start = ((), (), s32[]{:S(2)}) async-start(), calls=%async_computation.6 | async-start | bytes 2506752 | tf_op jit(solution)/shard_map/all_gather | solution.py:272
  27.1 12.4 %copy-start.4 = (bf16[8,3,128,128]{3,2,1,0:T(8,128)(2,1)}, bf16[8,3,128,128]{3,2,1,0:T(8,128)(2,1)S(1)}, u32[]{:S(2)}) copy-start(bf16[8,3,128,128]{3,2,1,0:T(8,128)(2,1)S(1)} %all-to-all-done.input_ref) | copy-start | bytes 2359300
  27.2 12.3 %copy-start.5 = (bf16[8,2,128,128]{3,2,1,0:T(8,128)(2,1)}, bf16[8,2,128,128]{3,2,1,0:T(8,128)(2,1)S(1)}, u32[]{:S(2)}) copy-start(bf16[8,2,128,128]{3,2,1,0:T(8,128)(2,1)S(1)} %slice.32.own_ref) | copy-start | bytes 1572868
  27.2 6.9 %collective-permute-start.1 = (bf16[8,2,128,128]{3,2,1,0:T(8,128)(2,1)S(1)}, bf16[8,2,128,128]{3,2,1,0:T(8,128)(2,1)S(1)}, u32[]{:S(2)}, u32[]{:S(2)}) collective-permute-start(bf16[8,2,128,128]{3,2,1,0:T(8,128)(2,1)S(1)} %slice.32.own_ref), channel_id=1, source_target_pairs={{0,16},{16,0},{32,48},{48,32},{64,80},{80,64},{96,112},{112,96},{1... | collective-permute-start | bytes 1572872 | tf_op jit(solution)/shard_map/ppermute | solution.py:37
  29.2 18.2 %collective-permute-start = (bf16[8,2,128,128]{3,2,1,0:T(8,128)(2,1)S(1)}, bf16[8,2,128,128]{3,2,1,0:T(8,128)(2,1)S(1)}, u32[]{:S(2)}, u32[]{:S(2)}) collective-permute-start(bf16[8,2,128,128]{3,2,1,0:T(8,128)(2,1)S(1)} %slice.32.own_ref), channel_id=1, source_target_pairs={{0,64},{16,80},{32,96},{48,112},{64,0},{80,16},{96,32},{112,48},{1... | collective-permute-start | bytes 1572872 | tf_op jit(solution)/shard_map/ppermute | solution.py:37
  34.1 5.4 %copy-start.7 = (bf16[8,2,128,128]{3,2,1,0:T(8,128)(2,1)}, bf16[8,2,128,128]{3,2,1,0:T(8,128)(2,1)S(1)}, u32[]{:S(2)}) copy-start(bf16[8,2,128,128]{3,2,1,0:T(8,128)(2,1)S(1)} %collective-permute-done.1.core_ref) | copy-start | bytes 1572868
  34.1 20.9 %all-to-all-start.1 = ((bf16[32,8,1536]{2,1,0:T(8,128)(2,1)}), bf16[32,8,1536]{2,1,0:T(8,128)(2,1)S(1)}, u32[]{:S(2)}, u32[]{:S(2)}) async-start(bf16[32,8,1536]{2,1,0:T(8,128)(2,1)} %bitcast.7), calls=%async_computation.1 | async-start | bytes 1572864 | tf_op jit(solution)/shard_map/all_to_all | solution.py:289
  47.4 10.4 %copy-start.8 = (bf16[8,2,128,128]{3,2,1,0:T(8,128)(2,1)}, bf16[8,2,128,128]{3,2,1,0:T(8,128)(2,1)S(1)}, u32[]{:S(2)}) copy-start(bf16[8,2,128,128]{3,2,1,0:T(8,128)(2,1)S(1)} %collective-permute-done.own_ref.far_ref) | copy-start | bytes 1572868
  47.4 8.5 %collective-permute-start.2 = (bf16[8,2,128,128]{3,2,1,0:T(8,128)(2,1)S(1)}, bf16[8,2,128,128]{3,2,1,0:T(8,128)(2,1)S(1)}, u32[]{:S(2)}, u32[]{:S(2)}) collective-permute-start(bf16[8,2,128,128]{3,2,1,0:T(8,128)(2,1)S(1)} %collective-permute-done.own_ref.far_ref), channel_id=1, source_target_pairs={{0,16},{16,0},{32,48},{48,32},{64,80},{80,64},{96,112},{112,96},{1... | collective-permute-start | bytes 1572872 | tf_op jit(solution)/shard_map/ppermute | solution.py:37
  55.9 1.9 %copy-start.9 = (bf16[8,2,128,128]{3,2,1,0:T(8,128)(2,1)}, bf16[8,2,128,128]{3,2,1,0:T(8,128)(2,1)S(1)}, u32[]{:S(2)}) copy-start(bf16[8,2,128,128]{3,2,1,0:T(8,128)(2,1)S(1)} %collective-permute-done.2.core_ref.far_core_ref) | copy-start | bytes 1572868
  57.8 43.1 %all-to-all-start.2 = ((bf16[8,128,1536]{2,1,0:T(8,128)(2,1)}), bf16[8,128,1536]{2,1,0:T(8,128)(2,1)S(1)}, u32[]{:S(2)}, u32[]{:S(2)}) async-start(bf16[8,128,1536]{2,1,0:T(8,128)(2,1)} %broadcast_in_dim.29), calls=%async_computation.2 | async-start | bytes 6291456 | tf_op jit(solution)/shard_map/all_to_all | solution.py:46
  100.9 1.0 copy-start.3
  102.5 0.7 copy-start.1
  103.2 11.7 %all-to-all-start.4 = ((bf16[4,32,1536]{2,1,0:T(8,128)(2,1)}), bf16[4,32,1536]{2,1,0:T(8,128)(2,1)}, u32[]{:S(2)}, u32[]{:S(2)}) async-start(bf16[4,32,1536]{2,1,0:T(8,128)(2,1)} %copy-done.1), calls=%async_computation.4 | async-start | bytes 786432 | tf_op jit(solution)/shard_map/all_to_all | solution.py:353
  111.1 0.7 copy-start.2
  116.8 29.3 %all-to-all-start.5 = ((bf16[16,32,96]{2,1,0:T(8,128)(2,1)}), bf16[16,32,96]{2,1,0:T(8,128)(2,1)S(1)}, u32[]{:S(2)}, u32[]{:S(2)}) async-start(bf16[16,32,96]{2,1,0:T(8,128)(2,1)} %sum.1), calls=%async_computation.5 | async-start | bytes 262144 | tf_op jit(solution)/shard_map/all_to_all | solution.py:369
  146.1 10.2 %all-to-all-start.3 = ((bf16[8,128,128]{2,1,0:T(8,128)(2,1)}), bf16[8,128,128]{2,1,0:T(8,128)(2,1)S(1)}, u32[]{:S(2)}, u32[]{:S(2)}) async-start(bf16[8,128,128]{2,1,0:T(8,128)(2,1)} %attend_grad.1), calls=%async_computation.3 | async-start | bytes 524288 | tf_op jit(solution)/shard_map/all_to_all | solution.py:46
  150.2 12.9 %collective-permute-start.4 = (f32[32,96]{1,0:T(8,128)S(1)}, f32[32,96]{1,0:T(8,128)S(1)}, u32[]{:S(2)}, u32[]{:S(2)}) collective-permute-start(f32[32,96]{1,0:T(8,128)S(1)} %broadcast_multiply_fusion), channel_id=1, source_target_pairs={{0,16},{64,32},{80,80},{48,96},{96,144},{128,160},{144,208},{208,2... | collective-permute-start | bytes 36872 | tf_op jit(solution)/shard_map/ppermute | solution.py:62
  157.0 6.2 %collective-permute-start.3 = (f32[32,96]{1,0:T(8,128)S(1)}, f32[32,96]{1,0:T(8,128)S(1)}, u32[]{:S(2)}, u32[]{:S(2)}) collective-permute-start(f32[32,96]{1,0:T(8,128)S(1)} %broadcast_multiply_fusion), channel_id=1, source_target_pairs={{0,0},{16,16},{64,48},{80,64},{32,80},{48,112},{96,128},{112,144},... | collective-permute-start | bytes 36872 | tf_op jit(solution)/shard_map/ppermute | solution.py:62
  161.8 7.1 %collective-permute-start.5 = (f32[32,96]{1,0:T(8,128)S(1)}, f32[32,96]{1,0:T(8,128)S(1)}, u32[]{:S(2)}, u32[]{:S(2)}) collective-permute-start(f32[32,96]{1,0:T(8,128)S(1)} %broadcast_multiply_fusion), channel_id=1, source_target_pairs={{16,32},{32,96},{112,160},{192,224},{176,288},{256,352},{336,416},... | collective-permute-start | bytes 36872 | tf_op jit(solution)/shard_map/ppermute | solution.py:62
Sparse Core Ops, SparseCore 0:
  18.3 78.2 all-gather.1

commit v5 on v4

--- a/solution.py
+++ b/solution.py
@@ -13,7 +13,7 @@
 PAIR = 2
 SLOTS = SIDE * PAIR
 QUERY_SLOTS = 2
-KEY_SLOTS = 4
+KEY_SLOTS = 8
 LOG2_E = 1.4426950408889634
 HIDDEN = -1e30
 LOWEST = -1e20
@@ -281,12 +281,10 @@
         scratch_shapes=[pltpu.SemaphoreType.DMA((SLOTS, 3))],
     )(student_query, key_cache, value_cache)
     inputs = trade(slots)
+    inputs, packed = lax.optimization_barrier((inputs, pack_rows(grad_rows[0], counts, me)))
     own = inputs[:, 1:]
-    own, packed = lax.optimization_barrier((own, pack_rows(grad_rows[0], counts, me)))
-    far = send(own, dx=PAIR)
+    arrived = lax.all_to_all(packed, "seq", 0, 0, tiled=True)
     beside = send(own, dcore=1)
-    packed, beside = lax.optimization_barrier((packed, beside))
-    arrived = lax.all_to_all(packed, "seq", 0, 0, tiled=True)
 
     rank = jnp.arange(SLOTS, dtype=jnp.int32)
 
@@ -322,12 +320,12 @@
     )(
         inputs, member, hidden, own, beside
     )
-    far, carry = lax.optimization_barrier((far, carry))
-    far_beside = send(far, dcore=1)
     ordered = unpack_rows(arrived, counts, me, row_count)
     copies = jnp.broadcast_to(ordered[None], (SLOTS,) + ordered.shape)
-    far_beside, copies = lax.optimization_barrier((far_beside, copies))
+    late_own, copies, carry = lax.optimization_barrier((own, copies, carry))
+    far = send(late_own, dx=PAIR)
     group_rows = trade(copies)
+    far_beside = send(far, dcore=1)
     attended, exact, level = call(
         functools.partial(far_kernel, scale),
         [narrow, wide, wide],
@@ -358,17 +356,18 @@
     (grad_query,) = call(functools.partial(grad_kernel, scale), [narrow], "attend_grad", 1e10, limit=56, blocks={0: only_query})(
         inputs, member, hidden, head_grad, exact, level, own, beside, far, far_beside
     )
-    grad_query = trade(grad_query)
-    (grad_query_rows,) = call(
-        functools.partial(join_kernel, head_count), [((1, row_count, head_width), jnp.bfloat16)], "join", 1e6
-    )(grad_query)
-
+    pieces, grad_query = lax.optimization_barrier((pieces, grad_query))
     (clip_parts,) = call(
         sum_kernel, [((clip_count, share, feature_count // clip_count), jnp.bfloat16)], "sum", 1e6
     )(pieces)
     terms = lax.all_to_all(clip_parts, "dp", 0, 0, tiled=True)
     total = jnp.sum(terms.astype(jnp.float32), axis=0) / float(clip_count)
+    total, grad_query = lax.optimization_barrier((total, grad_query))
     total = place_blocks(total, me)
+    grad_query = trade(grad_query)
+    (grad_query_rows,) = call(
+        functools.partial(join_kernel, head_count), [((1, row_count, head_width), jnp.bfloat16)], "join", 1e6
+    )(grad_query)
     return (grad_query_rows, total)
 
 

time: 177 us -> 196 us (1.11)
  the two profiles are of different devices: /device:TPU:6 before, /device:TPU:1 now
where the time goes in v5:
time: 196 us; the launch traced here: 195 us
  waiting for transfers between devices  63.5 us (32%)
  starting transfers between devices  47.5 us (24%)
  Pallas kernels  27.5 us (14%)
  blocking collectives  26.9 us (14%)
  between operations  14.4 us (7%)
  local copies, waits for them, and re-layouts  9.68 us (5%)
  other arithmetic  5.23 us (3%)
    ppermute x3, waiting for transfers between devices, send(): return lax.ppermute(value, 'seq', pairs)  46.1 us
    pallas_call x8, Pallas kernels, run(): pl.pallas_call(kernel, out_shape=[jax.ShapeDtypeStruct(shape, dtype) for...  27.5 us
    all_to_all x1, blocking collectives, shards(): terms = lax.all_to_all(clip_parts, 'dp', 0, 0, tiled=True)  26.9 us
    all_to_all x3, starting transfers between devices, trade(): lax.all_to_all(slots, 'seq', 0, 0, axis_index_groups=groups, tiled=True)  16.9 us
    ppermute x3, starting transfers between devices, send(): return lax.ppermute(value, 'seq', pairs)  13.3 us
    all_to_all x3, waiting for transfers between devices, trade(): lax.all_to_all(slots, 'seq', 0, 0, axis_index_groups=groups, tiled=True)  9.7 us
    ppermute x3, starting transfers between devices, pass_on(): lax.ppermute(block, 'seq', [(held[3 * turn + take], 4 * turn + put) for t...  8.97 us
    all_to_all x1, waiting for transfers between devices, shards(): arrived = lax.all_to_all(packed, 'seq', 0, 0, tiled=True)  6.99 us
  transfers between devices with their start and end apart: 12, of which 5 were waited for; matrix products, arithmetic and copies ran while one was open for 6% of the time, Pallas kernels for 13%

profile of v5, /device:TPU:1, one launch (start us, length us, event | category | flops | bytes accessed | tf_op | source)
XLA Modules:
  0.0 194.6 jit_solution(13183203779140090599)
XLA Ops:
  7.2 0.7 all-gather.2.cloned.1.call-update
  7.9 2.2 %pack.1 = bf16[8,3,128,128]{3,2,1,0:T(8,128)(2,1)} custom-call(bf16[1,128,768]{2,1,0:T(8,128)(2,1)} %query_ref.1, bf16[1,128,768]{2,1,0:T(8,128)(2,1)} %key_ref.1, bf16[1,128,768]{2,1,0:T(8,128)(2,1)} %value_ref.1), custom_call_target="tpu_custom_call" | custom-call | flops 1000000 | bytes 1000000 | tf_op jit(solution)/shard_map/pack/pallas_call | solution.py:224
  10.2 6.0 %all-to-all-start = ((bf16[8,3,128,128]{3,2,1,0:T(8,128)(2,1)}), bf16[8,3,128,128]{3,2,1,0:T(8,128)(2,1)S(1)}, u32[]{:S(2)}, u32[]{:S(2)}) async-start(bf16[8,3,128,128]{3,2,1,0:T(8,128)(2,1)} %pack.1), calls=%async_computation | async-start | bytes 1572864 | tf_op jit(solution)/shard_map/all_to_all | solution.py:46
  16.1 0.2 dynamic-slice_reduce_fusion
  16.4 0.1 iota_add_fusion
  16.4 0.1 pad_add_fusion
  16.5 0.1 add_bitcast_fusion
  16.6 0.2 reduce-window.26
  16.8 0.1 copy.13
  16.9 0.1 reduce
  17.1 0.1 compare_select_fusion
  17.1 0.1 reshape.246
  17.3 0.1 reduce.1
  17.4 2.2 %gather_fusion = bf16[256,1536]{1,0:T(8,128)(2,1)} fusion(bf16[128,1536]{1,0:T(8,128)(2,1)S(1)} %bitcast.28, s32[1024]{0:T(1024)S(1)} %pad_clamp_fusion.1), kind=kCustom, calls=%fused_computation | custom fusion | bytes 1573888 | tf_op jit(solution)/shard_map/gather | solution.py:246
  19.6 0.1 convert_reduce_fusion.1
  19.7 2.7 %select_convert_fusion.hidden_ref = bf16[4096,128]{1,0:T(8,128)(2,1)} fusion(s32[128]{0:T(128)S(1)} %pad.8, s32[4096]{0:T(1024)S(1)} %add_bitcast_fusion), kind=kLoop, calls=%fused_computation.2 | loop fusion | flops 1572864 | bytes 1065472 | tf_op jit(solution)/shard_map/convert_element_type | solution.py:303
  22.4 2.7 %all-to-all-done.input_ref = bf16[8,3,128,128]{3,2,1,0:T(8,128)(2,1)S(1)} async-done(((bf16[8,3,128,128]{3,2,1,0:T(8,128)(2,1)}), bf16[8,3,128,128]{3,2,1,0:T(8,128)(2,1)S(1)}, u32[]{:S(2)}, u32[]{:S(2)}) %all-to-all-start) | async-done | bytes 786464 | tf_op jit(solution)/shard_map/all_to_all | solution.py:46
  25.2 7.5 %collective-permute-start = (bf16[8,2,128,128]{3,2,1,0:T(8,128)(2,1)S(1)}, bf16[8,2,128,128]{3,2,1,0:T(8,128)(2,1)S(1)}, u32[]{:S(2)}, u32[]{:S(2)}) collective-permute-start(bf16[8,2,128,128]{3,2,1,0:T(8,128)(2,1)S(1)} %slice.21.own_ref), channel_id=1, source_target_pairs={{0,16},{16,0},{32,48},{48,32},{64,80},{80,64},{96,112},{112,96},{1... | collective-permute-start | bytes 1572872 | tf_op jit(solution)/shard_map/ppermute | solution.py:37
  32.7 3.9 %all-to-all-start.1 = ((bf16[32,8,1536]{2,1,0:T(8,128)(2,1)}), bf16[32,8,1536]{2,1,0:T(8,128)(2,1)S(1)}, u32[]{:S(2)}, u32[]{:S(2)}) async-start(bf16[32,8,1536]{2,1,0:T(8,128)(2,1)} %bitcast.3), calls=%async_computation.1 | async-start | bytes 1572864 | tf_op jit(solution)/shard_map/all_to_all | solution.py:286
  36.6 0.9 and_convert_fusion.member_ref
  37.5 0.8 copy-done.7
  38.3 5.4 %near.1 = (f32[8,128,1]{2,1,0:T(8,128)}, f32[8,128,256]{2,1,0:T(8,128)}) custom-call(bf16[8,3,128,128]{3,2,1,0:T(8,128)(2,1)} %copy-done.4, bf16[8,128,128]{2,1,0:T(8,128)(2,1)} %and_convert_fusion.member_ref, bf16[4096,128]{1,0:T(8,128)(2,1)} %select_convert_fusion.hidden_ref, bf16[8,2,128,128]{3,2,1,0:T(8,128)(2,1)} %copy-done.5, ...), custom_call_target="tpu_custom_call" | custom-call | flops 4000000000 | bytes 1000000 | tf_op jit(solution)/shard_map/near/pallas_call | solution.py:224
  43.8 7.0 %all-to-all-done.1 = bf16[32,8,1536]{2,1,0:T(8,128)(2,1)S(1)} async-done(((bf16[32,8,1536]{2,1,0:T(8,128)(2,1)}), bf16[32,8,1536]{2,1,0:T(8,128)(2,1)S(1)}, u32[]{:S(2)}, u32[]{:S(2)}) %all-to-all-start.1) | async-done | bytes 786464 | tf_op jit(solution)/shard_map/all_to_all | solution.py:286
  50.8 0.9 gather_fusion.1
  51.6 1.9 broadcast_in_dim.29
  53.6 3.7 %all-to-all-start.2 = ((bf16[8,128,1536]{2,1,0:T(8,128)(2,1)}), bf16[8,128,1536]{2,1,0:T(8,128)(2,1)S(1)}, u32[]{:S(2)}, u32[]{:S(2)}) async-start(bf16[8,128,1536]{2,1,0:T(8,128)(2,1)} %broadcast_in_dim.29), calls=%async_computation.2 | async-start | bytes 6291456 | tf_op jit(solution)/shard_map/all_to_all | solution.py:46
  57.2 3.0 %collective-permute-start.1 = (bf16[8,2,128,128]{3,2,1,0:T(8,128)(2,1)}, bf16[8,2,128,128]{3,2,1,0:T(8,128)(2,1)}, u32[]{:S(2)}, u32[]{:S(2)}) collective-permute-start(bf16[8,2,128,128]{3,2,1,0:T(8,128)(2,1)} %copy-done.5), channel_id=1, source_target_pairs={{0,64},{16,80},{32,96},{48,112},{64,0},{80,16},{96,32},{112,48},{1... | collective-permute-start | bytes 1572872 | tf_op jit(solution)/shard_map/ppermute | solution.py:37
  60.2 44.3 %collective-permute-done.1.own_ref.far_ref = bf16[8,2,128,128]{3,2,1,0:T(8,128)(2,1)} collective-permute-done((bf16[8,2,128,128]{3,2,1,0:T(8,128)(2,1)}, bf16[8,2,128,128]{3,2,1,0:T(8,128)(2,1)}, u32[]{:S(2)}, u32[]{:S(2)}) %collective-permute-start.1) | collective-permute-done | bytes 524320 | tf_op jit(solution)/shard_map/ppermute | solution.py:37
  104.5 2.9 %collective-permute-start.2 = (bf16[8,2,128,128]{3,2,1,0:T(8,128)(2,1)}, bf16[8,2,128,128]{3,2,1,0:T(8,128)(2,1)}, u32[]{:S(2)}, u32[]{:S(2)}) collective-permute-start(bf16[8,2,128,128]{3,2,1,0:T(8,128)(2,1)} %collective-permute-done.1.own_ref.far_ref), channel_id=1, source_target_pairs={{0,16},{16,0},{32,48},{48,32},{64,80},{80,64},{96,112},{112,96},{1... | collective-permute-start | bytes 1572872 | tf_op jit(solution)/shard_map/ppermute | solution.py:37
  107.4 1.8 collective-permute-done.2.core_ref.far_core_ref
  109.2 6.3 %far.1 = (bf16[8,128,128]{2,1,0:T(8,128)(2,1)}, f32[8,128,128]{2,1,0:T(8,128)}, f32[8,128,128]{2,1,0:T(8,128)}) custom-call(bf16[8,3,128,128]{3,2,1,0:T(8,128)(2,1)} %copy-done.4, bf16[8,128,128]{2,1,0:T(8,128)(2,1)} %and_convert_fusion.member_ref, bf16[4096,128]{1,0:T(8,128)(2,1)} %select_convert_fusion.hidden_ref, ...), custom_call_target="tpu_custom_call" | custom-call | flops 4000000000 | bytes 1000000 | tf_op jit(solution)/shard_map/far/pallas_call | solution.py:224
  115.6 0.9 copy-done.3
  116.5 0.6 outer.1
  117.1 0.8 copy-done.1
  117.9 4.5 %all-to-all-start.3 = ((bf16[4,32,1536]{2,1,0:T(8,128)(2,1)}), bf16[4,32,1536]{2,1,0:T(8,128)(2,1)}, u32[]{:S(2)}, u32[]{:S(2)}) async-start(bf16[4,32,1536]{2,1,0:T(8,128)(2,1)} %copy-done.1), calls=%async_computation.3 | async-start | bytes 786432 | tf_op jit(solution)/shard_map/all_to_all | solution.py:351
  122.3 1.0 constant_dynamic-slice_fusion.weight_ref
  123.4 1.0 project.1.grad_ref
  124.3 0.7 copy-done.2
  125.0 10.1 %attend_grad.1 = bf16[8,128,128]{2,1,0:T(8,128)(2,1)} custom-call(bf16[8,3,128,128]{3,2,1,0:T(8,128)(2,1)} %copy-done.4, bf16[8,128,128]{2,1,0:T(8,128)(2,1)} %and_convert_fusion.member_ref, bf16[4096,128]{1,0:T(8,128)(2,1)} %select_convert_fusion.hidden_ref, bf16[8,128,128]{2,1,0:T(8,128)(2,1)} %copy-done.2, f32[8,128,128]{2,1,0:T(8,128)} %get-tuple-element.26.exact_ref, ...), custom_call_target="tpu_custom_call" | custom-call | flops 10000000000 | bytes 1000000 | tf_op jit(solution)/shard_map/attend_grad/pallas_call | solution.py:224
  135.1 1.1 sum.1
  136.2 26.9 %all_to_all.30 = bf16[16,32,96]{2,1,0:T(8,128)(2,1)S(1)} all-to-all(bf16[16,32,96]{2,1,0:T(8,128)(2,1)S(1)} %sum.1), channel_id=1, replica_groups=mesh['seq'=32,'dp'=16] {'dp'}, dimensions={0} | all-to-all | bytes 196608 | tf_op jit(solution)/shard_map/all_to_all | solution.py:363
  163.2 1.3 collective-permute-start.4
  164.5 0.7 collective-permute-start.3
  165.2 7.0 %collective-permute-start.5 = (f32[32,96]{1,0:T(8,128)S(1)}, f32[32,96]{1,0:T(8,128)S(1)}, u32[]{:S(2)}, u32[]{:S(2)}) collective-permute-start(f32[32,96]{1,0:T(8,128)S(1)} %broadcast_multiply_fusion), channel_id=1, source_target_pairs={{16,32},{32,96},{112,160},{192,224},{176,288},{256,352},{336,416},... | collective-permute-start | bytes 36872 | tf_op jit(solution)/shard_map/ppermute | solution.py:62
  172.2 7.3 %all-to-all-start.5 = ((bf16[8,128,128]{2,1,0:T(8,128)(2,1)}), bf16[8,128,128]{2,1,0:T(8,128)(2,1)S(1)}, u32[]{:S(2)}, u32[]{:S(2)}) async-start(bf16[8,128,128]{2,1,0:T(8,128)(2,1)} %attend_grad.1), calls=%async_computation.5 | async-start | bytes 524288 | tf_op jit(solution)/shard_map/all_to_all | solution.py:46
  179.5 0.6 fusion
  180.1 7.0 %all-to-all-done.5.slots_ref = bf16[8,128,128]{2,1,0:T(8,128)(2,1)S(1)} async-done(((bf16[8,128,128]{2,1,0:T(8,128)(2,1)}), bf16[8,128,128]{2,1,0:T(8,128)(2,1)S(1)}, u32[]{:S(2)}, u32[]{:S(2)}) %all-to-all-start.5) | async-done | bytes 262176 | tf_op jit(solution)/shard_map/all_to_all | solution.py:46
  187.1 0.7 join.1
  (40 shorter events, 0.4 us)
Async XLA Ops:
  7.2 10.3 %copy-start = (bf16[1,128,1536]{2,1,0:T(8,128)(2,1)S(1)}, bf16[1,128,1536]{2,1,0:T(8,128)(2,1)}, u32[]{:S(2)}) copy-start(bf16[1,128,1536]{2,1,0:T(8,128)(2,1)} %param.10) | copy-start | bytes 1179652
  7.2 8.9 %copy-start.6 = (s32[1,32,32]{2,1,0:T(8,128)S(1)}, s32[1,32,32]{2,1,0:T(8,128)}, u32[]{:S(2)}) copy-start(s32[1,32,32]{2,1,0:T(8,128)} %param.12) | copy-start | bytes 12292
  7.2 9.4 %copy-start.8 = (s32[1,5]{1,0:T(1,128)S(1)}, s32[1,5]{1,0:T(1,128)}, u32[]{:S(2)}) copy-start(s32[1,5]{1,0:T(1,128)} %param.13) | copy-start | bytes 64
  7.2 115.1 %all-gather.2.cloned.1.call-start = ((), (), s32[]{:S(2)}) async-start(), calls=%async_computation.6 | async-start | bytes 2506752 | tf_op jit(solution)/shard_map/all_gather | solution.py:272
  10.2 15.0 %all-to-all-start = ((bf16[8,3,128,128]{3,2,1,0:T(8,128)(2,1)}), bf16[8,3,128,128]{3,2,1,0:T(8,128)(2,1)S(1)}, u32[]{:S(2)}, u32[]{:S(2)}) async-start(bf16[8,3,128,128]{3,2,1,0:T(8,128)(2,1)} %pack.1), calls=%async_computation | async-start | bytes 1572864 | tf_op jit(solution)/shard_map/all_to_all | solution.py:46
  25.1 12.3 %copy-start.4 = (bf16[8,3,128,128]{3,2,1,0:T(8,128)(2,1)}, bf16[8,3,128,128]{3,2,1,0:T(8,128)(2,1)S(1)}, u32[]{:S(2)}) copy-start(bf16[8,3,128,128]{3,2,1,0:T(8,128)(2,1)S(1)} %all-to-all-done.input_ref) | copy-start | bytes 2359300
  25.2 12.3 %copy-start.5 = (bf16[8,2,128,128]{3,2,1,0:T(8,128)(2,1)}, bf16[8,2,128,128]{3,2,1,0:T(8,128)(2,1)S(1)}, u32[]{:S(2)}) copy-start(bf16[8,2,128,128]{3,2,1,0:T(8,128)(2,1)S(1)} %slice.21.own_ref) | copy-start | bytes 1572868
  25.2 12.3 %collective-permute-start = (bf16[8,2,128,128]{3,2,1,0:T(8,128)(2,1)S(1)}, bf16[8,2,128,128]{3,2,1,0:T(8,128)(2,1)S(1)}, u32[]{:S(2)}, u32[]{:S(2)}) collective-permute-start(bf16[8,2,128,128]{3,2,1,0:T(8,128)(2,1)S(1)} %slice.21.own_ref), channel_id=1, source_target_pairs={{0,16},{16,0},{32,48},{48,32},{64,80},{80,64},{96,112},{112,96},{1... | collective-permute-start | bytes 1572872 | tf_op jit(solution)/shard_map/ppermute | solution.py:37
  32.7 18.1 %all-to-all-start.1 = ((bf16[32,8,1536]{2,1,0:T(8,128)(2,1)}), bf16[32,8,1536]{2,1,0:T(8,128)(2,1)S(1)}, u32[]{:S(2)}, u32[]{:S(2)}) async-start(bf16[32,8,1536]{2,1,0:T(8,128)(2,1)} %bitcast.3), calls=%async_computation.1 | async-start | bytes 1572864 | tf_op jit(solution)/shard_map/all_to_all | solution.py:286
  37.5 0.8 copy-start.7
  53.6 62.0 %all-to-all-start.2 = ((bf16[8,128,1536]{2,1,0:T(8,128)(2,1)}), bf16[8,128,1536]{2,1,0:T(8,128)(2,1)S(1)}, u32[]{:S(2)}, u32[]{:S(2)}) async-start(bf16[8,128,1536]{2,1,0:T(8,128)(2,1)} %broadcast_in_dim.29), calls=%async_computation.2 | async-start | bytes 6291456 | tf_op jit(solution)/shard_map/all_to_all | solution.py:46
  57.2 47.3 %collective-permute-start.1 = (bf16[8,2,128,128]{3,2,1,0:T(8,128)(2,1)}, bf16[8,2,128,128]{3,2,1,0:T(8,128)(2,1)}, u32[]{:S(2)}, u32[]{:S(2)}) collective-permute-start(bf16[8,2,128,128]{3,2,1,0:T(8,128)(2,1)} %copy-done.5), channel_id=1, source_target_pairs={{0,64},{16,80},{32,96},{48,112},{64,0},{80,16},{96,32},{112,48},{1... | collective-permute-start | bytes 1572872 | tf_op jit(solution)/shard_map/ppermute | solution.py:37
  104.5 4.7 %collective-permute-start.2 = (bf16[8,2,128,128]{3,2,1,0:T(8,128)(2,1)}, bf16[8,2,128,128]{3,2,1,0:T(8,128)(2,1)}, u32[]{:S(2)}, u32[]{:S(2)}) collective-permute-start(bf16[8,2,128,128]{3,2,1,0:T(8,128)(2,1)} %collective-permute-done.1.own_ref.far_ref), channel_id=1, source_target_pairs={{0,16},{16,0},{32,48},{48,32},{64,80},{80,64},{96,112},{112,96},{1... | collective-permute-start | bytes 1572872 | tf_op jit(solution)/shard_map/ppermute | solution.py:37
  115.5 1.0 copy-start.3
  117.1 0.8 copy-start.1
  117.9 17.2 %all-to-all-start.3 = ((bf16[4,32,1536]{2,1,0:T(8,128)(2,1)}), bf16[4,32,1536]{2,1,0:T(8,128)(2,1)}, u32[]{:S(2)}, u32[]{:S(2)}) async-start(bf16[4,32,1536]{2,1,0:T(8,128)(2,1)} %copy-done.1), calls=%async_computation.3 | async-start | bytes 786432 | tf_op jit(solution)/shard_map/all_to_all | solution.py:351
  124.3 0.7 copy-start.2
  163.2 16.3 %collective-permute-start.4 = (f32[32,96]{1,0:T(8,128)S(1)}, f32[32,96]{1,0:T(8,128)S(1)}, u32[]{:S(2)}, u32[]{:S(2)}) collective-permute-start(f32[32,96]{1,0:T(8,128)S(1)} %broadcast_multiply_fusion), channel_id=1, source_target_pairs={{0,16},{64,32},{80,80},{48,96},{96,144},{128,160},{144,208},{208,2... | collective-permute-start | bytes 36872 | tf_op jit(solution)/shard_map/ppermute | solution.py:62
  164.5 15.0 %collective-permute-start.3 = (f32[32,96]{1,0:T(8,128)S(1)}, f32[32,96]{1,0:T(8,128)S(1)}, u32[]{:S(2)}, u32[]{:S(2)}) collective-permute-start(f32[32,96]{1,0:T(8,128)S(1)} %broadcast_multiply_fusion), channel_id=1, source_target_pairs={{0,0},{16,16},{64,48},{80,64},{32,80},{48,112},{96,128},{112,144},... | collective-permute-start | bytes 36872 | tf_op jit(solution)/shard_map/ppermute | solution.py:62
  165.2 14.3 %collective-permute-start.5 = (f32[32,96]{1,0:T(8,128)S(1)}, f32[32,96]{1,0:T(8,128)S(1)}, u32[]{:S(2)}, u32[]{:S(2)}) collective-permute-start(f32[32,96]{1,0:T(8,128)S(1)} %broadcast_multiply_fusion), channel_id=1, source_target_pairs={{16,32},{32,96},{112,160},{192,224},{176,288},{256,352},{336,416},... | collective-permute-start | bytes 36872 | tf_op jit(solution)/shard_map/ppermute | solution.py:62
  172.2 14.9 %all-to-all-start.5 = ((bf16[8,128,128]{2,1,0:T(8,128)(2,1)}), bf16[8,128,128]{2,1,0:T(8,128)(2,1)S(1)}, u32[]{:S(2)}, u32[]{:S(2)}) async-start(bf16[8,128,128]{2,1,0:T(8,128)(2,1)} %attend_grad.1), calls=%async_computation.5 | async-start | bytes 524288 | tf_op jit(solution)/shard_map/all_to_all | solution.py:46
Sparse Core Ops, SparseCore 0:
  10.1 71.0 all-gather.1

commit v6 on v5

--- a/solution.py
+++ b/solution.py
@@ -27,9 +27,13 @@
     return (y % SIDE * SIDE + x % SIDE) * CORES + core % CORES
 
 
-def send(value, dx=0, dcore=0):
+def column_of(side, step):
+    return step if side == 0 else SIDE - 1 - step
+
+
+def send(value, mirror=False, dcore=0):
     pairs = [
-        (seat(y, x, core), seat(y, x + dx, core + dcore))
+        (seat(y, x, core), seat(y, SIDE - 1 - x if mirror else x, core + dcore))
         for y in range(SIDE)
         for x in range(SIDE)
         for core in range(CORES)
@@ -39,7 +43,7 @@
 
 def trade(slots):
     groups = [
-        [seat(y, PAIR * side + x, core) for y in range(SIDE) for x in range(PAIR)]
+        [seat(y, column_of(side, step), core) for y in range(SIDE) for step in range(PAIR)]
         for side in range(PAIR)
         for core in range(CORES)
     ]
@@ -48,7 +52,7 @@
 
 def holders():
     return [
-        seat(head // PAIR, PAIR * side + head % PAIR, core)
+        seat(head // PAIR, column_of(side, head % PAIR), core)
         for head in range(SLOTS - PAIR)
         for side in range(PAIR)
         for core in range(CORES)
@@ -144,10 +148,13 @@
 
 
 def grad_kernel(
-    scale, input_ref, member_ref, hidden_ref, grad_ref, exact_ref, level_ref, own_ref, core_ref, far_ref, far_core_ref, out_ref
+    scale, blocks, input_ref, member_ref, hidden_ref, grad_ref, exact_ref, level_ref, own_ref, core_ref, far_ref, far_core_ref, *out_refs
 ):
+    out_ref = out_refs[-1]
+    for early_ref in out_refs[:-1]:
+        out_ref[pl.ds(0, early_ref.shape[0])] = early_ref[...]
     tiles = tiles_of([own_ref, core_ref, far_ref, far_core_ref])
-    for block in range(SLOTS // QUERY_SLOTS):
+    for block in blocks:
         slots = pl.ds(block * QUERY_SLOTS, QUERY_SLOTS)
         query = jnp.concatenate([rows_of(input_ref.at[slots, 0]), rows_of(member_ref.at[slots])], axis=1)
         level = rows_of(level_ref.at[slots])
@@ -289,7 +296,8 @@
     rank = jnp.arange(SLOTS, dtype=jnp.int32)
 
     def bases(which_side, which_core):
-        return (((rank // PAIR) * SIDE + which_side * PAIR + rank % PAIR) * CORES + which_core) * row_count
+        column = which_side * (SIDE - 1) + (1 - 2 * which_side) * (rank % PAIR)
+        return (((rank // PAIR) * SIDE + column) * CORES + which_core) * row_count
 
     key_bases = jnp.concatenate(
         [bases(side, core), bases(side, 1 - core), bases(1 - side, core), bases(1 - side, 1 - core)]
@@ -323,8 +331,8 @@
     ordered = unpack_rows(arrived, counts, me, row_count)
     copies = jnp.broadcast_to(ordered[None], (SLOTS,) + ordered.shape)
     late_own, copies, carry = lax.optimization_barrier((own, copies, carry))
-    far = send(late_own, dx=PAIR)
     group_rows = trade(copies)
+    far = send(late_own, mirror=True)
     far_beside = send(far, dcore=1)
     attended, exact, level = call(
         functools.partial(far_kernel, scale),
@@ -344,22 +352,35 @@
         outer_kernel, [((parts, share, feature_count), jnp.bfloat16)], "outer", 1e9
     )(attended, group_rows)
     partners = [
-        [seat(y, PAIR * side + x, at) for side in range(PAIR) for at in range(CORES)]
+        [seat(y, column_of(side, step), at) for side in range(PAIR) for at in range(CORES)]
         for y in range(SIDE)
-        for x in range(PAIR)
+        for step in range(PAIR)
     ]
     pieces = lax.all_to_all(partial_sum, "seq", 0, 0, axis_index_groups=partners, tiled=True)
 
-    slot = me // (SIDE * CORES) * PAIR + me // CORES % PAIR
+    slot = me // (SIDE * CORES) * PAIR + (me // CORES + side) % PAIR
     head_weight = lax.dynamic_slice_in_dim(weight, slot % head_count * HEAD_DIM, HEAD_DIM, axis=0)
     (head_grad,) = call(project_kernel, [narrow], "project", 1e9)(group_rows, head_weight)
-    (grad_query,) = call(functools.partial(grad_kernel, scale), [narrow], "attend_grad", 1e10, limit=56, blocks={0: only_query})(
-        inputs, member, hidden, head_grad, exact, level, own, beside, far, far_beside
-    )
-    pieces, grad_query = lax.optimization_barrier((pieces, grad_query))
+    block_count = SLOTS // QUERY_SLOTS
+
+    def backward(blocks, grad, *early):
+        shape = ((blocks[-1] + 1) * QUERY_SLOTS, row_count, HEAD_DIM)
+        return call(
+            functools.partial(grad_kernel, scale, blocks),
+            [(shape, jnp.bfloat16)],
+            "attend_grad",
+            5e9,
+            limit=56,
+            blocks={0: only_query},
+        )(inputs, member, hidden, grad, exact, level, own, beside, far, far_beside, *early)[0]
+
+    early = backward(range(block_count // 2), head_grad)
+    pieces, early = lax.optimization_barrier((pieces, early))
     (clip_parts,) = call(
         sum_kernel, [((clip_count, share, feature_count // clip_count), jnp.bfloat16)], "sum", 1e6
     )(pieces)
+    clip_parts, head_grad = lax.optimization_barrier((clip_parts, head_grad))
+    grad_query = backward(range(block_count // 2, block_count), head_grad, early)
     terms = lax.all_to_all(clip_parts, "dp", 0, 0, tiled=True)
     total = jnp.sum(terms.astype(jnp.float32), axis=0) / float(clip_count)
     total, grad_query = lax.optimization_barrier((total, grad_query))

time: 196 us -> 172 us (0.88)
  the two profiles are of different devices: /device:TPU:1 before, /device:TPU:6 now
where the time goes in v6:
time: 172 us; the launch traced here: 169 us
  starting transfers between devices  56 us (33%)
  waiting for transfers between devices  52.7 us (31%)
  Pallas kernels  31.4 us (18%)
  between operations  14.4 us (8%)
  local copies, waits for them, and re-layouts  9.63 us (6%)
  other arithmetic  5.22 us (3%)
    pallas_call x9, Pallas kernels, run(): pl.pallas_call(kernel, out_shape=[jax.ShapeDtypeStruct(shape, dtype) for...  31.4 us
    all_to_all x3, waiting for transfers between devices, trade(): lax.all_to_all(slots, 'seq', 0, 0, axis_index_groups=groups, tiled=True)  21.5 us
    all_to_all x1, starting transfers between devices, shards(): terms = lax.all_to_all(clip_parts, 'dp', 0, 0, tiled=True)  15.2 us
    ppermute x3, waiting for transfers between devices, send(): return lax.ppermute(value, 'seq', pairs)  15.2 us
    all_to_all x3, starting transfers between devices, trade(): lax.all_to_all(slots, 'seq', 0, 0, axis_index_groups=groups, tiled=True)  11.8 us
    ppermute x3, starting transfers between devices, send(): return lax.ppermute(value, 'seq', pairs)  8.77 us
    ppermute x3, starting transfers between devices, pass_on(): lax.ppermute(block, 'seq', [(held[3 * turn + take], 4 * turn + put) for t...  8.35 us
    all_to_all x1, waiting for transfers between devices, shards(): terms = lax.all_to_all(clip_parts, 'dp', 0, 0, tiled=True)  8.04 us
  transfers between devices with their start and end apart: 13, of which 8 were waited for; matrix products, arithmetic and copies ran while one was open for 7% of the time, Pallas kernels for 17%

profile of v6, /device:TPU:6, one launch (start us, length us, event | category | flops | bytes accessed | tf_op | source)
XLA Modules:
  0.0 169.4 jit_solution(18134027215866006314)
XLA Ops:
  7.2 0.7 all-gather.2.cloned.1.call-update
  7.9 2.2 %pack.1 = bf16[8,3,128,128]{3,2,1,0:T(8,128)(2,1)} custom-call(bf16[1,128,768]{2,1,0:T(8,128)(2,1)} %query_ref.1, bf16[1,128,768]{2,1,0:T(8,128)(2,1)} %key_ref.1, bf16[1,128,768]{2,1,0:T(8,128)(2,1)} %value_ref.1), custom_call_target="tpu_custom_call" | custom-call | flops 1000000 | bytes 1000000 | tf_op jit(solution)/shard_map/pack/pallas_call | solution.py:231
  10.2 4.7 %all-to-all-start = ((bf16[8,3,128,128]{3,2,1,0:T(8,128)(2,1)}), bf16[8,3,128,128]{3,2,1,0:T(8,128)(2,1)S(1)}, u32[]{:S(2)}, u32[]{:S(2)}) async-start(bf16[8,3,128,128]{3,2,1,0:T(8,128)(2,1)} %pack.1), calls=%async_computation | async-start | bytes 1572864 | tf_op jit(solution)/shard_map/all_to_all | solution.py:50
  14.9 0.2 dynamic-slice_reduce_fusion
  15.4 0.2 reduce-window.26
  15.6 0.1 copy.13
  15.7 0.1 reduce
  15.9 0.1 reshape.247
  16.1 0.1 reduce.1
  16.2 2.1 %gather_fusion = bf16[256,1536]{1,0:T(8,128)(2,1)} fusion(bf16[128,1536]{1,0:T(8,128)(2,1)S(1)} %bitcast.28, s32[1024]{0:T(1024)S(1)} %pad_clamp_fusion.1), kind=kCustom, calls=%fused_computation | custom fusion | bytes 1573888 | tf_op jit(solution)/shard_map/gather | solution.py:253
  18.4 0.1 convert_reduce_fusion.1
  18.5 2.7 %select_convert_fusion.hidden_ref = bf16[4096,128]{1,0:T(8,128)(2,1)} fusion(s32[128]{0:T(128)S(1)} %pad.8, s32[4096]{0:T(1024)S(1)} %add_bitcast_fusion), kind=kLoop, calls=%fused_computation.2 | loop fusion | flops 1572864 | bytes 1065472 | tf_op jit(solution)/shard_map/convert_element_type | solution.py:311
  21.2 6.7 %all-to-all-done.input_ref = bf16[8,3,128,128]{3,2,1,0:T(8,128)(2,1)S(1)} async-done(((bf16[8,3,128,128]{3,2,1,0:T(8,128)(2,1)}), bf16[8,3,128,128]{3,2,1,0:T(8,128)(2,1)S(1)}, u32[]{:S(2)}, u32[]{:S(2)}) %all-to-all-start) | async-done | bytes 786464 | tf_op jit(solution)/shard_map/all_to_all | solution.py:50
  27.9 1.9 %collective-permute-start = (bf16[8,2,128,128]{3,2,1,0:T(8,128)(2,1)S(1)}, bf16[8,2,128,128]{3,2,1,0:T(8,128)(2,1)S(1)}, u32[]{:S(2)}, u32[]{:S(2)}) collective-permute-start(bf16[8,2,128,128]{3,2,1,0:T(8,128)(2,1)S(1)} %slice.21.own_ref), channel_id=1, source_target_pairs={{0,16},{16,0},{32,48},{48,32},{64,80},{80,64},{96,112},{112,96},{1... | collective-permute-start | bytes 1572872 | tf_op jit(solution)/shard_map/ppermute | solution.py:41
  29.8 5.7 %all-to-all-start.1 = ((bf16[32,8,1536]{2,1,0:T(8,128)(2,1)}), bf16[32,8,1536]{2,1,0:T(8,128)(2,1)S(1)}, u32[]{:S(2)}, u32[]{:S(2)}) async-start(bf16[32,8,1536]{2,1,0:T(8,128)(2,1)} %bitcast.3), calls=%async_computation.1 | async-start | bytes 1572864 | tf_op jit(solution)/shard_map/all_to_all | solution.py:293
  35.5 0.9 and_convert_fusion.member_ref
  36.5 0.8 copy-done.7
  37.3 5.4 %near.1 = (f32[8,128,1]{2,1,0:T(8,128)}, f32[8,128,256]{2,1,0:T(8,128)}) custom-call(bf16[8,3,128,128]{3,2,1,0:T(8,128)(2,1)} %copy-done.4, bf16[8,128,128]{2,1,0:T(8,128)(2,1)} %and_convert_fusion.member_ref, bf16[4096,128]{1,0:T(8,128)(2,1)} %select_convert_fusion.hidden_ref, bf16[8,2,128,128]{3,2,1,0:T(8,128)(2,1)} %copy-done.5, ...), custom_call_target="tpu_custom_call" | custom-call | flops 4000000000 | bytes 1000000 | tf_op jit(solution)/shard_map/near/pallas_call | solution.py:231
  42.7 4.8 %all-to-all-done.1 = bf16[32,8,1536]{2,1,0:T(8,128)(2,1)S(1)} async-done(((bf16[32,8,1536]{2,1,0:T(8,128)(2,1)}), bf16[32,8,1536]{2,1,0:T(8,128)(2,1)S(1)}, u32[]{:S(2)}, u32[]{:S(2)}) %all-to-all-start.1) | async-done | bytes 786464 | tf_op jit(solution)/shard_map/all_to_all | solution.py:293
  47.5 0.9 gather_fusion.1
  48.4 1.9 %broadcast_in_dim.29 = bf16[8,128,1536]{2,1,0:T(8,128)(2,1)} broadcast(bf16[128,1536]{1,0:T(8,128)(2,1)S(1)} %gather_fusion.1), dimensions={1,2} | broadcast | bytes 3538944 | tf_op jit(solution)/shard_map/broadcast_in_dim | solution.py:332
  50.3 3.7 %all-to-all-start.2 = ((bf16[8,128,1536]{2,1,0:T(8,128)(2,1)}), bf16[8,128,1536]{2,1,0:T(8,128)(2,1)S(1)}, u32[]{:S(2)}, u32[]{:S(2)}) async-start(bf16[8,128,1536]{2,1,0:T(8,128)(2,1)} %broadcast_in_dim.29), calls=%async_computation.2 | async-start | bytes 6291456 | tf_op jit(solution)/shard_map/all_to_all | solution.py:50
  53.9 4.7 %collective-permute-start.1 = (bf16[8,2,128,128]{3,2,1,0:T(8,128)(2,1)}, bf16[8,2,128,128]{3,2,1,0:T(8,128)(2,1)}, u32[]{:S(2)}, u32[]{:S(2)}) collective-permute-start(bf16[8,2,128,128]{3,2,1,0:T(8,128)(2,1)} %copy-done.5), channel_id=1, source_target_pairs={{0,96},{16,112},{32,64},{48,80},{64,32},{80,48},{96,0},{112,16},{1... | collective-permute-start | bytes 1572872 | tf_op jit(solution)/shard_map/ppermute | solution.py:41
  58.6 13.3 %collective-permute-done.1.own_ref.far_ref = bf16[8,2,128,128]{3,2,1,0:T(8,128)(2,1)} collective-permute-done((bf16[8,2,128,128]{3,2,1,0:T(8,128)(2,1)}, bf16[8,2,128,128]{3,2,1,0:T(8,128)(2,1)}, u32[]{:S(2)}, u32[]{:S(2)}) %collective-permute-start.1) | collective-permute-done | bytes 524320 | tf_op jit(solution)/shard_map/ppermute | solution.py:41
  71.9 2.2 %collective-permute-start.2 = (bf16[8,2,128,128]{3,2,1,0:T(8,128)(2,1)}, bf16[8,2,128,128]{3,2,1,0:T(8,128)(2,1)}, u32[]{:S(2)}, u32[]{:S(2)}) collective-permute-start(bf16[8,2,128,128]{3,2,1,0:T(8,128)(2,1)} %collective-permute-done.1.own_ref.far_ref), channel_id=1, source_target_pairs={{0,16},{16,0},{32,48},{48,32},{64,80},{80,64},{96,112},{112,96},{1... | collective-permute-start | bytes 1572872 | tf_op jit(solution)/shard_map/ppermute | solution.py:41
  74.1 1.9 %collective-permute-done.2.core_ref.far_core_ref = bf16[8,2,128,128]{3,2,1,0:T(8,128)(2,1)} collective-permute-done((bf16[8,2,128,128]{3,2,1,0:T(8,128)(2,1)}, bf16[8,2,128,128]{3,2,1,0:T(8,128)(2,1)}, u32[]{:S(2)}, u32[]{:S(2)}) %collective-permute-start.2) | collective-permute-done | bytes 524320 | tf_op jit(solution)/shard_map/ppermute | solution.py:41
  76.0 6.4 %far.1 = (bf16[8,128,128]{2,1,0:T(8,128)(2,1)}, f32[8,128,128]{2,1,0:T(8,128)}, f32[8,128,128]{2,1,0:T(8,128)}) custom-call(bf16[8,3,128,128]{3,2,1,0:T(8,128)(2,1)} %copy-done.4, bf16[8,128,128]{2,1,0:T(8,128)(2,1)} %and_convert_fusion.member_ref, bf16[4096,128]{1,0:T(8,128)(2,1)} %select_convert_fusion.hidden_ref, ...), custom_call_target="tpu_custom_call" | custom-call | flops 4000000000 | bytes 1000000 | tf_op jit(solution)/shard_map/far/pallas_call | solution.py:231
  82.4 10.8 %all-to-all-done.2.rows_ref = bf16[8,128,1536]{2,1,0:T(8,128)(2,1)S(1)} async-done(((bf16[8,128,1536]{2,1,0:T(8,128)(2,1)}), bf16[8,128,1536]{2,1,0:T(8,128)(2,1)S(1)}, u32[]{:S(2)}, u32[]{:S(2)}) %all-to-all-start.2) | async-done | bytes 3145760 | tf_op jit(solution)/shard_map/all_to_all | solution.py:50
  93.3 0.9 copy-done.3
  94.2 0.6 outer.1
  94.8 0.7 copy-done.1
  95.6 6.1 %all-to-all-start.3 = ((bf16[4,32,1536]{2,1,0:T(8,128)(2,1)}), bf16[4,32,1536]{2,1,0:T(8,128)(2,1)}, u32[]{:S(2)}, u32[]{:S(2)}) async-start(bf16[4,32,1536]{2,1,0:T(8,128)(2,1)} %copy-done.1), calls=%async_computation.3 | async-start | bytes 786432 | tf_op jit(solution)/shard_map/all_to_all | solution.py:359
  101.7 1.0 constant_dynamic-slice_fusion.weight_ref
  102.7 1.0 project.1.grad_ref
  103.7 0.7 copy-done.2
  104.4 6.6 %attend_grad.2.out_refs_0_ = bf16[4,128,128]{2,1,0:T(8,128)(2,1)} custom-call(bf16[8,3,128,128]{3,2,1,0:T(8,128)(2,1)} %copy-done.4, bf16[8,128,128]{2,1,0:T(8,128)(2,1)} %and_convert_fusion.member_ref, bf16[4096,128]{1,0:T(8,128)(2,1)} %select_convert_fusion.hidden_ref, bf16[8,128,128]{2,1,0:T(8,128)(2,1)} %copy-done.2, ...), custom_call_target="tpu_custom_call" | custom-call | flops 5000000000 | bytes 1000000 | tf_op jit(solution)/shard_map/attend_grad/pallas_call | solution.py:231
  111.0 1.8 %sum.1 = bf16[16,32,96]{2,1,0:T(8,128)(2,1)} custom-call(bf16[4,32,1536]{2,1,0:T(8,128)(2,1)} %all-to-all-done.3.pieces_ref), custom_call_target="tpu_custom_call" | custom-call | flops 1000000 | bytes 1000000 | tf_op jit(solution)/shard_map/sum/pallas_call | solution.py:231
  112.8 15.2 %all-to-all-start.4 = ((bf16[16,32,96]{2,1,0:T(8,128)(2,1)}), bf16[16,32,96]{2,1,0:T(8,128)(2,1)S(1)}, u32[]{:S(2)}, u32[]{:S(2)}) async-start(bf16[16,32,96]{2,1,0:T(8,128)(2,1)} %sum.1), calls=%async_computation.4 | async-start | bytes 262144 | tf_op jit(solution)/shard_map/all_to_all | solution.py:384
  128.0 6.7 %attend_grad.3 = bf16[8,128,128]{2,1,0:T(8,128)(2,1)} custom-call(bf16[8,3,128,128]{3,2,1,0:T(8,128)(2,1)} %copy-done.4, bf16[8,128,128]{2,1,0:T(8,128)(2,1)} %and_convert_fusion.member_ref, bf16[4096,128]{1,0:T(8,128)(2,1)} %select_convert_fusion.hidden_ref, bf16[8,128,128]{2,1,0:T(8,128)(2,1)} %copy-done.2, f32[8,128,128]{2,1,0:T(8,128)} %get-tuple-element.28.exact_ref, ...), custom_call_target="tpu_custom_call" | custom-call | flops 5000000000 | bytes 1000000 | tf_op jit(solution)/shard_map/attend_grad/pallas_call | solution.py:231
  134.7 8.0 %all-to-all-done.4 = bf16[16,32,96]{2,1,0:T(8,128)(2,1)S(1)} async-done(((bf16[16,32,96]{2,1,0:T(8,128)(2,1)}), bf16[16,32,96]{2,1,0:T(8,128)(2,1)S(1)}, u32[]{:S(2)}, u32[]{:S(2)}) %all-to-all-start.4) | async-done | bytes 98336 | tf_op jit(solution)/shard_map/all_to_all | solution.py:384
  142.8 2.5 %collective-permute-start.4 = (f32[32,96]{1,0:T(8,128)S(1)}, f32[32,96]{1,0:T(8,128)S(1)}, u32[]{:S(2)}, u32[]{:S(2)}) collective-permute-start(f32[32,96]{1,0:T(8,128)S(1)} %broadcast_multiply_fusion), channel_id=1, source_target_pairs={{0,16},{96,32},{112,80},{48,96},{64,144},{128,160},{144,208},{240,... | collective-permute-start | bytes 36872 | tf_op jit(solution)/shard_map/ppermute | solution.py:66
  145.2 4.6 %collective-permute-start.3 = (f32[32,96]{1,0:T(8,128)S(1)}, f32[32,96]{1,0:T(8,128)S(1)}, u32[]{:S(2)}, u32[]{:S(2)}) collective-permute-start(f32[32,96]{1,0:T(8,128)S(1)} %broadcast_multiply_fusion), channel_id=1, source_target_pairs={{0,0},{16,16},{96,48},{112,64},{32,80},{48,112},{64,128},{80,144},... | collective-permute-start | bytes 36872 | tf_op jit(solution)/shard_map/ppermute | solution.py:66
  149.9 1.3 collective-permute-start.5
  151.2 3.4 %all-to-all-start.5 = ((bf16[8,128,128]{2,1,0:T(8,128)(2,1)}), bf16[8,128,128]{2,1,0:T(8,128)(2,1)S(1)}, u32[]{:S(2)}, u32[]{:S(2)}) async-start(bf16[8,128,128]{2,1,0:T(8,128)(2,1)} %attend_grad.3), calls=%async_computation.5 | async-start | bytes 524288 | tf_op jit(solution)/shard_map/all_to_all | solution.py:50
  154.6 2.5 %collective-permute-done.5 = f32[32,96]{1,0:T(8,128)S(1)} collective-permute-done((f32[32,96]{1,0:T(8,128)S(1)}, f32[32,96]{1,0:T(8,128)S(1)}, u32[]{:S(2)}, u32[]{:S(2)}) %collective-permute-start.5) | collective-permute-done | bytes 12320 | tf_op jit(solution)/shard_map/ppermute | solution.py:66
  157.2 0.6 fusion
  157.8 4.0 %all-to-all-done.5.slots_ref = bf16[8,128,128]{2,1,0:T(8,128)(2,1)S(1)} async-done(((bf16[8,128,128]{2,1,0:T(8,128)(2,1)}), bf16[8,128,128]{2,1,0:T(8,128)(2,1)S(1)}, u32[]{:S(2)}, u32[]{:S(2)}) %all-to-all-start.5) | async-done | bytes 262176 | tf_op jit(solution)/shard_map/all_to_all | solution.py:50
  161.8 0.7 join.1
  (42 shorter events, 0.7 us)
Async XLA Ops:
  7.2 9.1 %copy-start = (bf16[1,128,1536]{2,1,0:T(8,128)(2,1)S(1)}, bf16[1,128,1536]{2,1,0:T(8,128)(2,1)}, u32[]{:S(2)}) copy-start(bf16[1,128,1536]{2,1,0:T(8,128)(2,1)} %param.10) | copy-start | bytes 1179652
  7.2 7.7 %copy-start.6 = (s32[1,32,32]{2,1,0:T(8,128)S(1)}, s32[1,32,32]{2,1,0:T(8,128)}, u32[]{:S(2)}) copy-start(s32[1,32,32]{2,1,0:T(8,128)} %param.12) | copy-start | bytes 12292
  7.2 8.2 %copy-start.8 = (s32[1,5]{1,0:T(1,128)S(1)}, s32[1,5]{1,0:T(1,128)}, u32[]{:S(2)}) copy-start(s32[1,5]{1,0:T(1,128)} %param.13) | copy-start | bytes 64
  7.2 94.5 %all-gather.2.cloned.1.call-start = ((), (), s32[]{:S(2)}) async-start(), calls=%async_computation.6 | async-start | bytes 2506752 | tf_op jit(solution)/shard_map/all_gather | solution.py:279
  10.2 17.6 %all-to-all-start = ((bf16[8,3,128,128]{3,2,1,0:T(8,128)(2,1)}), bf16[8,3,128,128]{3,2,1,0:T(8,128)(2,1)S(1)}, u32[]{:S(2)}, u32[]{:S(2)}) async-start(bf16[8,3,128,128]{3,2,1,0:T(8,128)(2,1)} %pack.1), calls=%async_computation | async-start | bytes 1572864 | tf_op jit(solution)/shard_map/all_to_all | solution.py:50
  27.8 8.6 %copy-start.4 = (bf16[8,3,128,128]{3,2,1,0:T(8,128)(2,1)}, bf16[8,3,128,128]{3,2,1,0:T(8,128)(2,1)S(1)}, u32[]{:S(2)}) copy-start(bf16[8,3,128,128]{3,2,1,0:T(8,128)(2,1)S(1)} %all-to-all-done.input_ref) | copy-start | bytes 2359300
  27.9 8.6 %copy-start.5 = (bf16[8,2,128,128]{3,2,1,0:T(8,128)(2,1)}, bf16[8,2,128,128]{3,2,1,0:T(8,128)(2,1)S(1)}, u32[]{:S(2)}) copy-start(bf16[8,2,128,128]{3,2,1,0:T(8,128)(2,1)S(1)} %slice.21.own_ref) | copy-start | bytes 1572868
  27.9 8.6 %collective-permute-start = (bf16[8,2,128,128]{3,2,1,0:T(8,128)(2,1)S(1)}, bf16[8,2,128,128]{3,2,1,0:T(8,128)(2,1)S(1)}, u32[]{:S(2)}, u32[]{:S(2)}) collective-permute-start(bf16[8,2,128,128]{3,2,1,0:T(8,128)(2,1)S(1)} %slice.21.own_ref), channel_id=1, source_target_pairs={{0,16},{16,0},{32,48},{48,32},{64,80},{80,64},{96,112},{112,96},{1... | collective-permute-start | bytes 1572872 | tf_op jit(solution)/shard_map/ppermute | solution.py:41
  29.8 17.7 %all-to-all-start.1 = ((bf16[32,8,1536]{2,1,0:T(8,128)(2,1)}), bf16[32,8,1536]{2,1,0:T(8,128)(2,1)S(1)}, u32[]{:S(2)}, u32[]{:S(2)}) async-start(bf16[32,8,1536]{2,1,0:T(8,128)(2,1)} %bitcast.3), calls=%async_computation.1 | async-start | bytes 1572864 | tf_op jit(solution)/shard_map/all_to_all | solution.py:293
  36.4 0.9 copy-start.7
  50.3 43.0 %all-to-all-start.2 = ((bf16[8,128,1536]{2,1,0:T(8,128)(2,1)}), bf16[8,128,1536]{2,1,0:T(8,128)(2,1)S(1)}, u32[]{:S(2)}, u32[]{:S(2)}) async-start(bf16[8,128,1536]{2,1,0:T(8,128)(2,1)} %broadcast_in_dim.29), calls=%async_computation.2 | async-start | bytes 6291456 | tf_op jit(solution)/shard_map/all_to_all | solution.py:50
  53.9 18.0 %collective-permute-start.1 = (bf16[8,2,128,128]{3,2,1,0:T(8,128)(2,1)}, bf16[8,2,128,128]{3,2,1,0:T(8,128)(2,1)}, u32[]{:S(2)}, u32[]{:S(2)}) collective-permute-start(bf16[8,2,128,128]{3,2,1,0:T(8,128)(2,1)} %copy-done.5), channel_id=1, source_target_pairs={{0,96},{16,112},{32,64},{48,80},{64,32},{80,48},{96,0},{112,16},{1... | collective-permute-start | bytes 1572872 | tf_op jit(solution)/shard_map/ppermute | solution.py:41
  71.9 4.1 %collective-permute-start.2 = (bf16[8,2,128,128]{3,2,1,0:T(8,128)(2,1)}, bf16[8,2,128,128]{3,2,1,0:T(8,128)(2,1)}, u32[]{:S(2)}, u32[]{:S(2)}) collective-permute-start(bf16[8,2,128,128]{3,2,1,0:T(8,128)(2,1)} %collective-permute-done.1.own_ref.far_ref), channel_id=1, source_target_pairs={{0,16},{16,0},{32,48},{48,32},{64,80},{80,64},{96,112},{112,96},{1... | collective-permute-start | bytes 1572872 | tf_op jit(solution)/shard_map/ppermute | solution.py:41
  93.3 1.0 copy-start.3
  94.8 0.8 copy-start.1
  95.6 15.4 %all-to-all-start.3 = ((bf16[4,32,1536]{2,1,0:T(8,128)(2,1)}), bf16[4,32,1536]{2,1,0:T(8,128)(2,1)}, u32[]{:S(2)}, u32[]{:S(2)}) async-start(bf16[4,32,1536]{2,1,0:T(8,128)(2,1)} %copy-done.1), calls=%async_computation.3 | async-start | bytes 786432 | tf_op jit(solution)/shard_map/all_to_all | solution.py:359
  103.7 0.7 copy-start.2
  112.8 29.9 %all-to-all-start.4 = ((bf16[16,32,96]{2,1,0:T(8,128)(2,1)}), bf16[16,32,96]{2,1,0:T(8,128)(2,1)S(1)}, u32[]{:S(2)}, u32[]{:S(2)}) async-start(bf16[16,32,96]{2,1,0:T(8,128)(2,1)} %sum.1), calls=%async_computation.4 | async-start | bytes 262144 | tf_op jit(solution)/shard_map/all_to_all | solution.py:384
  142.8 11.8 %collective-permute-start.4 = (f32[32,96]{1,0:T(8,128)S(1)}, f32[32,96]{1,0:T(8,128)S(1)}, u32[]{:S(2)}, u32[]{:S(2)}) collective-permute-start(f32[32,96]{1,0:T(8,128)S(1)} %broadcast_multiply_fusion), channel_id=1, source_target_pairs={{0,16},{96,32},{112,80},{48,96},{64,144},{128,160},{144,208},{240,... | collective-permute-start | bytes 36872 | tf_op jit(solution)/shard_map/ppermute | solution.py:66
  145.2 9.4 %collective-permute-start.3 = (f32[32,96]{1,0:T(8,128)S(1)}, f32[32,96]{1,0:T(8,128)S(1)}, u32[]{:S(2)}, u32[]{:S(2)}) collective-permute-start(f32[32,96]{1,0:T(8,128)S(1)} %broadcast_multiply_fusion), channel_id=1, source_target_pairs={{0,0},{16,16},{96,48},{112,64},{32,80},{48,112},{64,128},{80,144},... | collective-permute-start | bytes 36872 | tf_op jit(solution)/shard_map/ppermute | solution.py:66
  149.9 7.3 %collective-permute-start.5 = (f32[32,96]{1,0:T(8,128)S(1)}, f32[32,96]{1,0:T(8,128)S(1)}, u32[]{:S(2)}, u32[]{:S(2)}) collective-permute-start(f32[32,96]{1,0:T(8,128)S(1)} %broadcast_multiply_fusion), channel_id=1, source_target_pairs={{16,32},{32,96},{80,160},{224,224},{176,288},{256,352},{368,416},{... | collective-permute-start | bytes 36872 | tf_op jit(solution)/shard_map/ppermute | solution.py:66
  151.2 10.6 %all-to-all-start.5 = ((bf16[8,128,128]{2,1,0:T(8,128)(2,1)}), bf16[8,128,128]{2,1,0:T(8,128)(2,1)S(1)}, u32[]{:S(2)}, u32[]{:S(2)}) async-start(bf16[8,128,128]{2,1,0:T(8,128)(2,1)} %attend_grad.3), calls=%async_computation.5 | async-start | bytes 524288 | tf_op jit(solution)/shard_map/all_to_all | solution.py:50
Sparse Core Ops, SparseCore 0:
  10.1 78.7 all-gather.1

commit v7 on v6

--- a/solution.py
+++ b/solution.py
@@ -180,14 +180,17 @@
         )
 
 
-def outer_kernel(attended_ref, rows_ref, out_ref):
-    parts, share, feature_count = out_ref.shape
+def outer_kernel(order_ref, attended_ref, rows_ref, *refs):
+    out_refs, held_ref = refs[:-1], refs[-1]
+    parts, share, feature_count = held_ref.shape
     attended = attended_ref[...].reshape(-1, HEAD_DIM)
     for first in range(0, feature_count, 4 * HEAD_DIM):
         columns = pl.ds(first, 4 * HEAD_DIM)
         rows = rows_ref[:, :, columns].reshape(attended.shape[0], -1)
         term = lax.dot_general(attended, rows, TN, preferred_element_type=jnp.float32).astype(jnp.bfloat16)
-        out_ref[:, :, columns] = term.reshape(parts, share, -1)
+        held_ref[:, :, columns] = term.reshape(parts, share, -1)
+    for place, out_ref in enumerate(out_refs):
+        out_ref[...] = held_ref[order_ref[place]]
 
 
 def pack_kernel(head_count, query_ref, key_ref, value_ref, out_ref, sems):
@@ -209,10 +212,11 @@
         out_ref[0, :, pl.ds(head * HEAD_DIM, HEAD_DIM)] = slots_ref[head]
 
 
-def sum_kernel(pieces_ref, out_ref):
-    total = pieces_ref[0].astype(jnp.float32)
-    for piece in range(1, pieces_ref.shape[0]):
-        total = total + pieces_ref[piece].astype(jnp.float32)
+def sum_kernel(*refs):
+    piece_refs, out_ref = refs[:-1], refs[-1]
+    total = piece_refs[0][...].astype(jnp.float32)
+    for piece_ref in piece_refs[1:]:
+        total = total + piece_ref[...].astype(jnp.float32)
     width = out_ref.shape[2]
     for clip in range(out_ref.shape[0]):
         out_ref[clip] = total[:, clip * width : (clip + 1) * width].astype(jnp.bfloat16)
@@ -348,15 +352,19 @@
     feature_count = ordered.shape[1]
     parts = PAIR * CORES
     share = HEAD_DIM // parts
-    (partial_sum,) = call(
-        outer_kernel, [((parts, share, feature_count), jnp.bfloat16)], "outer", 1e9
-    )(attended, group_rows)
-    partners = [
-        [seat(y, column_of(side, step), at) for side in range(PAIR) for at in range(CORES)]
-        for y in range(SIDE)
-        for step in range(PAIR)
-    ]
-    pieces = lax.all_to_all(partial_sum, "seq", 0, 0, axis_index_groups=partners, tiled=True)
+    member_at = side * CORES + core
+    order = jnp.stack([member_at ^ step for step in range(parts)])
+    pieces = call(
+        outer_kernel,
+        [((share, feature_count), jnp.bfloat16)] * parts,
+        "outer",
+        1e9,
+        scalars=1,
+        scratch_shapes=[pltpu.VMEM((parts, share, feature_count), jnp.bfloat16)],
+    )(order, attended, group_rows)
+    pieces = [pieces[0]] + [
+        send(pieces[step], mirror=step >= CORES, dcore=step % CORES) for step in range(1, parts)
+    ]
 
     slot = me // (SIDE * CORES) * PAIR + (me // CORES + side) % PAIR
     head_weight = lax.dynamic_slice_in_dim(weight, slot % head_count * HEAD_DIM, HEAD_DIM, axis=0)
@@ -374,18 +382,17 @@
             blocks={0: only_query},
         )(inputs, member, hidden, grad, exact, level, own, beside, far, far_beside, *early)[0]
 
-    early = backward(range(block_count // 2), head_grad)
-    pieces, early = lax.optimization_barrier((pieces, early))
+    *pieces, head_grad = lax.optimization_barrier((*pieces, head_grad))
     (clip_parts,) = call(
         sum_kernel, [((clip_count, share, feature_count // clip_count), jnp.bfloat16)], "sum", 1e6
-    )(pieces)
+    )(*pieces)
     clip_parts, head_grad = lax.optimization_barrier((clip_parts, head_grad))
-    grad_query = backward(range(block_count // 2, block_count), head_grad, early)
+    grad_query = backward(range(block_count), head_grad)
     terms = lax.all_to_all(clip_parts, "dp", 0, 0, tiled=True)
+    terms, grad_query = lax.optimization_barrier((terms, grad_query))
     total = jnp.sum(terms.astype(jnp.float32), axis=0) / float(clip_count)
-    total, grad_query = lax.optimization_barrier((total, grad_query))
+    grad_query = trade(grad_query)
     total = place_blocks(total, me)
-    grad_query = trade(grad_query)
     (grad_query_rows,) = call(
         functools.partial(join_kernel, head_count), [((1, row_count, head_width), jnp.bfloat16)], "join", 1e6
     )(grad_query)

time: 172 us -> 169 us (0.983)
  waiting for transfers between devices: 52.7 us -> 49.5 us
  starting transfers between devices: 56 us -> 58.1 us
  Pallas kernels: 31.4 us -> 29.5 us
    ppermute x3 -> x6, starting transfers between devices: 8.77 us -> 17.8 us  [send(): return lax.ppermute(value, 'seq', pairs)]
    all_to_all x1 -> x0, starting transfers between devices: 6.1 us -> none  [shards(): lax.all_to_all(partial_sum, 'seq', 0, 0, axis_index_groups=partners, tile...]
    all_to_all x1, waiting for transfers between devices: 8.04 us -> 4.65 us  [shards(): terms = lax.all_to_all(clip_parts, 'dp', 0, 0, tiled=True)]
    ppermute x3 -> x6, waiting for transfers between devices: 15.2 us -> 18.3 us  [send(): return lax.ppermute(value, 'seq', pairs)]
    all_to_all x1, waiting for transfers between devices: 4.76 us -> 1.88 us  [shards(): arrived = lax.all_to_all(packed, 'seq', 0, 0, tiled=True)]
    ppermute x3, waiting for transfers between devices: 2.53 us -> 0.01 us  [pass_on(): lax.ppermute(block, 'seq', [(held[3 * turn + take], 4 * turn + put) for t...]
    all_to_all x3, waiting for transfers between devices: 21.5 us -> 24 us  [trade(): lax.all_to_all(slots, 'seq', 0, 0, axis_index_groups=groups, tiled=True)]
    pallas_call x9 -> x8, Pallas kernels: 31.4 us -> 29.5 us  [run(): pl.pallas_call(kernel, out_shape=[jax.ShapeDtypeStruct(shape, dtype) for...]
  transfers between devices with their start and end apart: 13 -> 15, of which waited for: 8 -> 9; matrix products, arithmetic and copies ran while one was open for 7% -> 7% of each run, Pallas kernels for 17% -> 16%
where the time goes in v7:
time: 169 us; the launch traced here: 166 us
  starting transfers between devices  58.1 us (34%)
  waiting for transfers between devices  49.5 us (29%)
  Pallas kernels  29.5 us (17%)
  between operations  14.4 us (9%)
  local copies, waits for them, and re-layouts  9.54 us (6%)
  other arithmetic  5.28 us (3%)
    pallas_call x8, Pallas kernels, run(): pl.pallas_call(kernel, out_shape=[jax.ShapeDtypeStruct(shape, dtype) for...  29.5 us
    all_to_all x3, waiting for transfers between devices, trade(): lax.all_to_all(slots, 'seq', 0, 0, axis_index_groups=groups, tiled=True)  24 us
    ppermute x6, waiting for transfers between devices, send(): return lax.ppermute(value, 'seq', pairs)  18.3 us
    ppermute x6, starting transfers between devices, send(): return lax.ppermute(value, 'seq', pairs)  17.8 us
    all_to_all x1, starting transfers between devices, shards(): terms = lax.all_to_all(clip_parts, 'dp', 0, 0, tiled=True)  15.2 us
    all_to_all x3, starting transfers between devices, trade(): lax.all_to_all(slots, 'seq', 0, 0, axis_index_groups=groups, tiled=True)  11.8 us
    ppermute x3, starting transfers between devices, pass_on(): lax.ppermute(block, 'seq', [(held[3 * turn + take], 4 * turn + put) for t...  7.72 us
    all_to_all x1, starting transfers between devices, shards(): arrived = lax.all_to_all(packed, 'seq', 0, 0, tiled=True)  5.57 us
  transfers between devices with their start and end apart: 15, of which 9 were waited for; matrix products, arithmetic and copies ran while one was open for 7% of the time, Pallas kernels for 16%

profile of v7, /device:TPU:6, one launch (start us, length us, event | category | flops | bytes accessed | tf_op | source)
XLA Modules:
  0.0 166.4 jit_solution(6407537524806917826)
XLA Ops:
  7.2 0.7 all-gather.2.cloned.1.call-update
  7.9 2.2 %pack.1 = bf16[8,3,128,128]{3,2,1,0:T(8,128)(2,1)} custom-call(bf16[1,128,768]{2,1,0:T(8,128)(2,1)} %query_ref.1, bf16[1,128,768]{2,1,0:T(8,128)(2,1)} %key_ref.1, bf16[1,128,768]{2,1,0:T(8,128)(2,1)} %value_ref.1), custom_call_target="tpu_custom_call" | custom-call | flops 1000000 | bytes 1000000 | tf_op jit(solution)/shard_map/pack/pallas_call | solution.py:235
  10.2 4.7 %all-to-all-start = ((bf16[8,3,128,128]{3,2,1,0:T(8,128)(2,1)}), bf16[8,3,128,128]{3,2,1,0:T(8,128)(2,1)S(1)}, u32[]{:S(2)}, u32[]{:S(2)}) async-start(bf16[8,3,128,128]{3,2,1,0:T(8,128)(2,1)} %pack.1), calls=%async_computation | async-start | bytes 1572864 | tf_op jit(solution)/shard_map/all_to_all | solution.py:50
  15.0 0.2 dynamic-slice_reduce_fusion
  15.2 0.2 reduce-window.26
  15.6 0.1 reduce
  16.1 0.1 reduce.1
  16.2 0.1 convert_reduce_fusion.1
  16.3 2.2 %gather_fusion = bf16[256,1536]{1,0:T(8,128)(2,1)} fusion(bf16[128,1536]{1,0:T(8,128)(2,1)S(1)} %bitcast.32, s32[1024]{0:T(1024)S(1)} %pad_clamp_fusion.1), kind=kCustom, calls=%fused_computation | custom fusion | bytes 1573888 | tf_op jit(solution)/shard_map/gather | solution.py:257
  18.5 2.7 %select_convert_fusion.hidden_ref = bf16[4096,128]{1,0:T(8,128)(2,1)} fusion(s32[128]{0:T(128)S(1)} %pad.8, s32[4096]{0:T(1024)S(1)} %add_bitcast_fusion), kind=kLoop, calls=%fused_computation.2 | loop fusion | flops 1572864 | bytes 1065472 | tf_op jit(solution)/shard_map/convert_element_type | solution.py:315
  21.2 6.7 %all-to-all-done.input_ref = bf16[8,3,128,128]{3,2,1,0:T(8,128)(2,1)S(1)} async-done(((bf16[8,3,128,128]{3,2,1,0:T(8,128)(2,1)}), bf16[8,3,128,128]{3,2,1,0:T(8,128)(2,1)S(1)}, u32[]{:S(2)}, u32[]{:S(2)}) %all-to-all-start) | async-done | bytes 786464 | tf_op jit(solution)/shard_map/all_to_all | solution.py:50
  27.8 5.6 %all-to-all-start.1 = ((bf16[32,8,1536]{2,1,0:T(8,128)(2,1)}), bf16[32,8,1536]{2,1,0:T(8,128)(2,1)S(1)}, u32[]{:S(2)}, u32[]{:S(2)}) async-start(bf16[32,8,1536]{2,1,0:T(8,128)(2,1)} %bitcast.7), calls=%async_computation.1 | async-start | bytes 1572864 | tf_op jit(solution)/shard_map/all_to_all | solution.py:297
  33.4 2.1 %collective-permute-start = (bf16[8,2,128,128]{3,2,1,0:T(8,128)(2,1)S(1)}, bf16[8,2,128,128]{3,2,1,0:T(8,128)(2,1)S(1)}, u32[]{:S(2)}, u32[]{:S(2)}) collective-permute-start(bf16[8,2,128,128]{3,2,1,0:T(8,128)(2,1)S(1)} %slice.21.own_ref), channel_id=1, source_target_pairs={{0,16},{16,0},{32,48},{48,32},{64,80},{80,64},{96,112},{112,96},{1... | collective-permute-start | bytes 1572872 | tf_op jit(solution)/shard_map/ppermute | solution.py:41
  35.6 0.9 and_convert_fusion.member_ref
  36.5 0.8 collective-permute-done.core_ref
  37.3 0.8 copy-done.8
  38.1 5.4 %near.1 = (f32[8,128,1]{2,1,0:T(8,128)}, f32[8,128,256]{2,1,0:T(8,128)}) custom-call(bf16[8,3,128,128]{3,2,1,0:T(8,128)(2,1)} %copy-done.5, bf16[8,128,128]{2,1,0:T(8,128)(2,1)} %and_convert_fusion.member_ref, bf16[4096,128]{1,0:T(8,128)(2,1)} %select_convert_fusion.hidden_ref, bf16[8,2,128,128]{3,2,1,0:T(8,128)(2,1)} %copy-done.6, ...), custom_call_target="tpu_custom_call" | custom-call | flops 4000000000 | bytes 1000000 | tf_op jit(solution)/shard_map/near/pallas_call | solution.py:235
  43.5 1.9 %all-to-all-done.1 = bf16[32,8,1536]{2,1,0:T(8,128)(2,1)S(1)} async-done(((bf16[32,8,1536]{2,1,0:T(8,128)(2,1)}), bf16[32,8,1536]{2,1,0:T(8,128)(2,1)S(1)}, u32[]{:S(2)}, u32[]{:S(2)}) %all-to-all-start.1) | async-done | bytes 786464 | tf_op jit(solution)/shard_map/all_to_all | solution.py:297
  45.4 0.9 gather_fusion.1
  46.3 1.9 %broadcast_in_dim.29 = bf16[8,128,1536]{2,1,0:T(8,128)(2,1)} broadcast(bf16[128,1536]{1,0:T(8,128)(2,1)S(1)} %gather_fusion.1), dimensions={1,2} | broadcast | bytes 3538944 | tf_op jit(solution)/shard_map/broadcast_in_dim | solution.py:336
  48.2 3.6 %all-to-all-start.2 = ((bf16[8,128,1536]{2,1,0:T(8,128)(2,1)}), bf16[8,128,1536]{2,1,0:T(8,128)(2,1)S(1)}, u32[]{:S(2)}, u32[]{:S(2)}) async-start(bf16[8,128,1536]{2,1,0:T(8,128)(2,1)} %broadcast_in_dim.29), calls=%async_computation.2 | async-start | bytes 6291456 | tf_op jit(solution)/shard_map/all_to_all | solution.py:50
  51.8 4.7 %collective-permute-start.1 = (bf16[8,2,128,128]{3,2,1,0:T(8,128)(2,1)}, bf16[8,2,128,128]{3,2,1,0:T(8,128)(2,1)}, u32[]{:S(2)}, u32[]{:S(2)}) collective-permute-start(bf16[8,2,128,128]{3,2,1,0:T(8,128)(2,1)} %copy-done.6), channel_id=1, source_target_pairs={{0,96},{16,112},{32,64},{48,80},{64,32},{80,48},{96,0},{112,16},{1... | collective-permute-start | bytes 1572872 | tf_op jit(solution)/shard_map/ppermute | solution.py:41
  56.6 13.3 %collective-permute-done.1.own_ref.far_ref = bf16[8,2,128,128]{3,2,1,0:T(8,128)(2,1)} collective-permute-done((bf16[8,2,128,128]{3,2,1,0:T(8,128)(2,1)}, bf16[8,2,128,128]{3,2,1,0:T(8,128)(2,1)}, u32[]{:S(2)}, u32[]{:S(2)}) %collective-permute-start.1) | collective-permute-done | bytes 524320 | tf_op jit(solution)/shard_map/ppermute | solution.py:41
  69.8 2.3 %collective-permute-start.2 = (bf16[8,2,128,128]{3,2,1,0:T(8,128)(2,1)}, bf16[8,2,128,128]{3,2,1,0:T(8,128)(2,1)}, u32[]{:S(2)}, u32[]{:S(2)}) collective-permute-start(bf16[8,2,128,128]{3,2,1,0:T(8,128)(2,1)} %collective-permute-done.1.own_ref.far_ref), channel_id=1, source_target_pairs={{0,16},{16,0},{32,48},{48,32},{64,80},{80,64},{96,112},{112,96},{1... | collective-permute-start | bytes 1572872 | tf_op jit(solution)/shard_map/ppermute | solution.py:41
  72.2 1.7 %collective-permute-done.2.core_ref.far_core_ref = bf16[8,2,128,128]{3,2,1,0:T(8,128)(2,1)} collective-permute-done((bf16[8,2,128,128]{3,2,1,0:T(8,128)(2,1)}, bf16[8,2,128,128]{3,2,1,0:T(8,128)(2,1)}, u32[]{:S(2)}, u32[]{:S(2)}) %collective-permute-start.2) | collective-permute-done | bytes 524320 | tf_op jit(solution)/shard_map/ppermute | solution.py:41
  74.0 6.4 %far.1 = (bf16[8,128,128]{2,1,0:T(8,128)(2,1)}, f32[8,128,128]{2,1,0:T(8,128)}, f32[8,128,128]{2,1,0:T(8,128)}) custom-call(bf16[8,3,128,128]{3,2,1,0:T(8,128)(2,1)} %copy-done.5, bf16[8,128,128]{2,1,0:T(8,128)(2,1)} %and_convert_fusion.member_ref, bf16[4096,128]{1,0:T(8,128)(2,1)} %select_convert_fusion.hidden_ref, ...), custom_call_target="tpu_custom_call" | custom-call | flops 4000000000 | bytes 1000000 | tf_op jit(solution)/shard_map/far/pallas_call | solution.py:235
  80.4 10.8 %all-to-all-done.2.rows_ref = bf16[8,128,1536]{2,1,0:T(8,128)(2,1)S(1)} async-done(((bf16[8,128,1536]{2,1,0:T(8,128)(2,1)}), bf16[8,128,1536]{2,1,0:T(8,128)(2,1)S(1)}, u32[]{:S(2)}, u32[]{:S(2)}) %all-to-all-start.2) | async-done | bytes 3145760 | tf_op jit(solution)/shard_map/all_to_all | solution.py:50
  91.2 0.9 copy-done.4
  92.1 1.9 %outer.1 = (bf16[32,1536]{1,0:T(8,128)(2,1)S(1)}, bf16[32,1536]{1,0:T(8,128)(2,1)}, bf16[32,1536]{1,0:T(8,128)(2,1)}, bf16[32,1536]{1,0:T(8,128)(2,1)}) custom-call(s32[4]{0:T(128)S(1)} %pad_add_fusion.order_ref, bf16[8,128,128]{2,1,0:T(8,128)(2,1)S(1)} %copy-done.4, bf16[8,128,1536]{2,1,0:T(8,128)(2,1)S(1)} %all-to-all-done.2.rows_ref), custom_call_target="tpu_custom_call" | custom-call | flops 1000000000 | bytes 1000000 | tf_op jit(solution)/shard_map/outer/pallas_call | solution.py:235
  94.0 0.6 copy-done.2
  94.6 2.0 %collective-permute-start.3 = (bf16[32,1536]{1,0:T(8,128)(2,1)}, bf16[32,1536]{1,0:T(8,128)(2,1)}, u32[]{:S(2)}, u32[]{:S(2)}) collective-permute-start(bf16[32,1536]{1,0:T(8,128)(2,1)} %get-tuple-element.36), channel_id=1, source_target_pairs={{0,16},{16,0},{32,48},{48,32},{64,80},{80,64},{96,112},{112,96},{1... | collective-permute-start | bytes 294920 | tf_op jit(solution)/shard_map/ppermute | solution.py:41
  96.6 3.8 %collective-permute-start.4 = (bf16[32,1536]{1,0:T(8,128)(2,1)}, bf16[32,1536]{1,0:T(8,128)(2,1)}, u32[]{:S(2)}, u32[]{:S(2)}) collective-permute-start(bf16[32,1536]{1,0:T(8,128)(2,1)} %get-tuple-element.37), channel_id=1, source_target_pairs={{0,96},{16,112},{32,64},{48,80},{64,32},{80,48},{96,0},{112,16},{1... | collective-permute-start | bytes 294920 | tf_op jit(solution)/shard_map/ppermute | solution.py:41
  100.5 3.0 %collective-permute-start.5 = (bf16[32,1536]{1,0:T(8,128)(2,1)}, bf16[32,1536]{1,0:T(8,128)(2,1)}, u32[]{:S(2)}, u32[]{:S(2)}) collective-permute-start(bf16[32,1536]{1,0:T(8,128)(2,1)} %get-tuple-element.38), channel_id=1, source_target_pairs={{0,112},{16,96},{32,80},{48,64},{64,48},{80,32},{96,16},{112,0},{1... | collective-permute-start | bytes 294920 | tf_op jit(solution)/shard_map/ppermute | solution.py:41
  103.4 1.0 constant_dynamic-slice_fusion.weight_ref
  104.5 1.0 project.1.grad_ref
  105.5 0.7 copy-done.1
  106.2 2.5 %collective-permute-done.5.refs_3_ = bf16[32,1536]{1,0:T(8,128)(2,1)} collective-permute-done((bf16[32,1536]{1,0:T(8,128)(2,1)}, bf16[32,1536]{1,0:T(8,128)(2,1)}, u32[]{:S(2)}, u32[]{:S(2)}) %collective-permute-start.5) | collective-permute-done | bytes 98336 | tf_op jit(solution)/shard_map/ppermute | solution.py:41
  108.7 1.8 %sum.1 = bf16[16,32,96]{2,1,0:T(8,128)(2,1)} custom-call(bf16[32,1536]{1,0:T(8,128)(2,1)S(1)} %copy-done.3, bf16[32,1536]{1,0:T(8,128)(2,1)} %collective-permute-done.3.refs_1_, bf16[32,1536]{1,0:T(8,128)(2,1)} %collective-permute-done.4.refs_2_, bf16[32,1536]{1,0:T(8,128)(2,1)} %collective-permute-done.5.refs_3_), custom_call_target="tpu_custom_call" | custom-call | flops 1000000 | bytes 1000000 | tf_op jit(solution)/shard_map/sum/pallas_call | solution.py:235
  110.4 15.2 %all-to-all-start.3 = ((bf16[16,32,96]{2,1,0:T(8,128)(2,1)}), bf16[16,32,96]{2,1,0:T(8,128)(2,1)S(1)}, u32[]{:S(2)}, u32[]{:S(2)}) async-start(bf16[16,32,96]{2,1,0:T(8,128)(2,1)} %sum.1), calls=%async_computation.3 | async-start | bytes 262144 | tf_op jit(solution)/shard_map/all_to_all | solution.py:391
  125.6 10.1 %attend_grad.1 = bf16[8,128,128]{2,1,0:T(8,128)(2,1)} custom-call(bf16[8,3,128,128]{3,2,1,0:T(8,128)(2,1)} %copy-done.5, bf16[8,128,128]{2,1,0:T(8,128)(2,1)} %and_convert_fusion.member_ref, bf16[4096,128]{1,0:T(8,128)(2,1)} %select_convert_fusion.hidden_ref, bf16[8,128,128]{2,1,0:T(8,128)(2,1)} %copy-done.1, f32[8,128,128]{2,1,0:T(8,128)} %get-tuple-element.46.exact_ref, ...), custom_call_target="tpu_custom_call" | custom-call | flops 5000000000 | bytes 1000000 | tf_op jit(solution)/shard_map/attend_grad/pallas_call | solution.py:235
  135.7 4.6 %all-to-all-done.3 = bf16[16,32,96]{2,1,0:T(8,128)(2,1)S(1)} async-done(((bf16[16,32,96]{2,1,0:T(8,128)(2,1)}), bf16[16,32,96]{2,1,0:T(8,128)(2,1)S(1)}, u32[]{:S(2)}, u32[]{:S(2)}) %all-to-all-start.3) | async-done | bytes 98336 | tf_op jit(solution)/shard_map/all_to_all | solution.py:391
  140.4 1.9 %collective-permute-start.7 = (f32[32,96]{1,0:T(8,128)S(1)}, f32[32,96]{1,0:T(8,128)S(1)}, u32[]{:S(2)}, u32[]{:S(2)}) collective-permute-start(f32[32,96]{1,0:T(8,128)S(1)} %broadcast_multiply_fusion), channel_id=1, source_target_pairs={{0,16},{96,32},{112,80},{48,96},{64,144},{128,160},{144,208},{240,... | collective-permute-start | bytes 36872 | tf_op jit(solution)/shard_map/ppermute | solution.py:66
  142.4 1.3 collective-permute-start.8
  143.7 4.5 %collective-permute-start.6 = (f32[32,96]{1,0:T(8,128)S(1)}, f32[32,96]{1,0:T(8,128)S(1)}, u32[]{:S(2)}, u32[]{:S(2)}) collective-permute-start(f32[32,96]{1,0:T(8,128)S(1)} %broadcast_multiply_fusion), channel_id=1, source_target_pairs={{0,0},{16,16},{96,48},{112,64},{32,80},{48,112},{64,128},{80,144},... | collective-permute-start | bytes 36872 | tf_op jit(solution)/shard_map/ppermute | solution.py:66
  148.2 3.4 %all-to-all-start.4 = ((bf16[8,128,128]{2,1,0:T(8,128)(2,1)}), bf16[8,128,128]{2,1,0:T(8,128)(2,1)S(1)}, u32[]{:S(2)}, u32[]{:S(2)}) async-start(bf16[8,128,128]{2,1,0:T(8,128)(2,1)} %attend_grad.1), calls=%async_computation.4 | async-start | bytes 524288 | tf_op jit(solution)/shard_map/all_to_all | solution.py:50
  151.7 0.6 fusion
  152.3 6.5 %all-to-all-done.4.slots_ref = bf16[8,128,128]{2,1,0:T(8,128)(2,1)S(1)} async-done(((bf16[8,128,128]{2,1,0:T(8,128)(2,1)}), bf16[8,128,128]{2,1,0:T(8,128)(2,1)S(1)}, u32[]{:S(2)}, u32[]{:S(2)}) %all-to-all-start.4) | async-done | bytes 262176 | tf_op jit(solution)/shard_map/all_to_all | solution.py:50
  158.8 0.7 join.1
  (48 shorter events, 0.9 us)
Async XLA Ops:
  7.2 9.2 %copy-start = (bf16[1,128,1536]{2,1,0:T(8,128)(2,1)S(1)}, bf16[1,128,1536]{2,1,0:T(8,128)(2,1)}, u32[]{:S(2)}) copy-start(bf16[1,128,1536]{2,1,0:T(8,128)(2,1)} %param.10) | copy-start | bytes 1179652
  7.2 7.8 %copy-start.7 = (s32[1,32,32]{2,1,0:T(8,128)S(1)}, s32[1,32,32]{2,1,0:T(8,128)}, u32[]{:S(2)}) copy-start(s32[1,32,32]{2,1,0:T(8,128)} %param.12) | copy-start | bytes 12292
  7.2 8.0 %copy-start.9 = (s32[1,5]{1,0:T(1,128)S(1)}, s32[1,5]{1,0:T(1,128)}, u32[]{:S(2)}) copy-start(s32[1,5]{1,0:T(1,128)} %param.13) | copy-start | bytes 64
  7.2 96.2 %all-gather.2.cloned.1.call-start = ((), (), s32[]{:S(2)}) async-start(), calls=%async_computation.5 | async-start | bytes 2506752 | tf_op jit(solution)/shard_map/all_gather | solution.py:283
  10.2 17.6 %all-to-all-start = ((bf16[8,3,128,128]{3,2,1,0:T(8,128)(2,1)}), bf16[8,3,128,128]{3,2,1,0:T(8,128)(2,1)S(1)}, u32[]{:S(2)}, u32[]{:S(2)}) async-start(bf16[8,3,128,128]{3,2,1,0:T(8,128)(2,1)} %pack.1), calls=%async_computation | async-start | bytes 1572864 | tf_op jit(solution)/shard_map/all_to_all | solution.py:50
  27.8 9.4 %copy-start.5 = (bf16[8,3,128,128]{3,2,1,0:T(8,128)(2,1)}, bf16[8,3,128,128]{3,2,1,0:T(8,128)(2,1)S(1)}, u32[]{:S(2)}) copy-start(bf16[8,3,128,128]{3,2,1,0:T(8,128)(2,1)S(1)} %all-to-all-done.input_ref) | copy-start | bytes 2359300
  27.8 17.6 %all-to-all-start.1 = ((bf16[32,8,1536]{2,1,0:T(8,128)(2,1)}), bf16[32,8,1536]{2,1,0:T(8,128)(2,1)S(1)}, u32[]{:S(2)}, u32[]{:S(2)}) async-start(bf16[32,8,1536]{2,1,0:T(8,128)(2,1)} %bitcast.7), calls=%async_computation.1 | async-start | bytes 1572864 | tf_op jit(solution)/shard_map/all_to_all | solution.py:297
  33.4 3.8 %copy-start.6 = (bf16[8,2,128,128]{3,2,1,0:T(8,128)(2,1)}, bf16[8,2,128,128]{3,2,1,0:T(8,128)(2,1)S(1)}, u32[]{:S(2)}) copy-start(bf16[8,2,128,128]{3,2,1,0:T(8,128)(2,1)S(1)} %slice.21.own_ref) | copy-start | bytes 1572868
  33.4 3.8 %collective-permute-start = (bf16[8,2,128,128]{3,2,1,0:T(8,128)(2,1)S(1)}, bf16[8,2,128,128]{3,2,1,0:T(8,128)(2,1)S(1)}, u32[]{:S(2)}, u32[]{:S(2)}) collective-permute-start(bf16[8,2,128,128]{3,2,1,0:T(8,128)(2,1)S(1)} %slice.21.own_ref), channel_id=1, source_target_pairs={{0,16},{16,0},{32,48},{48,32},{64,80},{80,64},{96,112},{112,96},{1... | collective-permute-start | bytes 1572872 | tf_op jit(solution)/shard_map/ppermute | solution.py:41
  37.3 0.8 copy-start.8
  48.2 43.0 %all-to-all-start.2 = ((bf16[8,128,1536]{2,1,0:T(8,128)(2,1)}), bf16[8,128,1536]{2,1,0:T(8,128)(2,1)S(1)}, u32[]{:S(2)}, u32[]{:S(2)}) async-start(bf16[8,128,1536]{2,1,0:T(8,128)(2,1)} %broadcast_in_dim.29), calls=%async_computation.2 | async-start | bytes 6291456 | tf_op jit(solution)/shard_map/all_to_all | solution.py:50
  51.8 18.0 %collective-permute-start.1 = (bf16[8,2,128,128]{3,2,1,0:T(8,128)(2,1)}, bf16[8,2,128,128]{3,2,1,0:T(8,128)(2,1)}, u32[]{:S(2)}, u32[]{:S(2)}) collective-permute-start(bf16[8,2,128,128]{3,2,1,0:T(8,128)(2,1)} %copy-done.6), channel_id=1, source_target_pairs={{0,96},{16,112},{32,64},{48,80},{64,32},{80,48},{96,0},{112,16},{1... | collective-permute-start | bytes 1572872 | tf_op jit(solution)/shard_map/ppermute | solution.py:41
  69.8 4.1 %collective-permute-start.2 = (bf16[8,2,128,128]{3,2,1,0:T(8,128)(2,1)}, bf16[8,2,128,128]{3,2,1,0:T(8,128)(2,1)}, u32[]{:S(2)}, u32[]{:S(2)}) collective-permute-start(bf16[8,2,128,128]{3,2,1,0:T(8,128)(2,1)} %collective-permute-done.1.own_ref.far_ref), channel_id=1, source_target_pairs={{0,16},{16,0},{32,48},{48,32},{64,80},{80,64},{96,112},{112,96},{1... | collective-permute-start | bytes 1572872 | tf_op jit(solution)/shard_map/ppermute | solution.py:41
  91.2 1.0 copy-start.4
  94.0 0.6 copy-start.2
  94.6 11.6 %collective-permute-start.3 = (bf16[32,1536]{1,0:T(8,128)(2,1)}, bf16[32,1536]{1,0:T(8,128)(2,1)}, u32[]{:S(2)}, u32[]{:S(2)}) collective-permute-start(bf16[32,1536]{1,0:T(8,128)(2,1)} %get-tuple-element.36), channel_id=1, source_target_pairs={{0,16},{16,0},{32,48},{48,32},{64,80},{80,64},{96,112},{112,96},{1... | collective-permute-start | bytes 294920 | tf_op jit(solution)/shard_map/ppermute | solution.py:41
  96.6 9.5 %collective-permute-start.4 = (bf16[32,1536]{1,0:T(8,128)(2,1)}, bf16[32,1536]{1,0:T(8,128)(2,1)}, u32[]{:S(2)}, u32[]{:S(2)}) collective-permute-start(bf16[32,1536]{1,0:T(8,128)(2,1)} %get-tuple-element.37), channel_id=1, source_target_pairs={{0,96},{16,112},{32,64},{48,80},{64,32},{80,48},{96,0},{112,16},{1... | collective-permute-start | bytes 294920 | tf_op jit(solution)/shard_map/ppermute | solution.py:41
  100.5 8.2 %collective-permute-start.5 = (bf16[32,1536]{1,0:T(8,128)(2,1)}, bf16[32,1536]{1,0:T(8,128)(2,1)}, u32[]{:S(2)}, u32[]{:S(2)}) collective-permute-start(bf16[32,1536]{1,0:T(8,128)(2,1)} %get-tuple-element.38), channel_id=1, source_target_pairs={{0,112},{16,96},{32,80},{48,64},{64,48},{80,32},{96,16},{112,0},{1... | collective-permute-start | bytes 294920 | tf_op jit(solution)/shard_map/ppermute | solution.py:41
  104.5 4.2 %copy-start.3 = (bf16[32,1536]{1,0:T(8,128)(2,1)S(1)}, bf16[32,1536]{1,0:T(8,128)(2,1)}, u32[]{:S(2)}) copy-start(bf16[32,1536]{1,0:T(8,128)(2,1)} %copy-done.2) | copy-start | bytes 294916
  105.5 0.7 copy-start.1
  110.4 29.9 %all-to-all-start.3 = ((bf16[16,32,96]{2,1,0:T(8,128)(2,1)}), bf16[16,32,96]{2,1,0:T(8,128)(2,1)S(1)}, u32[]{:S(2)}, u32[]{:S(2)}) async-start(bf16[16,32,96]{2,1,0:T(8,128)(2,1)} %sum.1), calls=%async_computation.3 | async-start | bytes 262144 | tf_op jit(solution)/shard_map/all_to_all | solution.py:391
  140.4 11.2 %collective-permute-start.7 = (f32[32,96]{1,0:T(8,128)S(1)}, f32[32,96]{1,0:T(8,128)S(1)}, u32[]{:S(2)}, u32[]{:S(2)}) collective-permute-start(f32[32,96]{1,0:T(8,128)S(1)} %broadcast_multiply_fusion), channel_id=1, source_target_pairs={{0,16},{96,32},{112,80},{48,96},{64,144},{128,160},{144,208},{240,... | collective-permute-start | bytes 36872 | tf_op jit(solution)/shard_map/ppermute | solution.py:66
  142.4 9.3 %collective-permute-start.8 = (f32[32,96]{1,0:T(8,128)S(1)}, f32[32,96]{1,0:T(8,128)S(1)}, u32[]{:S(2)}, u32[]{:S(2)}) collective-permute-start(f32[32,96]{1,0:T(8,128)S(1)} %broadcast_multiply_fusion), channel_id=1, source_target_pairs={{16,32},{32,96},{80,160},{224,224},{176,288},{256,352},{368,416},{... | collective-permute-start | bytes 36872 | tf_op jit(solution)/shard_map/ppermute | solution.py:66
  143.7 8.0 %collective-permute-start.6 = (f32[32,96]{1,0:T(8,128)S(1)}, f32[32,96]{1,0:T(8,128)S(1)}, u32[]{:S(2)}, u32[]{:S(2)}) collective-permute-start(f32[32,96]{1,0:T(8,128)S(1)} %broadcast_multiply_fusion), channel_id=1, source_target_pairs={{0,0},{16,16},{96,48},{112,64},{32,80},{48,112},{64,128},{80,144},... | collective-permute-start | bytes 36872 | tf_op jit(solution)/shard_map/ppermute | solution.py:66
  148.2 10.6 %all-to-all-start.4 = ((bf16[8,128,128]{2,1,0:T(8,128)(2,1)}), bf16[8,128,128]{2,1,0:T(8,128)(2,1)S(1)}, u32[]{:S(2)}, u32[]{:S(2)}) async-start(bf16[8,128,128]{2,1,0:T(8,128)(2,1)} %attend_grad.1), calls=%async_computation.4 | async-start | bytes 524288 | tf_op jit(solution)/shard_map/all_to_all | solution.py:50
Sparse Core Ops, SparseCore 0:
  10.1 78.8 all-gather.1

commit v8 on v7

--- a/solution.py
+++ b/solution.py
@@ -207,6 +207,11 @@
         copy.wait()
 
 
+def copy_kernel(rows_ref, out_ref):
+    for slot in range(SLOTS):
+        out_ref[slot] = rows_ref[...]
+
+
 def join_kernel(head_count, slots_ref, out_ref):
     for head in range(head_count):
         out_ref[0, :, pl.ds(head * HEAD_DIM, HEAD_DIM)] = slots_ref[head]
@@ -291,10 +296,10 @@
         in_specs=[pl.BlockSpec(memory_space=pl.ANY)] * 3,
         scratch_shapes=[pltpu.SemaphoreType.DMA((SLOTS, 3))],
     )(student_query, key_cache, value_cache)
+    arrived = lax.all_to_all(pack_rows(grad_rows[0], counts, me), "seq", 0, 0, tiled=True)
+    slots, arrived = lax.optimization_barrier((slots, arrived))
     inputs = trade(slots)
-    inputs, packed = lax.optimization_barrier((inputs, pack_rows(grad_rows[0], counts, me)))
     own = inputs[:, 1:]
-    arrived = lax.all_to_all(packed, "seq", 0, 0, tiled=True)
     beside = send(own, dcore=1)
 
     rank = jnp.arange(SLOTS, dtype=jnp.int32)
@@ -333,10 +338,11 @@
         inputs, member, hidden, own, beside
     )
     ordered = unpack_rows(arrived, counts, me, row_count)
-    copies = jnp.broadcast_to(ordered[None], (SLOTS,) + ordered.shape)
-    late_own, copies, carry = lax.optimization_barrier((own, copies, carry))
+    (copies,) = call(copy_kernel, [((SLOTS,) + ordered.shape, jnp.bfloat16)], "copies", 8e9)(ordered)
+    late_own, copies = lax.optimization_barrier((own, copies))
     group_rows = trade(copies)
     far = send(late_own, mirror=True)
+    far, carry = lax.optimization_barrier((far, carry))
     far_beside = send(far, dcore=1)
     attended, exact, level = call(
         functools.partial(far_kernel, scale),

time: 169 us -> 170 us (level)
  waiting for transfers between devices: 49.5 us -> 44.4 us
  other arithmetic: 5.28 us -> 8.66 us
  local copies, waits for them, and re-layouts: 9.54 us -> 12.2 us
    ppermute x6, waiting for transfers between devices: 18.3 us -> 9.54 us  [send(): return lax.ppermute(value, 'seq', pairs)]
    all_to_all x1, waiting for transfers between devices: 1.88 us -> 7.84 us  [shards(): lax.all_to_all(pack_rows(grad_rows[0], counts, me), 'seq', 0, 0, tiled=True)]
    all_to_all x3, waiting for transfers between devices: 24 us -> 19.1 us  [trade(): lax.all_to_all(slots, 'seq', 0, 0, axis_index_groups=groups, tiled=True)]
    all_to_all x1, starting transfers between devices: 5.57 us -> 9.44 us  [shards(): lax.all_to_all(pack_rows(grad_rows[0], counts, me), 'seq', 0, 0, tiled=True)]
    ppermute x3, waiting for transfers between devices: 0.01 us -> 2.53 us  [pass_on(): lax.ppermute(block, 'seq', [(held[3 * turn + take], 4 * turn + put) for t...]
    unnamed x20 -> x24, local copies, waits for them, and re-layouts: 3.13 us -> 5.55 us
    all_to_all x1, starting transfers between devices: 15.2 us -> 13.2 us  [shards(): terms = lax.all_to_all(clip_parts, 'dp', 0, 0, tiled=True)]
    broadcast_in_dim x1 -> x0, local copies, waits for them, and re-layouts: 1.9 us -> none  [shards(): copies = jnp.broadcast_to(ordered[None], (SLOTS,) + ordered.shape)]
  transfers between devices with their start and end apart: 15 -> 15, of which waited for: 9 -> 9; matrix products, arithmetic and copies ran while one was open for 7% -> 9% of each run, Pallas kernels for 16% -> 16%
where the time goes in v8:
time: 170 us; the launch traced here: 167 us
  starting transfers between devices  58.2 us (34%)
  waiting for transfers between devices  44.4 us (26%)
  Pallas kernels  29.6 us (17%)
  between operations  14.5 us (9%)
  local copies, waits for them, and re-layouts  12.2 us (7%)
  other arithmetic  8.66 us (5%)
    pallas_call x9, Pallas kernels, run(): pl.pallas_call(kernel, out_shape=[jax.ShapeDtypeStruct(shape, dtype) for...  29.6 us
    all_to_all x3, waiting for transfers between devices, trade(): lax.all_to_all(slots, 'seq', 0, 0, axis_index_groups=groups, tiled=True)  19.1 us
    ppermute x6, starting transfers between devices, send(): return lax.ppermute(value, 'seq', pairs)  16.5 us
    all_to_all x1, starting transfers between devices, shards(): terms = lax.all_to_all(clip_parts, 'dp', 0, 0, tiled=True)  13.2 us
    all_to_all x3, starting transfers between devices, trade(): lax.all_to_all(slots, 'seq', 0, 0, axis_index_groups=groups, tiled=True)  10.6 us
    ppermute x6, waiting for transfers between devices, send(): return lax.ppermute(value, 'seq', pairs)  9.54 us
    all_to_all x1, starting transfers between devices, shards(): lax.all_to_all(pack_rows(grad_rows[0], counts, me), 'seq', 0, 0, tiled=True)  9.44 us
    ppermute x3, starting transfers between devices, pass_on(): lax.ppermute(block, 'seq', [(held[3 * turn + take], 4 * turn + put) for t...  8.35 us
  transfers between devices with their start and end apart: 15, of which 9 were waited for; matrix products, arithmetic and copies ran while one was open for 9% of the time, Pallas kernels for 16%

profile of v8, /device:TPU:6, one launch (start us, length us, event | category | flops | bytes accessed | tf_op | source)
XLA Modules:
  0.0 167.5 jit_solution(6234934274927412037)
XLA Ops:
  7.2 0.7 all-gather.2.cloned.1.call-update
  7.9 0.7 fusion.4
  8.9 0.7 bitcast_subtract_fusion.2
  9.8 2.2 %gather_fusion = bf16[256,1536]{1,0:T(8,128)(2,1)} fusion(bf16[128,1536]{1,0:T(8,128)(2,1)S(1)} %bitcast.32, s32[1024]{0:T(1024)S(1)} %pad_clamp_fusion.1), kind=kCustom, calls=%fused_computation | custom fusion | bytes 1573888 | tf_op jit(solution)/shard_map/gather | solution.py:262
  12.0 9.4 %all-to-all-start = ((bf16[32,8,1536]{2,1,0:T(8,128)(2,1)}), bf16[32,8,1536]{2,1,0:T(8,128)(2,1)S(1)}, u32[]{:S(2)}, u32[]{:S(2)}) async-start(bf16[32,8,1536]{2,1,0:T(8,128)(2,1)} %bitcast.7), calls=%async_computation | async-start | bytes 1572864 | tf_op jit(solution)/shard_map/all_to_all | solution.py:299
  23.2 2.2 %pack.1 = bf16[8,3,128,128]{3,2,1,0:T(8,128)(2,1)} custom-call(bf16[1,128,768]{2,1,0:T(8,128)(2,1)} %query_ref.1, bf16[1,128,768]{2,1,0:T(8,128)(2,1)} %key_ref.1, bf16[1,128,768]{2,1,0:T(8,128)(2,1)} %value_ref.1), custom_call_target="tpu_custom_call" | custom-call | flops 1000000 | bytes 1000000 | tf_op jit(solution)/shard_map/pack/pallas_call | solution.py:240
  25.6 7.8 %all-to-all-done = bf16[32,8,1536]{2,1,0:T(8,128)(2,1)S(1)} async-done(((bf16[32,8,1536]{2,1,0:T(8,128)(2,1)}), bf16[32,8,1536]{2,1,0:T(8,128)(2,1)S(1)}, u32[]{:S(2)}, u32[]{:S(2)}) %all-to-all-start) | async-done | bytes 786464 | tf_op jit(solution)/shard_map/all_to_all | solution.py:299
  33.5 3.5 %all-to-all-start.1 = ((bf16[8,3,128,128]{3,2,1,0:T(8,128)(2,1)}), bf16[8,3,128,128]{3,2,1,0:T(8,128)(2,1)S(1)}, u32[]{:S(2)}, u32[]{:S(2)}) async-start(bf16[8,3,128,128]{3,2,1,0:T(8,128)(2,1)} %pack.1), calls=%async_computation.1 | async-start | bytes 1572864 | tf_op jit(solution)/shard_map/all_to_all | solution.py:50
  37.0 0.9 gather_fusion.1
  38.2 1.6 copy-done.1
  39.8 11.3 %all-to-all-done.1.input_ref = bf16[8,3,128,128]{3,2,1,0:T(8,128)(2,1)S(1)} async-done(((bf16[8,3,128,128]{3,2,1,0:T(8,128)(2,1)}), bf16[8,3,128,128]{3,2,1,0:T(8,128)(2,1)S(1)}, u32[]{:S(2)}, u32[]{:S(2)}) %all-to-all-start.1) | async-done | bytes 786464 | tf_op jit(solution)/shard_map/all_to_all | solution.py:50
  51.1 0.9 slice.32.own_ref
  52.3 3.6 %all-to-all-start.2 = ((bf16[8,128,1536]{2,1,0:T(8,128)(2,1)}), bf16[8,128,1536]{2,1,0:T(8,128)(2,1)S(1)}, u32[]{:S(2)}, u32[]{:S(2)}) async-start(bf16[8,128,1536]{2,1,0:T(8,128)(2,1)} %copy-done.1), calls=%async_computation.2 | async-start | bytes 6291456 | tf_op jit(solution)/shard_map/all_to_all | solution.py:50
  55.9 3.3 %select_convert_fusion.hidden_ref = bf16[4096,128]{1,0:T(8,128)(2,1)} fusion(s32[128]{0:T(128)} %pad.8, s32[4096]{0:T(1024)S(1)} %add_bitcast_fusion), kind=kLoop, calls=%fused_computation.2 | loop fusion | flops 1572864 | bytes 1065472 | tf_op jit(solution)/shard_map/convert_element_type | solution.py:320
  59.3 2.0 %collective-permute-start.1 = (bf16[8,2,128,128]{3,2,1,0:T(8,128)(2,1)}, bf16[8,2,128,128]{3,2,1,0:T(8,128)(2,1)S(1)}, u32[]{:S(2)}, u32[]{:S(2)}) collective-permute-start(bf16[8,2,128,128]{3,2,1,0:T(8,128)(2,1)} %slice.32.own_ref), channel_id=1, source_target_pairs={{0,16},{16,0},{32,48},{48,32},{64,80},{80,64},{96,112},{112,96},{1... | collective-permute-start | bytes 1572872 | tf_op jit(solution)/shard_map/ppermute | solution.py:41
  61.3 0.7 bitcast_subtract_fusion.1
  62.0 0.8 iota_add_fusion
  62.7 3.8 %collective-permute-start = (bf16[8,2,128,128]{3,2,1,0:T(8,128)(2,1)}, bf16[8,2,128,128]{3,2,1,0:T(8,128)(2,1)}, u32[]{:S(2)}, u32[]{:S(2)}) collective-permute-start(bf16[8,2,128,128]{3,2,1,0:T(8,128)(2,1)} %slice.32.own_ref), channel_id=1, source_target_pairs={{0,96},{16,112},{32,64},{48,80},{64,32},{80,48},{96,0},{112,16},{1... | collective-permute-start | bytes 1572872 | tf_op jit(solution)/shard_map/ppermute | solution.py:41
  66.5 1.6 and_convert_fusion.member_ref
  68.1 0.8 copy-done.9
  68.9 5.4 %near.1 = (f32[8,128,1]{2,1,0:T(8,128)}, f32[8,128,256]{2,1,0:T(8,128)}) custom-call(bf16[8,3,128,128]{3,2,1,0:T(8,128)(2,1)} %copy-done.6, bf16[8,128,128]{2,1,0:T(8,128)(2,1)} %and_convert_fusion.member_ref, bf16[4096,128]{1,0:T(8,128)(2,1)} %select_convert_fusion.hidden_ref, bf16[8,2,128,128]{3,2,1,0:T(8,128)(2,1)} %slice.32.own_ref, ...), custom_call_target="tpu_custom_call" | custom-call | flops 4000000000 | bytes 1000000 | tf_op jit(solution)/shard_map/near/pallas_call | solution.py:240
  74.3 6.0 %collective-permute-done.own_ref.far_ref = bf16[8,2,128,128]{3,2,1,0:T(8,128)(2,1)} collective-permute-done((bf16[8,2,128,128]{3,2,1,0:T(8,128)(2,1)}, bf16[8,2,128,128]{3,2,1,0:T(8,128)(2,1)}, u32[]{:S(2)}, u32[]{:S(2)}) %collective-permute-start) | collective-permute-done | bytes 524320 | tf_op jit(solution)/shard_map/ppermute | solution.py:41
  80.3 1.9 %collective-permute-start.2 = (bf16[8,2,128,128]{3,2,1,0:T(8,128)(2,1)}, bf16[8,2,128,128]{3,2,1,0:T(8,128)(2,1)}, u32[]{:S(2)}, u32[]{:S(2)}) collective-permute-start(bf16[8,2,128,128]{3,2,1,0:T(8,128)(2,1)} %collective-permute-done.own_ref.far_ref), channel_id=1, source_target_pairs={{0,16},{16,0},{32,48},{48,32},{64,80},{80,64},{96,112},{112,96},{1... | collective-permute-start | bytes 1572872 | tf_op jit(solution)/shard_map/ppermute | solution.py:41
  82.4 2.1 %collective-permute-done.2.core_ref.far_core_ref = bf16[8,2,128,128]{3,2,1,0:T(8,128)(2,1)} collective-permute-done((bf16[8,2,128,128]{3,2,1,0:T(8,128)(2,1)}, bf16[8,2,128,128]{3,2,1,0:T(8,128)(2,1)}, u32[]{:S(2)}, u32[]{:S(2)}) %collective-permute-start.2) | collective-permute-done | bytes 524320 | tf_op jit(solution)/shard_map/ppermute | solution.py:41
  84.5 6.4 %far.1 = (bf16[8,128,128]{2,1,0:T(8,128)(2,1)}, f32[8,128,128]{2,1,0:T(8,128)}, f32[8,128,128]{2,1,0:T(8,128)}) custom-call(bf16[8,3,128,128]{3,2,1,0:T(8,128)(2,1)} %copy-done.6, bf16[8,128,128]{2,1,0:T(8,128)(2,1)} %and_convert_fusion.member_ref, bf16[4096,128]{1,0:T(8,128)(2,1)} %select_convert_fusion.hidden_ref, ...), custom_call_target="tpu_custom_call" | custom-call | flops 4000000000 | bytes 1000000 | tf_op jit(solution)/shard_map/far/pallas_call | solution.py:240
  90.9 3.8 %all-to-all-done.2.rows_ref = bf16[8,128,1536]{2,1,0:T(8,128)(2,1)S(1)} async-done(((bf16[8,128,1536]{2,1,0:T(8,128)(2,1)}), bf16[8,128,1536]{2,1,0:T(8,128)(2,1)S(1)}, u32[]{:S(2)}, u32[]{:S(2)}) %all-to-all-start.2) | async-done | bytes 3145760 | tf_op jit(solution)/shard_map/all_to_all | solution.py:50
  94.6 0.9 copy-done.5
  95.6 1.9 %outer.1 = (bf16[32,1536]{1,0:T(8,128)(2,1)S(1)}, bf16[32,1536]{1,0:T(8,128)(2,1)}, bf16[32,1536]{1,0:T(8,128)(2,1)}, bf16[32,1536]{1,0:T(8,128)(2,1)}) custom-call(s32[4]{0:T(128)S(1)} %pad_add_fusion.order_ref, bf16[8,128,128]{2,1,0:T(8,128)(2,1)S(1)} %copy-done.5, bf16[8,128,1536]{2,1,0:T(8,128)(2,1)S(1)} %all-to-all-done.2.rows_ref), custom_call_target="tpu_custom_call" | custom-call | flops 1000000000 | bytes 1000000 | tf_op jit(solution)/shard_map/outer/pallas_call | solution.py:240
  97.4 0.6 copy-done.3
  98.1 1.9 %collective-permute-start.3 = (bf16[32,1536]{1,0:T(8,128)(2,1)}, bf16[32,1536]{1,0:T(8,128)(2,1)}, u32[]{:S(2)}, u32[]{:S(2)}) collective-permute-start(bf16[32,1536]{1,0:T(8,128)(2,1)} %get-tuple-element.38), channel_id=1, source_target_pairs={{0,16},{16,0},{32,48},{48,32},{64,80},{80,64},{96,112},{112,96},{1... | collective-permute-start | bytes 294920 | tf_op jit(solution)/shard_map/ppermute | solution.py:41
  100.0 2.9 %collective-permute-start.4 = (bf16[32,1536]{1,0:T(8,128)(2,1)}, bf16[32,1536]{1,0:T(8,128)(2,1)}, u32[]{:S(2)}, u32[]{:S(2)}) collective-permute-start(bf16[32,1536]{1,0:T(8,128)(2,1)} %get-tuple-element.39), channel_id=1, source_target_pairs={{0,96},{16,112},{32,64},{48,80},{64,32},{80,48},{96,0},{112,16},{1... | collective-permute-start | bytes 294920 | tf_op jit(solution)/shard_map/ppermute | solution.py:41
  102.9 4.0 %collective-permute-start.5 = (bf16[32,1536]{1,0:T(8,128)(2,1)}, bf16[32,1536]{1,0:T(8,128)(2,1)}, u32[]{:S(2)}, u32[]{:S(2)}) collective-permute-start(bf16[32,1536]{1,0:T(8,128)(2,1)} %get-tuple-element.40), channel_id=1, source_target_pairs={{0,112},{16,96},{32,80},{48,64},{64,48},{80,32},{96,16},{112,0},{1... | collective-permute-start | bytes 294920 | tf_op jit(solution)/shard_map/ppermute | solution.py:41
  106.9 1.0 constant_dynamic-slice_fusion.weight_ref
  107.9 1.0 project.1.grad_ref
  108.9 0.7 copy-done.2
  109.6 1.4 collective-permute-done.5.refs_3_
  111.1 1.8 %sum.1 = bf16[16,32,96]{2,1,0:T(8,128)(2,1)} custom-call(bf16[32,1536]{1,0:T(8,128)(2,1)S(1)} %copy-done.4, bf16[32,1536]{1,0:T(8,128)(2,1)} %collective-permute-done.3.refs_1_, bf16[32,1536]{1,0:T(8,128)(2,1)} %collective-permute-done.4.refs_2_, bf16[32,1536]{1,0:T(8,128)(2,1)} %collective-permute-done.5.refs_3_), custom_call_target="tpu_custom_call" | custom-call | flops 1000000 | bytes 1000000 | tf_op jit(solution)/shard_map/sum/pallas_call | solution.py:240
  112.9 13.2 %all-to-all-start.3 = ((bf16[16,32,96]{2,1,0:T(8,128)(2,1)}), bf16[16,32,96]{2,1,0:T(8,128)(2,1)S(1)}, u32[]{:S(2)}, u32[]{:S(2)}) async-start(bf16[16,32,96]{2,1,0:T(8,128)(2,1)} %sum.1), calls=%async_computation.3 | async-start | bytes 262144 | tf_op jit(solution)/shard_map/all_to_all | solution.py:397
  126.1 10.1 %attend_grad.1 = bf16[8,128,128]{2,1,0:T(8,128)(2,1)} custom-call(bf16[8,3,128,128]{3,2,1,0:T(8,128)(2,1)} %copy-done.6, bf16[8,128,128]{2,1,0:T(8,128)(2,1)} %and_convert_fusion.member_ref, bf16[4096,128]{1,0:T(8,128)(2,1)} %select_convert_fusion.hidden_ref, bf16[8,128,128]{2,1,0:T(8,128)(2,1)} %copy-done.2, f32[8,128,128]{2,1,0:T(8,128)} %get-tuple-element.48.exact_ref, ...), custom_call_target="tpu_custom_call" | custom-call | flops 5000000000 | bytes 1000000 | tf_op jit(solution)/shard_map/attend_grad/pallas_call | solution.py:240
  136.2 4.7 %all-to-all-done.3 = bf16[16,32,96]{2,1,0:T(8,128)(2,1)S(1)} async-done(((bf16[16,32,96]{2,1,0:T(8,128)(2,1)}), bf16[16,32,96]{2,1,0:T(8,128)(2,1)S(1)}, u32[]{:S(2)}, u32[]{:S(2)}) %all-to-all-start.3) | async-done | bytes 98336 | tf_op jit(solution)/shard_map/all_to_all | solution.py:397
  140.9 2.6 %collective-permute-start.7 = (f32[32,96]{1,0:T(8,128)S(1)}, f32[32,96]{1,0:T(8,128)S(1)}, u32[]{:S(2)}, u32[]{:S(2)}) collective-permute-start(f32[32,96]{1,0:T(8,128)S(1)} %broadcast_multiply_fusion), channel_id=1, source_target_pairs={{0,16},{96,32},{112,80},{48,96},{64,144},{128,160},{144,208},{240,... | collective-permute-start | bytes 36872 | tf_op jit(solution)/shard_map/ppermute | solution.py:66
  143.5 4.5 %collective-permute-start.6 = (f32[32,96]{1,0:T(8,128)S(1)}, f32[32,96]{1,0:T(8,128)S(1)}, u32[]{:S(2)}, u32[]{:S(2)}) collective-permute-start(f32[32,96]{1,0:T(8,128)S(1)} %broadcast_multiply_fusion), channel_id=1, source_target_pairs={{0,0},{16,16},{96,48},{112,64},{32,80},{48,112},{64,128},{80,144},... | collective-permute-start | bytes 36872 | tf_op jit(solution)/shard_map/ppermute | solution.py:66
  148.0 1.3 collective-permute-start.8
  149.3 3.4 %all-to-all-start.4 = ((bf16[8,128,128]{2,1,0:T(8,128)(2,1)}), bf16[8,128,128]{2,1,0:T(8,128)(2,1)S(1)}, u32[]{:S(2)}, u32[]{:S(2)}) async-start(bf16[8,128,128]{2,1,0:T(8,128)(2,1)} %attend_grad.1), calls=%async_computation.4 | async-start | bytes 524288 | tf_op jit(solution)/shard_map/all_to_all | solution.py:50
  152.7 2.5 %collective-permute-done.8 = f32[32,96]{1,0:T(8,128)S(1)} collective-permute-done((f32[32,96]{1,0:T(8,128)S(1)}, f32[32,96]{1,0:T(8,128)S(1)}, u32[]{:S(2)}, u32[]{:S(2)}) %collective-permute-start.8) | collective-permute-done | bytes 12320 | tf_op jit(solution)/shard_map/ppermute | solution.py:66
  155.3 0.6 fusion
  155.9 4.0 %all-to-all-done.4.slots_ref = bf16[8,128,128]{2,1,0:T(8,128)(2,1)S(1)} async-done(((bf16[8,128,128]{2,1,0:T(8,128)(2,1)}), bf16[8,128,128]{2,1,0:T(8,128)(2,1)S(1)}, u32[]{:S(2)}, u32[]{:S(2)}) %all-to-all-start.4) | async-done | bytes 262176 | tf_op jit(solution)/shard_map/all_to_all | solution.py:50
  159.9 0.7 join.1
  (52 shorter events, 3.0 us)
Async XLA Ops:
  7.2 2.6 %copy-start = (bf16[1,128,1536]{2,1,0:T(8,128)(2,1)S(1)}, bf16[1,128,1536]{2,1,0:T(8,128)(2,1)}, u32[]{:S(2)}) copy-start(bf16[1,128,1536]{2,1,0:T(8,128)(2,1)} %param.10) | copy-start | bytes 1179652
  7.2 99.7 %all-gather.2.cloned.1.call-start = ((), (), s32[]{:S(2)}) async-start(), calls=%async_computation.5 | async-start | bytes 2506752 | tf_op jit(solution)/shard_map/all_gather | solution.py:288
  9.8 12.4 %copy-start.7 = (s32[1,32,32]{2,1,0:T(8,128)S(1)}, s32[1,32,32]{2,1,0:T(8,128)}, u32[]{:S(2)}) copy-start(s32[1,32,32]{2,1,0:T(8,128)} %param.12) | copy-start | bytes 12292
  9.8 12.8 %copy-start.10 = (s32[1,5]{1,0:T(1,128)S(1)}, s32[1,5]{1,0:T(1,128)}, u32[]{:S(2)}) copy-start(s32[1,5]{1,0:T(1,128)} %param.13) | copy-start | bytes 64
  12.0 21.5 %all-to-all-start = ((bf16[32,8,1536]{2,1,0:T(8,128)(2,1)}), bf16[32,8,1536]{2,1,0:T(8,128)(2,1)S(1)}, u32[]{:S(2)}, u32[]{:S(2)}) async-start(bf16[32,8,1536]{2,1,0:T(8,128)(2,1)} %bitcast.7), calls=%async_computation | async-start | bytes 1572864 | tf_op jit(solution)/shard_map/all_to_all | solution.py:299
  21.5 0.6 copy-start.8
  22.7 2.7 %copy-start.11 = (s32[5,1]{0,1:T(1,128)}, s32[5,1]{0,1:T(1,128)S(1)}, u32[]{:S(2)}) copy-start(s32[5,1]{0,1:T(1,128)S(1)} %reduce-window.26) | copy-start | bytes 64
  33.5 17.6 %all-to-all-start.1 = ((bf16[8,3,128,128]{3,2,1,0:T(8,128)(2,1)}), bf16[8,3,128,128]{3,2,1,0:T(8,128)(2,1)S(1)}, u32[]{:S(2)}, u32[]{:S(2)}) async-start(bf16[8,3,128,128]{3,2,1,0:T(8,128)(2,1)} %pack.1), calls=%async_computation.1 | async-start | bytes 1572864 | tf_op jit(solution)/shard_map/all_to_all | solution.py:50
  38.2 1.6 copy-start.1
  51.1 1.2 copy-start.6
  52.3 42.4 %all-to-all-start.2 = ((bf16[8,128,1536]{2,1,0:T(8,128)(2,1)}), bf16[8,128,1536]{2,1,0:T(8,128)(2,1)S(1)}, u32[]{:S(2)}, u32[]{:S(2)}) async-start(bf16[8,128,1536]{2,1,0:T(8,128)(2,1)} %copy-done.1), calls=%async_computation.2 | async-start | bytes 6291456 | tf_op jit(solution)/shard_map/all_to_all | solution.py:50
  59.3 8.8 %collective-permute-start.1 = (bf16[8,2,128,128]{3,2,1,0:T(8,128)(2,1)}, bf16[8,2,128,128]{3,2,1,0:T(8,128)(2,1)S(1)}, u32[]{:S(2)}, u32[]{:S(2)}) collective-permute-start(bf16[8,2,128,128]{3,2,1,0:T(8,128)(2,1)} %slice.32.own_ref), channel_id=1, source_target_pairs={{0,16},{16,0},{32,48},{48,32},{64,80},{80,64},{96,112},{112,96},{1... | collective-permute-start | bytes 1572872 | tf_op jit(solution)/shard_map/ppermute | solution.py:41
  62.7 17.6 %collective-permute-start = (bf16[8,2,128,128]{3,2,1,0:T(8,128)(2,1)}, bf16[8,2,128,128]{3,2,1,0:T(8,128)(2,1)}, u32[]{:S(2)}, u32[]{:S(2)}) collective-permute-start(bf16[8,2,128,128]{3,2,1,0:T(8,128)(2,1)} %slice.32.own_ref), channel_id=1, source_target_pairs={{0,96},{16,112},{32,64},{48,80},{64,32},{80,48},{96,0},{112,16},{1... | collective-permute-start | bytes 1572872 | tf_op jit(solution)/shard_map/ppermute | solution.py:41
  68.1 0.8 copy-start.9
  80.3 4.1 %collective-permute-start.2 = (bf16[8,2,128,128]{3,2,1,0:T(8,128)(2,1)}, bf16[8,2,128,128]{3,2,1,0:T(8,128)(2,1)}, u32[]{:S(2)}, u32[]{:S(2)}) collective-permute-start(bf16[8,2,128,128]{3,2,1,0:T(8,128)(2,1)} %collective-permute-done.own_ref.far_ref), channel_id=1, source_target_pairs={{0,16},{16,0},{32,48},{48,32},{64,80},{80,64},{96,112},{112,96},{1... | collective-permute-start | bytes 1572872 | tf_op jit(solution)/shard_map/ppermute | solution.py:41
  94.6 1.0 copy-start.5
  97.4 0.6 copy-start.3
  98.1 11.6 %collective-permute-start.3 = (bf16[32,1536]{1,0:T(8,128)(2,1)}, bf16[32,1536]{1,0:T(8,128)(2,1)}, u32[]{:S(2)}, u32[]{:S(2)}) collective-permute-start(bf16[32,1536]{1,0:T(8,128)(2,1)} %get-tuple-element.38), channel_id=1, source_target_pairs={{0,16},{16,0},{32,48},{48,32},{64,80},{80,64},{96,112},{112,96},{1... | collective-permute-start | bytes 294920 | tf_op jit(solution)/shard_map/ppermute | solution.py:41
  100.0 9.6 %collective-permute-start.4 = (bf16[32,1536]{1,0:T(8,128)(2,1)}, bf16[32,1536]{1,0:T(8,128)(2,1)}, u32[]{:S(2)}, u32[]{:S(2)}) collective-permute-start(bf16[32,1536]{1,0:T(8,128)(2,1)} %get-tuple-element.39), channel_id=1, source_target_pairs={{0,96},{16,112},{32,64},{48,80},{64,32},{80,48},{96,0},{112,16},{1... | collective-permute-start | bytes 294920 | tf_op jit(solution)/shard_map/ppermute | solution.py:41
  102.9 8.2 %collective-permute-start.5 = (bf16[32,1536]{1,0:T(8,128)(2,1)}, bf16[32,1536]{1,0:T(8,128)(2,1)}, u32[]{:S(2)}, u32[]{:S(2)}) collective-permute-start(bf16[32,1536]{1,0:T(8,128)(2,1)} %get-tuple-element.40), channel_id=1, source_target_pairs={{0,112},{16,96},{32,80},{48,64},{64,48},{80,32},{96,16},{112,0},{1... | collective-permute-start | bytes 294920 | tf_op jit(solution)/shard_map/ppermute | solution.py:41
  107.9 3.1 %copy-start.4 = (bf16[32,1536]{1,0:T(8,128)(2,1)S(1)}, bf16[32,1536]{1,0:T(8,128)(2,1)}, u32[]{:S(2)}) copy-start(bf16[32,1536]{1,0:T(8,128)(2,1)} %copy-done.3) | copy-start | bytes 294916
  108.9 0.7 copy-start.2
  112.9 28.0 %all-to-all-start.3 = ((bf16[16,32,96]{2,1,0:T(8,128)(2,1)}), bf16[16,32,96]{2,1,0:T(8,128)(2,1)S(1)}, u32[]{:S(2)}, u32[]{:S(2)}) async-start(bf16[16,32,96]{2,1,0:T(8,128)(2,1)} %sum.1), calls=%async_computation.3 | async-start | bytes 262144 | tf_op jit(solution)/shard_map/all_to_all | solution.py:397
  140.9 11.8 %collective-permute-start.7 = (f32[32,96]{1,0:T(8,128)S(1)}, f32[32,96]{1,0:T(8,128)S(1)}, u32[]{:S(2)}, u32[]{:S(2)}) collective-permute-start(f32[32,96]{1,0:T(8,128)S(1)} %broadcast_multiply_fusion), channel_id=1, source_target_pairs={{0,16},{96,32},{112,80},{48,96},{64,144},{128,160},{144,208},{240,... | collective-permute-start | bytes 36872 | tf_op jit(solution)/shard_map/ppermute | solution.py:66
  143.5 9.2 %collective-permute-start.6 = (f32[32,96]{1,0:T(8,128)S(1)}, f32[32,96]{1,0:T(8,128)S(1)}, u32[]{:S(2)}, u32[]{:S(2)}) collective-permute-start(f32[32,96]{1,0:T(8,128)S(1)} %broadcast_multiply_fusion), channel_id=1, source_target_pairs={{0,0},{16,16},{96,48},{112,64},{32,80},{48,112},{64,128},{80,144},... | collective-permute-start | bytes 36872 | tf_op jit(solution)/shard_map/ppermute | solution.py:66
  148.0 7.3 %collective-permute-start.8 = (f32[32,96]{1,0:T(8,128)S(1)}, f32[32,96]{1,0:T(8,128)S(1)}, u32[]{:S(2)}, u32[]{:S(2)}) collective-permute-start(f32[32,96]{1,0:T(8,128)S(1)} %broadcast_multiply_fusion), channel_id=1, source_target_pairs={{16,32},{32,96},{80,160},{224,224},{176,288},{256,352},{368,416},{... | collective-permute-start | bytes 36872 | tf_op jit(solution)/shard_map/ppermute | solution.py:66
  149.3 10.6 %all-to-all-start.4 = ((bf16[8,128,128]{2,1,0:T(8,128)(2,1)}), bf16[8,128,128]{2,1,0:T(8,128)(2,1)S(1)}, u32[]{:S(2)}, u32[]{:S(2)}) async-start(bf16[8,128,128]{2,1,0:T(8,128)(2,1)} %attend_grad.1), calls=%async_computation.4 | async-start | bytes 524288 | tf_op jit(solution)/shard_map/all_to_all | solution.py:50
Sparse Core Ops, SparseCore 0:
  10.1 78.6 all-gather.1

commit v9 on v7

--- a/solution.py
+++ b/solution.py
@@ -392,6 +392,7 @@
     terms, grad_query = lax.optimization_barrier((terms, grad_query))
     total = jnp.sum(terms.astype(jnp.float32), axis=0) / float(clip_count)
     grad_query = trade(grad_query)
+    total, grad_query = lax.optimization_barrier((total, grad_query))
     total = place_blocks(total, me)
     (grad_query_rows,) = call(
         functools.partial(join_kernel, head_count), [((1, row_count, head_width), jnp.bfloat16)], "join", 1e6

time: 169 us -> 171 us (1.012)
  waiting for transfers between devices: 49.5 us -> 52.3 us
    ppermute x3, waiting for transfers between devices: 0.01 us -> 2.2 us  [pass_on(): lax.ppermute(block, 'seq', [(held[3 * turn + take], 4 * turn + put) for t...]
  transfers between devices with their start and end apart: 15 -> 15, of which waited for: 9 -> 10; matrix products, arithmetic and copies ran while one was open for 7% -> 7% of each run, Pallas kernels for 16% -> 16%
where the time goes in v9:
time: 171 us; the launch traced here: 169 us
  starting transfers between devices  58.1 us (34%)
  waiting for transfers between devices  52.3 us (31%)
  Pallas kernels  29.5 us (17%)
  between operations  14.4 us (8%)
  local copies, waits for them, and re-layouts  9.53 us (6%)
  other arithmetic  5.27 us (3%)
    pallas_call x8, Pallas kernels, run(): pl.pallas_call(kernel, out_shape=[jax.ShapeDtypeStruct(shape, dtype) for...  29.5 us
    all_to_all x3, waiting for transfers between devices, trade(): lax.all_to_all(slots, 'seq', 0, 0, axis_index_groups=groups, tiled=True)  24.6 us
    ppermute x6, waiting for transfers between devices, send(): return lax.ppermute(value, 'seq', pairs)  18.3 us
    ppermute x6, starting transfers between devices, send(): return lax.ppermute(value, 'seq', pairs)  17.8 us
    all_to_all x1, starting transfers between devices, shards(): terms = lax.all_to_all(clip_parts, 'dp', 0, 0, tiled=True)  15.2 us
    all_to_all x3, starting transfers between devices, trade(): lax.all_to_all(slots, 'seq', 0, 0, axis_index_groups=groups, tiled=True)  11.8 us
    ppermute x3, starting transfers between devices, pass_on(): lax.ppermute(block, 'seq', [(held[3 * turn + take], 4 * turn + put) for t...  7.71 us
    all_to_all x1, starting transfers between devices, shards(): arrived = lax.all_to_all(packed, 'seq', 0, 0, tiled=True)  5.57 us
  transfers between devices with their start and end apart: 15, of which 10 were waited for; matrix products, arithmetic and copies ran while one was open for 7% of the time, Pallas kernels for 16%

profile of v9, /device:TPU:6, one launch (start us, length us, event | category | flops | bytes accessed | tf_op | source)
XLA Modules:
  0.0 169.1 jit_solution(15508861608742776290)
XLA Ops:
  7.2 0.7 all-gather.2.cloned.1.call-update
  7.9 2.2 %pack.1 = bf16[8,3,128,128]{3,2,1,0:T(8,128)(2,1)} custom-call(bf16[1,128,768]{2,1,0:T(8,128)(2,1)} %query_ref.1, bf16[1,128,768]{2,1,0:T(8,128)(2,1)} %key_ref.1, bf16[1,128,768]{2,1,0:T(8,128)(2,1)} %value_ref.1), custom_call_target="tpu_custom_call" | custom-call | flops 1000000 | bytes 1000000 | tf_op jit(solution)/shard_map/pack/pallas_call | solution.py:235
  10.2 4.7 %all-to-all-start = ((bf16[8,3,128,128]{3,2,1,0:T(8,128)(2,1)}), bf16[8,3,128,128]{3,2,1,0:T(8,128)(2,1)S(1)}, u32[]{:S(2)}, u32[]{:S(2)}) async-start(bf16[8,3,128,128]{3,2,1,0:T(8,128)(2,1)} %pack.1), calls=%async_computation | async-start | bytes 1572864 | tf_op jit(solution)/shard_map/all_to_all | solution.py:50
  15.0 0.2 dynamic-slice_reduce_fusion
  15.2 0.2 reduce-window.26
  15.6 0.1 reduce
  16.1 0.1 reduce.1
  16.3 2.2 %gather_fusion = bf16[256,1536]{1,0:T(8,128)(2,1)} fusion(bf16[128,1536]{1,0:T(8,128)(2,1)S(1)} %bitcast.32, s32[1024]{0:T(1024)S(1)} %pad_clamp_fusion.1), kind=kCustom, calls=%fused_computation | custom fusion | bytes 1573888 | tf_op jit(solution)/shard_map/gather | solution.py:257
  18.5 2.7 %select_convert_fusion.hidden_ref = bf16[4096,128]{1,0:T(8,128)(2,1)} fusion(s32[128]{0:T(128)S(1)} %pad.8, s32[4096]{0:T(1024)S(1)} %add_bitcast_fusion), kind=kLoop, calls=%fused_computation.2 | loop fusion | flops 1572864 | bytes 1065472 | tf_op jit(solution)/shard_map/convert_element_type | solution.py:315
  21.2 6.7 %all-to-all-done.input_ref = bf16[8,3,128,128]{3,2,1,0:T(8,128)(2,1)S(1)} async-done(((bf16[8,3,128,128]{3,2,1,0:T(8,128)(2,1)}), bf16[8,3,128,128]{3,2,1,0:T(8,128)(2,1)S(1)}, u32[]{:S(2)}, u32[]{:S(2)}) %all-to-all-start) | async-done | bytes 786464 | tf_op jit(solution)/shard_map/all_to_all | solution.py:50
  27.8 5.6 %all-to-all-start.1 = ((bf16[32,8,1536]{2,1,0:T(8,128)(2,1)}), bf16[32,8,1536]{2,1,0:T(8,128)(2,1)S(1)}, u32[]{:S(2)}, u32[]{:S(2)}) async-start(bf16[32,8,1536]{2,1,0:T(8,128)(2,1)} %bitcast.7), calls=%async_computation.1 | async-start | bytes 1572864 | tf_op jit(solution)/shard_map/all_to_all | solution.py:297
  33.4 2.1 %collective-permute-start = (bf16[8,2,128,128]{3,2,1,0:T(8,128)(2,1)S(1)}, bf16[8,2,128,128]{3,2,1,0:T(8,128)(2,1)S(1)}, u32[]{:S(2)}, u32[]{:S(2)}) collective-permute-start(bf16[8,2,128,128]{3,2,1,0:T(8,128)(2,1)S(1)} %slice.21.own_ref), channel_id=1, source_target_pairs={{0,16},{16,0},{32,48},{48,32},{64,80},{80,64},{96,112},{112,96},{1... | collective-permute-start | bytes 1572872 | tf_op jit(solution)/shard_map/ppermute | solution.py:41
  35.6 0.9 and_convert_fusion.member_ref
  36.5 0.8 collective-permute-done.core_ref
  37.3 0.8 copy-done.8
  38.1 5.4 %near.1 = (f32[8,128,1]{2,1,0:T(8,128)}, f32[8,128,256]{2,1,0:T(8,128)}) custom-call(bf16[8,3,128,128]{3,2,1,0:T(8,128)(2,1)} %copy-done.5, bf16[8,128,128]{2,1,0:T(8,128)(2,1)} %and_convert_fusion.member_ref, bf16[4096,128]{1,0:T(8,128)(2,1)} %select_convert_fusion.hidden_ref, bf16[8,2,128,128]{3,2,1,0:T(8,128)(2,1)} %copy-done.6, ...), custom_call_target="tpu_custom_call" | custom-call | flops 4000000000 | bytes 1000000 | tf_op jit(solution)/shard_map/near/pallas_call | solution.py:235
  43.5 1.9 %all-to-all-done.1 = bf16[32,8,1536]{2,1,0:T(8,128)(2,1)S(1)} async-done(((bf16[32,8,1536]{2,1,0:T(8,128)(2,1)}), bf16[32,8,1536]{2,1,0:T(8,128)(2,1)S(1)}, u32[]{:S(2)}, u32[]{:S(2)}) %all-to-all-start.1) | async-done | bytes 786464 | tf_op jit(solution)/shard_map/all_to_all | solution.py:297
  45.4 0.9 gather_fusion.1
  46.3 1.9 %broadcast_in_dim.29 = bf16[8,128,1536]{2,1,0:T(8,128)(2,1)} broadcast(bf16[128,1536]{1,0:T(8,128)(2,1)S(1)} %gather_fusion.1), dimensions={1,2} | broadcast | bytes 3538944 | tf_op jit(solution)/shard_map/broadcast_in_dim | solution.py:336
  48.2 3.6 %all-to-all-start.2 = ((bf16[8,128,1536]{2,1,0:T(8,128)(2,1)}), bf16[8,128,1536]{2,1,0:T(8,128)(2,1)S(1)}, u32[]{:S(2)}, u32[]{:S(2)}) async-start(bf16[8,128,1536]{2,1,0:T(8,128)(2,1)} %broadcast_in_dim.29), calls=%async_computation.2 | async-start | bytes 6291456 | tf_op jit(solution)/shard_map/all_to_all | solution.py:50
  51.8 4.7 %collective-permute-start.1 = (bf16[8,2,128,128]{3,2,1,0:T(8,128)(2,1)}, bf16[8,2,128,128]{3,2,1,0:T(8,128)(2,1)}, u32[]{:S(2)}, u32[]{:S(2)}) collective-permute-start(bf16[8,2,128,128]{3,2,1,0:T(8,128)(2,1)} %copy-done.6), channel_id=1, source_target_pairs={{0,96},{16,112},{32,64},{48,80},{64,32},{80,48},{96,0},{112,16},{1... | collective-permute-start | bytes 1572872 | tf_op jit(solution)/shard_map/ppermute | solution.py:41
  56.6 13.2 %collective-permute-done.1.own_ref.far_ref = bf16[8,2,128,128]{3,2,1,0:T(8,128)(2,1)} collective-permute-done((bf16[8,2,128,128]{3,2,1,0:T(8,128)(2,1)}, bf16[8,2,128,128]{3,2,1,0:T(8,128)(2,1)}, u32[]{:S(2)}, u32[]{:S(2)}) %collective-permute-start.1) | collective-permute-done | bytes 524320 | tf_op jit(solution)/shard_map/ppermute | solution.py:41
  69.8 2.3 %collective-permute-start.2 = (bf16[8,2,128,128]{3,2,1,0:T(8,128)(2,1)}, bf16[8,2,128,128]{3,2,1,0:T(8,128)(2,1)}, u32[]{:S(2)}, u32[]{:S(2)}) collective-permute-start(bf16[8,2,128,128]{3,2,1,0:T(8,128)(2,1)} %collective-permute-done.1.own_ref.far_ref), channel_id=1, source_target_pairs={{0,16},{16,0},{32,48},{48,32},{64,80},{80,64},{96,112},{112,96},{1... | collective-permute-start | bytes 1572872 | tf_op jit(solution)/shard_map/ppermute | solution.py:41
  72.2 1.7 %collective-permute-done.2.core_ref.far_core_ref = bf16[8,2,128,128]{3,2,1,0:T(8,128)(2,1)} collective-permute-done((bf16[8,2,128,128]{3,2,1,0:T(8,128)(2,1)}, bf16[8,2,128,128]{3,2,1,0:T(8,128)(2,1)}, u32[]{:S(2)}, u32[]{:S(2)}) %collective-permute-start.2) | collective-permute-done | bytes 524320 | tf_op jit(solution)/shard_map/ppermute | solution.py:41
  73.9 6.4 %far.1 = (bf16[8,128,128]{2,1,0:T(8,128)(2,1)}, f32[8,128,128]{2,1,0:T(8,128)}, f32[8,128,128]{2,1,0:T(8,128)}) custom-call(bf16[8,3,128,128]{3,2,1,0:T(8,128)(2,1)} %copy-done.5, bf16[8,128,128]{2,1,0:T(8,128)(2,1)} %and_convert_fusion.member_ref, bf16[4096,128]{1,0:T(8,128)(2,1)} %select_convert_fusion.hidden_ref, ...), custom_call_target="tpu_custom_call" | custom-call | flops 4000000000 | bytes 1000000 | tf_op jit(solution)/shard_map/far/pallas_call | solution.py:235
  80.4 10.8 %all-to-all-done.2.rows_ref = bf16[8,128,1536]{2,1,0:T(8,128)(2,1)S(1)} async-done(((bf16[8,128,1536]{2,1,0:T(8,128)(2,1)}), bf16[8,128,1536]{2,1,0:T(8,128)(2,1)S(1)}, u32[]{:S(2)}, u32[]{:S(2)}) %all-to-all-start.2) | async-done | bytes 3145760 | tf_op jit(solution)/shard_map/all_to_all | solution.py:50
  91.2 0.9 copy-done.4
  92.1 1.9 %outer.1 = (bf16[32,1536]{1,0:T(8,128)(2,1)S(1)}, bf16[32,1536]{1,0:T(8,128)(2,1)}, bf16[32,1536]{1,0:T(8,128)(2,1)}, bf16[32,1536]{1,0:T(8,128)(2,1)}) custom-call(s32[4]{0:T(128)S(1)} %pad_add_fusion.order_ref, bf16[8,128,128]{2,1,0:T(8,128)(2,1)S(1)} %copy-done.4, bf16[8,128,1536]{2,1,0:T(8,128)(2,1)S(1)} %all-to-all-done.2.rows_ref), custom_call_target="tpu_custom_call" | custom-call | flops 1000000000 | bytes 1000000 | tf_op jit(solution)/shard_map/outer/pallas_call | solution.py:235
  94.0 0.6 copy-done.2
  94.6 2.0 %collective-permute-start.3 = (bf16[32,1536]{1,0:T(8,128)(2,1)}, bf16[32,1536]{1,0:T(8,128)(2,1)}, u32[]{:S(2)}, u32[]{:S(2)}) collective-permute-start(bf16[32,1536]{1,0:T(8,128)(2,1)} %get-tuple-element.38), channel_id=1, source_target_pairs={{0,16},{16,0},{32,48},{48,32},{64,80},{80,64},{96,112},{112,96},{1... | collective-permute-start | bytes 294920 | tf_op jit(solution)/shard_map/ppermute | solution.py:41
  96.6 3.8 %collective-permute-start.4 = (bf16[32,1536]{1,0:T(8,128)(2,1)}, bf16[32,1536]{1,0:T(8,128)(2,1)}, u32[]{:S(2)}, u32[]{:S(2)}) collective-permute-start(bf16[32,1536]{1,0:T(8,128)(2,1)} %get-tuple-element.39), channel_id=1, source_target_pairs={{0,96},{16,112},{32,64},{48,80},{64,32},{80,48},{96,0},{112,16},{1... | collective-permute-start | bytes 294920 | tf_op jit(solution)/shard_map/ppermute | solution.py:41
  100.5 2.9 %collective-permute-start.5 = (bf16[32,1536]{1,0:T(8,128)(2,1)}, bf16[32,1536]{1,0:T(8,128)(2,1)}, u32[]{:S(2)}, u32[]{:S(2)}) collective-permute-start(bf16[32,1536]{1,0:T(8,128)(2,1)} %get-tuple-element.40), channel_id=1, source_target_pairs={{0,112},{16,96},{32,80},{48,64},{64,48},{80,32},{96,16},{112,0},{1... | collective-permute-start | bytes 294920 | tf_op jit(solution)/shard_map/ppermute | solution.py:41
  103.4 1.0 constant_dynamic-slice_fusion.weight_ref
  104.5 1.0 project.1.grad_ref
  105.5 0.7 copy-done.1
  106.2 2.5 %collective-permute-done.5.refs_3_ = bf16[32,1536]{1,0:T(8,128)(2,1)} collective-permute-done((bf16[32,1536]{1,0:T(8,128)(2,1)}, bf16[32,1536]{1,0:T(8,128)(2,1)}, u32[]{:S(2)}, u32[]{:S(2)}) %collective-permute-start.5) | collective-permute-done | bytes 98336 | tf_op jit(solution)/shard_map/ppermute | solution.py:41
  108.7 1.8 %sum.1 = bf16[16,32,96]{2,1,0:T(8,128)(2,1)} custom-call(bf16[32,1536]{1,0:T(8,128)(2,1)S(1)} %copy-done.3, bf16[32,1536]{1,0:T(8,128)(2,1)} %collective-permute-done.3.refs_1_, bf16[32,1536]{1,0:T(8,128)(2,1)} %collective-permute-done.4.refs_2_, bf16[32,1536]{1,0:T(8,128)(2,1)} %collective-permute-done.5.refs_3_), custom_call_target="tpu_custom_call" | custom-call | flops 1000000 | bytes 1000000 | tf_op jit(solution)/shard_map/sum/pallas_call | solution.py:235
  110.4 15.2 %all-to-all-start.3 = ((bf16[16,32,96]{2,1,0:T(8,128)(2,1)}), bf16[16,32,96]{2,1,0:T(8,128)(2,1)S(1)}, u32[]{:S(2)}, u32[]{:S(2)}) async-start(bf16[16,32,96]{2,1,0:T(8,128)(2,1)} %sum.1), calls=%async_computation.3 | async-start | bytes 262144 | tf_op jit(solution)/shard_map/all_to_all | solution.py:391
  125.6 10.1 %attend_grad.1 = bf16[8,128,128]{2,1,0:T(8,128)(2,1)} custom-call(bf16[8,3,128,128]{3,2,1,0:T(8,128)(2,1)} %copy-done.5, bf16[8,128,128]{2,1,0:T(8,128)(2,1)} %and_convert_fusion.member_ref, bf16[4096,128]{1,0:T(8,128)(2,1)} %select_convert_fusion.hidden_ref, bf16[8,128,128]{2,1,0:T(8,128)(2,1)} %copy-done.1, f32[8,128,128]{2,1,0:T(8,128)} %get-tuple-element.48.exact_ref, ...), custom_call_target="tpu_custom_call" | custom-call | flops 5000000000 | bytes 1000000 | tf_op jit(solution)/shard_map/attend_grad/pallas_call | solution.py:235
  135.7 4.6 %all-to-all-done.3 = bf16[16,32,96]{2,1,0:T(8,128)(2,1)S(1)} async-done(((bf16[16,32,96]{2,1,0:T(8,128)(2,1)}), bf16[16,32,96]{2,1,0:T(8,128)(2,1)S(1)}, u32[]{:S(2)}, u32[]{:S(2)}) %all-to-all-start.3) | async-done | bytes 98336 | tf_op jit(solution)/shard_map/all_to_all | solution.py:391
  140.4 3.4 %all-to-all-start.4 = ((bf16[8,128,128]{2,1,0:T(8,128)(2,1)}), bf16[8,128,128]{2,1,0:T(8,128)(2,1)S(1)}, u32[]{:S(2)}, u32[]{:S(2)}) async-start(bf16[8,128,128]{2,1,0:T(8,128)(2,1)} %attend_grad.1), calls=%async_computation.4 | async-start | bytes 524288 | tf_op jit(solution)/shard_map/all_to_all | solution.py:50
  143.8 7.2 %all-to-all-done.4.slots_ref = bf16[8,128,128]{2,1,0:T(8,128)(2,1)S(1)} async-done(((bf16[8,128,128]{2,1,0:T(8,128)(2,1)}), bf16[8,128,128]{2,1,0:T(8,128)(2,1)S(1)}, u32[]{:S(2)}, u32[]{:S(2)}) %all-to-all-start.4) | async-done | bytes 262176 | tf_op jit(solution)/shard_map/all_to_all | solution.py:50
  151.0 3.5 %collective-permute-start.7 = (f32[32,96]{1,0:T(8,128)S(1)}, f32[32,96]{1,0:T(8,128)S(1)}, u32[]{:S(2)}, u32[]{:S(2)}) collective-permute-start(f32[32,96]{1,0:T(8,128)S(1)} %broadcast_multiply_fusion), channel_id=1, source_target_pairs={{0,16},{96,32},{112,80},{48,96},{64,144},{128,160},{144,208},{240,... | collective-permute-start | bytes 36872 | tf_op jit(solution)/shard_map/ppermute | solution.py:66
  154.5 1.3 collective-permute-start.8
  155.8 2.9 %collective-permute-start.6 = (f32[32,96]{1,0:T(8,128)S(1)}, f32[32,96]{1,0:T(8,128)S(1)}, u32[]{:S(2)}, u32[]{:S(2)}) collective-permute-start(f32[32,96]{1,0:T(8,128)S(1)} %broadcast_multiply_fusion), channel_id=1, source_target_pairs={{0,0},{16,16},{96,48},{112,64},{32,80},{48,112},{64,128},{80,144},... | collective-permute-start | bytes 36872 | tf_op jit(solution)/shard_map/ppermute | solution.py:66
  158.7 0.7 join.1
  159.5 2.2 %collective-permute-done.8 = f32[32,96]{1,0:T(8,128)S(1)} collective-permute-done((f32[32,96]{1,0:T(8,128)S(1)}, f32[32,96]{1,0:T(8,128)S(1)}, u32[]{:S(2)}, u32[]{:S(2)}) %collective-permute-start.8) | collective-permute-done | bytes 12320 | tf_op jit(solution)/shard_map/ppermute | solution.py:66
  161.7 0.6 fusion
  (48 shorter events, 1.0 us)
Async XLA Ops:
  7.2 9.2 %copy-start = (bf16[1,128,1536]{2,1,0:T(8,128)(2,1)S(1)}, bf16[1,128,1536]{2,1,0:T(8,128)(2,1)}, u32[]{:S(2)}) copy-start(bf16[1,128,1536]{2,1,0:T(8,128)(2,1)} %param.10) | copy-start | bytes 1179652
  7.2 7.8 %copy-start.7 = (s32[1,32,32]{2,1,0:T(8,128)S(1)}, s32[1,32,32]{2,1,0:T(8,128)}, u32[]{:S(2)}) copy-start(s32[1,32,32]{2,1,0:T(8,128)} %param.12) | copy-start | bytes 12292
  7.2 8.0 %copy-start.9 = (s32[1,5]{1,0:T(1,128)S(1)}, s32[1,5]{1,0:T(1,128)}, u32[]{:S(2)}) copy-start(s32[1,5]{1,0:T(1,128)} %param.13) | copy-start | bytes 64
  7.2 96.2 %all-gather.2.cloned.1.call-start = ((), (), s32[]{:S(2)}) async-start(), calls=%async_computation.5 | async-start | bytes 2506752 | tf_op jit(solution)/shard_map/all_gather | solution.py:283
  10.2 17.6 %all-to-all-start = ((bf16[8,3,128,128]{3,2,1,0:T(8,128)(2,1)}), bf16[8,3,128,128]{3,2,1,0:T(8,128)(2,1)S(1)}, u32[]{:S(2)}, u32[]{:S(2)}) async-start(bf16[8,3,128,128]{3,2,1,0:T(8,128)(2,1)} %pack.1), calls=%async_computation | async-start | bytes 1572864 | tf_op jit(solution)/shard_map/all_to_all | solution.py:50
  27.8 9.4 %copy-start.5 = (bf16[8,3,128,128]{3,2,1,0:T(8,128)(2,1)}, bf16[8,3,128,128]{3,2,1,0:T(8,128)(2,1)S(1)}, u32[]{:S(2)}) copy-start(bf16[8,3,128,128]{3,2,1,0:T(8,128)(2,1)S(1)} %all-to-all-done.input_ref) | copy-start | bytes 2359300
  27.8 17.6 %all-to-all-start.1 = ((bf16[32,8,1536]{2,1,0:T(8,128)(2,1)}), bf16[32,8,1536]{2,1,0:T(8,128)(2,1)S(1)}, u32[]{:S(2)}, u32[]{:S(2)}) async-start(bf16[32,8,1536]{2,1,0:T(8,128)(2,1)} %bitcast.7), calls=%async_computation.1 | async-start | bytes 1572864 | tf_op jit(solution)/shard_map/all_to_all | solution.py:297
  33.4 3.8 %copy-start.6 = (bf16[8,2,128,128]{3,2,1,0:T(8,128)(2,1)}, bf16[8,2,128,128]{3,2,1,0:T(8,128)(2,1)S(1)}, u32[]{:S(2)}) copy-start(bf16[8,2,128,128]{3,2,1,0:T(8,128)(2,1)S(1)} %slice.21.own_ref) | copy-start | bytes 1572868
  33.4 3.8 %collective-permute-start = (bf16[8,2,128,128]{3,2,1,0:T(8,128)(2,1)S(1)}, bf16[8,2,128,128]{3,2,1,0:T(8,128)(2,1)S(1)}, u32[]{:S(2)}, u32[]{:S(2)}) collective-permute-start(bf16[8,2,128,128]{3,2,1,0:T(8,128)(2,1)S(1)} %slice.21.own_ref), channel_id=1, source_target_pairs={{0,16},{16,0},{32,48},{48,32},{64,80},{80,64},{96,112},{112,96},{1... | collective-permute-start | bytes 1572872 | tf_op jit(solution)/shard_map/ppermute | solution.py:41
  37.3 0.8 copy-start.8
  48.2 43.0 %all-to-all-start.2 = ((bf16[8,128,1536]{2,1,0:T(8,128)(2,1)}), bf16[8,128,1536]{2,1,0:T(8,128)(2,1)S(1)}, u32[]{:S(2)}, u32[]{:S(2)}) async-start(bf16[8,128,1536]{2,1,0:T(8,128)(2,1)} %broadcast_in_dim.29), calls=%async_computation.2 | async-start | bytes 6291456 | tf_op jit(solution)/shard_map/all_to_all | solution.py:50
  51.8 18.0 %collective-permute-start.1 = (bf16[8,2,128,128]{3,2,1,0:T(8,128)(2,1)}, bf16[8,2,128,128]{3,2,1,0:T(8,128)(2,1)}, u32[]{:S(2)}, u32[]{:S(2)}) collective-permute-start(bf16[8,2,128,128]{3,2,1,0:T(8,128)(2,1)} %copy-done.6), channel_id=1, source_target_pairs={{0,96},{16,112},{32,64},{48,80},{64,32},{80,48},{96,0},{112,16},{1... | collective-permute-start | bytes 1572872 | tf_op jit(solution)/shard_map/ppermute | solution.py:41
  69.8 4.1 %collective-permute-start.2 = (bf16[8,2,128,128]{3,2,1,0:T(8,128)(2,1)}, bf16[8,2,128,128]{3,2,1,0:T(8,128)(2,1)}, u32[]{:S(2)}, u32[]{:S(2)}) collective-permute-start(bf16[8,2,128,128]{3,2,1,0:T(8,128)(2,1)} %collective-permute-done.1.own_ref.far_ref), channel_id=1, source_target_pairs={{0,16},{16,0},{32,48},{48,32},{64,80},{80,64},{96,112},{112,96},{1... | collective-permute-start | bytes 1572872 | tf_op jit(solution)/shard_map/ppermute | solution.py:41
  91.2 1.0 copy-start.4
  94.0 0.6 copy-start.2
  94.6 11.6 %collective-permute-start.3 = (bf16[32,1536]{1,0:T(8,128)(2,1)}, bf16[32,1536]{1,0:T(8,128)(2,1)}, u32[]{:S(2)}, u32[]{:S(2)}) collective-permute-start(bf16[32,1536]{1,0:T(8,128)(2,1)} %get-tuple-element.38), channel_id=1, source_target_pairs={{0,16},{16,0},{32,48},{48,32},{64,80},{80,64},{96,112},{112,96},{1... | collective-permute-start | bytes 294920 | tf_op jit(solution)/shard_map/ppermute | solution.py:41
  96.6 9.5 %collective-permute-start.4 = (bf16[32,1536]{1,0:T(8,128)(2,1)}, bf16[32,1536]{1,0:T(8,128)(2,1)}, u32[]{:S(2)}, u32[]{:S(2)}) collective-permute-start(bf16[32,1536]{1,0:T(8,128)(2,1)} %get-tuple-element.39), channel_id=1, source_target_pairs={{0,96},{16,112},{32,64},{48,80},{64,32},{80,48},{96,0},{112,16},{1... | collective-permute-start | bytes 294920 | tf_op jit(solution)/shard_map/ppermute | solution.py:41
  100.5 8.2 %collective-permute-start.5 = (bf16[32,1536]{1,0:T(8,128)(2,1)}, bf16[32,1536]{1,0:T(8,128)(2,1)}, u32[]{:S(2)}, u32[]{:S(2)}) collective-permute-start(bf16[32,1536]{1,0:T(8,128)(2,1)} %get-tuple-element.40), channel_id=1, source_target_pairs={{0,112},{16,96},{32,80},{48,64},{64,48},{80,32},{96,16},{112,0},{1... | collective-permute-start | bytes 294920 | tf_op jit(solution)/shard_map/ppermute | solution.py:41
  104.5 4.2 %copy-start.3 = (bf16[32,1536]{1,0:T(8,128)(2,1)S(1)}, bf16[32,1536]{1,0:T(8,128)(2,1)}, u32[]{:S(2)}) copy-start(bf16[32,1536]{1,0:T(8,128)(2,1)} %copy-done.2) | copy-start | bytes 294916
  105.5 0.7 copy-start.1
  110.4 29.9 %all-to-all-start.3 = ((bf16[16,32,96]{2,1,0:T(8,128)(2,1)}), bf16[16,32,96]{2,1,0:T(8,128)(2,1)S(1)}, u32[]{:S(2)}, u32[]{:S(2)}) async-start(bf16[16,32,96]{2,1,0:T(8,128)(2,1)} %sum.1), calls=%async_computation.3 | async-start | bytes 262144 | tf_op jit(solution)/shard_map/all_to_all | solution.py:391
  140.4 10.6 %all-to-all-start.4 = ((bf16[8,128,128]{2,1,0:T(8,128)(2,1)}), bf16[8,128,128]{2,1,0:T(8,128)(2,1)S(1)}, u32[]{:S(2)}, u32[]{:S(2)}) async-start(bf16[8,128,128]{2,1,0:T(8,128)(2,1)} %attend_grad.1), calls=%async_computation.4 | async-start | bytes 524288 | tf_op jit(solution)/shard_map/all_to_all | solution.py:50
  151.0 8.5 %collective-permute-start.7 = (f32[32,96]{1,0:T(8,128)S(1)}, f32[32,96]{1,0:T(8,128)S(1)}, u32[]{:S(2)}, u32[]{:S(2)}) collective-permute-start(f32[32,96]{1,0:T(8,128)S(1)} %broadcast_multiply_fusion), channel_id=1, source_target_pairs={{0,16},{96,32},{112,80},{48,96},{64,144},{128,160},{144,208},{240,... | collective-permute-start | bytes 36872 | tf_op jit(solution)/shard_map/ppermute | solution.py:66
  154.5 7.1 %collective-permute-start.8 = (f32[32,96]{1,0:T(8,128)S(1)}, f32[32,96]{1,0:T(8,128)S(1)}, u32[]{:S(2)}, u32[]{:S(2)}) collective-permute-start(f32[32,96]{1,0:T(8,128)S(1)} %broadcast_multiply_fusion), channel_id=1, source_target_pairs={{16,32},{32,96},{80,160},{224,224},{176,288},{256,352},{368,416},{... | collective-permute-start | bytes 36872 | tf_op jit(solution)/shard_map/ppermute | solution.py:66
  155.8 5.8 %collective-permute-start.6 = (f32[32,96]{1,0:T(8,128)S(1)}, f32[32,96]{1,0:T(8,128)S(1)}, u32[]{:S(2)}, u32[]{:S(2)}) collective-permute-start(f32[32,96]{1,0:T(8,128)S(1)} %broadcast_multiply_fusion), channel_id=1, source_target_pairs={{0,0},{16,16},{96,48},{112,64},{32,80},{48,112},{64,128},{80,144},... | collective-permute-start | bytes 36872 | tf_op jit(solution)/shard_map/ppermute | solution.py:66
Sparse Core Ops, SparseCore 0:
  10.1 78.8 all-gather.1
